TPU v7x, 32 devices: a whole 2x2x4 slice. The times are simulated.
32 devices in a mesh: circ: 4 (over z), span: 4 (over y, core), axial: 2 (over x).
Axes of the slice: x: 2, y: 2, z: 4, core: 2. Of those that a mesh axis runs over, the one named last changes fastest.
Arguments:
- rotor_outlet: float32 [5, 64, 512], P(None, ('span', 'axial'), 'circ'), may hold values from -6 to 6
- blade_count: int32 [1], replicated, may hold values from 3 to 15
- harmonic_list: int32 [8], replicated, may hold values from 1 to 16
- donor_index: int32 [128], P('span'), may hold values from 0 to 62, as said below
- donor_weight: float32 [128], P('span'), may hold values from 0 to 1
- state: float32 [5, 128, 32, 512], P(None, 'span', 'axial', 'circ'), may hold values from -6 to 6
- time_step: float32 [128, 32, 512], P('span', 'axial', 'circ'), may hold values from 0.05 to 0.4
- flux_jacobian: float32 [3, 5, 5], replicated, may hold values from -2.5 to 2.5
Outputs:
- new_state: float32 [5, 128, 32, 512], P(None, 'span', 'axial', 'circ')
- residual: float32 [5, 128, 32, 512], P(None, 'span', 'axial', 'circ')
Inputs may be any that keep to these rules, and one draw needn't show every extreme that they name: `donor_index`: the stator spanwise cells g * 32 to (g + 1) * 32 - 1 form group g; every entry of group g lies between g * 16 - 1 (0 for g = 0) and (g + 1) * 16 - 2; the first entry of each group equals that lower end and the last entry that upper end.
All inputs are finite; a program needn't handle non-finite values.
Results may differ from a plain program's by a relative error of at most 0.0001.
Values sent between devices are 32-bit elements; how exact they have to be, the bound alone decides.
No kernel may reach another device: no remote copies, remote signals or barrier semaphores. Data moves between devices by JAX's collectives and lax.ppermute only.
A program may use at most 128 MiB of HBM per device.

v0:
```python
import jax
import jax.numpy as jnp
from jax import lax
from jax.sharding import PartitionSpec as P

SEGMENTS = 4


SEGMENT_COEF = (0.25, 1.0 / 3.0, 0.5, 1.0)
DISSIP = 0.2


def padded_2(cells, sides, width, closed):
    for axis, dim in sides:
        count = lax.axis_size(axis)
        ends = count if closed else count - 1
        head = lax.slice_in_dim(cells, 0, width, axis=dim)
        tail = lax.slice_in_dim(cells, cells.shape[dim] - width, cells.shape[dim], axis=dim)
        cells = jnp.concatenate(
            [
                lax.ppermute(tail, axis, [(i, (i + 1) % count) for i in range(ends)]),
                cells,
                lax.ppermute(head, axis, [((i + 1) % count, i) for i in range(ends)]),
            ],
            axis=dim,
        )
    return cells


def make_basis(harmonic_list, blade_count, ncells, start, count):
    cells = start + jnp.arange(count, dtype=jnp.int32)
    waves = harmonic_list * blade_count[0]
    phase = waves[:, None] * cells[None, :] % ncells
    angle = 2.0 * jnp.pi * phase.astype(jnp.float32) / ncells
    return jnp.concatenate([jnp.cos(angle), jnp.sin(angle)], axis=0)


def apply_jac(matrix, field):
    return jnp.einsum("uv,vsat->usat", matrix, field, precision=lax.Precision.HIGHEST)


def combine_terms(
    flux_jacobian, field, span_plus, span_minus, axial_plus, axial_minus, theta_plus, theta_minus
):
    total = apply_jac(flux_jacobian[0], (axial_plus - axial_minus) * 0.5)
    total = total + apply_jac(flux_jacobian[1], (span_plus - span_minus) * 0.5)
    total = total + apply_jac(flux_jacobian[2], (theta_plus - theta_minus) * 0.5)
    second = (
        axial_plus
        + axial_minus
        + (span_plus + span_minus)
        + (theta_plus + theta_minus)
        - 6.0 * field
    )
    return total - DISSIP * second


def operate(field, ghost, is_first, flux_jacobian):
    padded = padded_2(field, (("span", 1), ("axial", 2)), 1, False)
    circ_padded = padded_2(field, (("circ", 3),), 1, True)
    span_plus = padded[:, 2:, 1:-1, :]
    span_minus = padded[:, :-2, 1:-1, :]
    axial_plus = padded[:, 1:-1, 2:, :]
    lower_layer = jnp.where(is_first, ghost[:, :, None, :], padded[:, 1:-1, 0:1, :])
    axial_minus = jnp.concatenate([lower_layer, field[:, :, :-1]], axis=2)
    theta_plus = circ_padded[:, :, :, 2:]
    theta_minus = circ_padded[:, :, :, :-2]
    return combine_terms(
        flux_jacobian,
        field,
        span_plus,
        span_minus,
        axial_plus,
        axial_minus,
        theta_plus,
        theta_minus,
    )


def local(
    rotor_outlet,
    blade_count,
    harmonic_list,
    donor_index,
    donor_weight,
    state,
    time_step,
    flux_jacobian,
):
    n_circ = lax.axis_size("circ")
    n_span = lax.axis_size("span")
    n_axial = lax.axis_size("axial")
    local_cells = state.shape[3]
    ncells = local_cells * n_circ
    start = lax.axis_index("circ") * local_cells
    nvars = rotor_outlet.shape[0]
    stations = rotor_outlet.shape[1] // n_circ
    whole_outlet = lax.all_to_all(rotor_outlet, "circ", split_axis=1, concat_axis=2, tiled=True)
    full_basis = make_basis(harmonic_list, blade_count, ncells, 0, ncells)
    coef = (
        2.0
        / ncells
        * jnp.einsum("vrj,kj->vrk", whole_outlet, full_basis, precision=lax.Precision.HIGHEST)
    )
    modes = coef.shape[2]
    gathered = lax.all_gather(coef, ("circ", "span", "axial"), axis=1, tiled=True)
    gathered = gathered.reshape(nvars, n_circ, n_span * n_axial, stations, modes)
    station_table = jnp.transpose(gathered, (0, 2, 1, 3, 4)).reshape(
        nvars, n_circ * n_span * n_axial * stations, modes
    )
    lower = jnp.take(station_table, donor_index, axis=1)
    upper = jnp.take(station_table, donor_index + 1, axis=1)
    weight = donor_weight[None, :, None]
    inter = (1.0 - weight) * lower + weight * upper
    is_first = lax.axis_index("axial") == 0
    own_basis = make_basis(harmonic_list, blade_count, ncells, start, local_cells)
    ghost = jnp.einsum("vsk,kj->vsj", inter, own_basis, precision=lax.Precision.HIGHEST)
    residual = operate(state, ghost, is_first, flux_jacobian)
    field = state - SEGMENT_COEF[0] * time_step[None] * residual
    for segment in range(1, SEGMENTS):
        field = state - SEGMENT_COEF[segment] * time_step[None] * operate(
            field, ghost, is_first, flux_jacobian
        )
    return (field, residual)


def solution(mesh):
    return jax.shard_map(
        local,
        mesh=mesh,
        in_specs=(
            P(None, ("span", "axial"), "circ"),
            P(),
            P(),
            P("span"),
            P("span"),
            P(None, "span", "axial", "circ"),
            P("span", "axial", "circ"),
            P(),
        ),
        out_specs=(P(None, "span", "axial", "circ"), P(None, "span", "axial", "circ")),
        check_vma=False,
    )
```

profile of v0, /device:TPU:1, one launch (start us, length us, event | category | flops | bytes accessed | tf_op | source)
XLA Modules:
  0.0 282.6 jit_solution(15269675486514689491)
XLA Ops:
  2.1 4.5 %collective-permute-start = (f32[5,1,16,128]{3,1,0,2:T(1,128)}, f32[5,1,16,128]{3,1,0,2:T(1,128)S(1)}, u32[]{:S(2)}, u32[]{:S(2)}) collective-permute-start(f32[5,1,16,128]{3,1,0,2:T(1,128)} %copy.186), channel_id=1, source_target_pairs={{0,2},{2,4},{4,6},{1,3},{3,5},{5,7},{8,10},{10,12},{12,14},{9,11},... | collective-permute-start | bytes 122888 | tf_op jit(solution)/shard_map/ppermute | solution.py:21
  7.3 1.9 collective-permute-start.1
  10.5 4.6 %all-to-all-start = ((f32[5,8,128]{2,0,1:T(8,128)}), f32[5,8,128]{2,0,1:T(8,128)S(1)}, u32[]{:S(2)}, u32[]{:S(2)}) async-start(f32[5,8,128]{2,0,1:T(8,128)} %copy.189), calls=%async_computation | async-start | bytes 65536 | tf_op jit(solution)/shard_map/all_to_all | solution.py:98
  15.1 2.3 fusion.68
  18.7 3.3 %collective-permute-start.4 = (f32[5,32,16,1]{1,2,3,0:T(8,128)}, f32[5,32,16,1]{1,2,3,0:T(8,128)}, u32[]{:S(2)}, u32[]{:S(2)}) collective-permute-start(f32[5,32,16,1]{1,2,3,0:T(8,128)} %copy.257), channel_id=1, source_target_pairs={{8,0},{16,8},{24,16},{0,24},{9,1},{17,9},{25,17},{1,25},{10,2},{18... | collective-permute-start | bytes 30728 | tf_op jit(solution)/shard_map/ppermute | solution.py:23
  29.2 2.4 copy.208
  31.6 2.4 copy.210
  34.8 3.8 %collective-permute-start.3 = (f32[5,34,1,128]{3,1,0,2:T(8,128)}, f32[5,34,1,128]{3,1,0,2:T(8,128)}, u32[]{:S(2)}, u32[]{:S(2)}) collective-permute-start(f32[5,34,1,128]{3,1,0,2:T(8,128)} %get-tuple-element.30), channel_id=1, source_target_pairs={{0,1},{2,3},{4,5},{6,7},{8,9},{10,11},{12,13},{14,15},{16,17},{18,... | collective-permute-start | bytes 261128 | tf_op jit(solution)/shard_map/ppermute | solution.py:21
  38.7 63.2 %all_gather.3 = f32[5,64,16]{2,0,1:T(8,128)S(1)} all-gather(f32[5,2,16]{2,0,1:T(8,128)S(1)} %fusion.30), channel_id=1, replica_groups=mesh['circ'=4,'span'=4,'axial'=2] {'circ','span','axial'}, dimensions={1}, use_global_device_ids=true | all-gather | bytes 21120 | tf_op jit(solution)/shard_map/all_gather | solution.py:106
  106.6 1.5 collective-permute-start.2
  109.4 2.8 collective-permute-done.2
  112.2 3.6 %subtract_multiply_fusion.11 = (f32[5,32,16,128]{3,1,0,2:T(8,128)S(1)}, f32[5,32,16,128]{3,1,0,2:T(8,128)S(1)}, f32[5,32,16,128]{3,1,0,2:T(8,128)S(1)}) fusion(f32[5,32,15,128]{3,1,0,2:T(8,128)} %slice.250, f32[5,32,1,128]{3,1,0,2:T(8,128)S(1)} %get-tuple-element.62, f32[5,34,1,128]{3,1,0,2:T(8,128)S(1)} %collective-permute-done.2, ...), kind=kLoop, calls=%fused_computation.88 | loop fusion | flops 4587520 | bytes 6743040 | tf_op jit(solution)/shard_map/mul | solution.py:45
  115.9 2.8 fusion.18
  118.7 2.8 fusion.20
  121.5 2.8 fusion.22
  124.4 5.9 %multiply_subtract_fusion = (f32[5,32,16,128]{3,1,0,2:T(8,128)S(1)}, f32[5,32,16,128]{3,1,0,2:T(8,128)}) fusion(f32[32,16,128]{2,0,1:T(8,128)S(1)} %copy-done.20, f32[5,32,16,128]{3,2,1,0:T(8,128)S(1)} %copy-done, f32[5,32,16,128]{3,1,0,2:T(8,128)S(1)} %copy-done.6, f32[5,32,16,1]{3,1,0,2:T(8,128)S(1)} %copy-done.14, f32[5,32,16,1]{3,1,0,2:T(8,128)S(1)} %copy-done.13, ...), kind=kLoop, calls=%fused_computation.85 | loop fusion | flops 6881280 | bytes 10937344 | tf_op jit(solution)/shard_map/sub | solution.py:119
  130.4 1.9 collective-permute-start.6
  132.3 5.8 %collective-permute-start.7 = (f32[5,1,16,128]{3,1,0,2:T(1,128)S(1)}, f32[5,1,16,128]{3,1,0,2:T(1,128)S(1)}, u32[]{:S(2)}, u32[]{:S(2)}) collective-permute-start(f32[5,1,16,128]{3,1,0,2:T(1,128)S(1)} %get-tuple-element.43), channel_id=1, source_target_pairs={{2,0},{4,2},{6,4},{3,1},{5,3},{7,5},{10,8},{12,10},{14,12},{11,9},... | collective-permute-start | bytes 122888 | tf_op jit(solution)/shard_map/ppermute | solution.py:23
  139.7 2.0 collective-permute-start.9
  141.7 2.0 fusion.66
  143.7 2.5 copy.221
  146.1 2.5 copy.223
  148.6 1.5 collective-permute-start.11
  152.3 2.4 copy.222
  154.6 2.4 copy.224
  159.2 3.4 %collective-permute-done.8 = f32[5,34,1,128]{3,1,0,2:T(8,128)S(1)} collective-permute-done((f32[5,34,1,128]{3,1,0,2:T(8,128)}, f32[5,34,1,128]{3,1,0,2:T(8,128)S(1)}, u32[]{:S(2)}, u32[]{:S(2)}) %collective-permute-start.8) | collective-permute-done | bytes 87072 | tf_op jit(solution)/shard_map/ppermute | solution.py:23
  162.6 3.6 %subtract_multiply_fusion.8 = (f32[5,32,16,128]{3,1,0,2:T(8,128)S(1)}, f32[5,32,16,128]{3,1,0,2:T(8,128)S(1)}, f32[5,32,16,128]{3,1,0,2:T(8,128)S(1)}) fusion(f32[5,32,15,128]{3,1,0,2:T(8,128)} %slice.254, f32[5,32,1,128]{3,1,0,2:T(8,128)S(1)} %slice_select_fusion.2, f32[5,34,1,128]{3,1,0,2:T(8,128)S(1)} %collective-permute-done.8, ...), kind=kLoop, calls=%fused_computation.84 | loop fusion | flops 4587520 | bytes 6743040 | tf_op jit(solution)/shard_map/mul | solution.py:45
  166.3 2.8 %fusion.14 = f32[32,16,128,5]{2,3,1,0:T(8,128)S(1)} fusion(f32[5,32,16,128]{3,1,0,2:T(8,128)S(1)} %get-tuple-element.24, f32[1,5,5]{2,0,1:T(1,128)S(1)} %get-tuple-element.55), kind=kOutput, calls=%fused_computation.16 | convolution fusion | flops 19660800 | bytes 2621540 | tf_op jit(solution)/shard_map/uv,vsat->usat/dot_general | solution.py:39
  169.1 2.8 fusion.16
  172.0 2.8 fusion.12
  174.8 4.6 %fusion.29 = f32[5,32,16,128]{3,1,0,2:T(8,128)S(1)} fusion(f32[32,16,128,5]{2,3,1,0:T(8,128)S(1)} %fusion.12, f32[32,16,128,5]{2,3,1,0:T(8,128)S(1)} %fusion.14, f32[32,16,128,5]{2,3,1,0:T(8,128)S(1)} %fusion.16, f32[5,32,16,128]{3,1,0,2:T(8,128)S(1)} %copy-done.4, f32[5,32,15,128]{3,1,0,2:T(8,128)S(1)} %copy-done.16, ...), kind=kLoop, calls=%fused_computation.66 | loop fusion | flops 6881280 | bytes 9626624 | tf_op jit(solution)/shard_map/sub | solution.py:121
  179.5 2.8 collective-permute-start.12
  182.3 2.7 collective-permute-start.13
  185.1 2.6 collective-permute-done.13
  188.4 2.0 collective-permute-start.15
  190.3 2.0 fusion.64
  192.3 2.5 copy.232
  194.8 1.5 collective-permute-start.16
  196.3 2.5 copy.234
  200.0 2.4 copy.233
  203.8 2.4 copy.235
  208.4 3.7 %collective-permute-done.14 = f32[5,34,1,128]{3,1,0,2:T(8,128)S(1)} collective-permute-done((f32[5,34,1,128]{3,1,0,2:T(8,128)S(1)}, f32[5,34,1,128]{3,1,0,2:T(8,128)S(1)}, u32[]{:S(2)}, u32[]{:S(2)}) %collective-permute-start.14) | collective-permute-done | bytes 87072 | tf_op jit(solution)/shard_map/ppermute | solution.py:23
  212.2 3.6 %subtract_multiply_fusion.5 = (f32[5,32,16,128]{3,1,0,2:T(8,128)S(1)}, f32[5,32,16,128]{3,1,0,2:T(8,128)S(1)}, f32[5,32,16,128]{3,1,0,2:T(8,128)S(1)}) fusion(f32[5,32,15,128]{3,1,0,2:T(8,128)} %slice.260, f32[5,32,1,128]{3,1,0,2:T(8,128)S(1)} %slice_select_fusion.1, f32[5,34,1,128]{3,1,0,2:T(8,128)S(1)} %collective-permute-done.14, ...), kind=kLoop, calls=%fused_computation.81 | loop fusion | flops 4587520 | bytes 6743040 | tf_op jit(solution)/shard_map/mul | solution.py:45
  215.8 2.8 %fusion.10 = f32[32,16,128,5]{2,3,1,0:T(8,128)S(1)} fusion(f32[5,32,16,128]{3,1,0,2:T(8,128)S(1)} %get-tuple-element.19, f32[1,5,5]{2,0,1:T(1,128)S(1)} %get-tuple-element.54), kind=kOutput, calls=%fused_computation.12 | convolution fusion | flops 19660800 | bytes 2621540 | tf_op jit(solution)/shard_map/uv,vsat->usat/dot_general | solution.py:39
  218.6 2.8 fusion.8
  221.5 2.8 fusion.6
  224.3 4.7 %fusion.27 = f32[5,32,16,128]{3,1,0,2:T(8,128)S(1)} fusion(f32[32,16,128,5]{2,3,1,0:T(8,128)S(1)} %fusion.6, f32[32,16,128,5]{2,3,1,0:T(8,128)S(1)} %fusion.8, f32[32,16,128,5]{2,3,1,0:T(8,128)S(1)} %fusion.10, f32[5,32,16,128]{3,1,0,2:T(8,128)S(1)} %copy-done.2, f32[5,32,15,128]{3,1,0,2:T(8,128)S(1)} %copy-done.17, ...), kind=kLoop, calls=%fused_computation.63 | loop fusion | flops 6881280 | bytes 9626624 | tf_op jit(solution)/shard_map/sub | solution.py:121
  229.1 4.1 %collective-permute-start.18 = (f32[5,1,16,128]{3,1,0,2:T(1,128)S(1)}, f32[5,1,16,128]{3,1,0,2:T(1,128)S(1)}, u32[]{:S(2)}, u32[]{:S(2)}) collective-permute-start(f32[5,1,16,128]{3,1,0,2:T(1,128)S(1)} %get-tuple-element.32), channel_id=1, source_target_pairs={{0,2},{2,4},{4,6},{1,3},{3,5},{5,7},{8,10},{10,12},{12,14},{9,11},... | collective-permute-start | bytes 122888 | tf_op jit(solution)/shard_map/ppermute | solution.py:21
  233.2 1.9 collective-permute-start.19
  235.2 3.4 %collective-permute-done.19 = f32[5,1,16,128]{3,1,0,2:T(1,128)S(1)} collective-permute-done((f32[5,1,16,128]{3,1,0,2:T(1,128)S(1)}, f32[5,1,16,128]{3,1,0,2:T(1,128)S(1)}, u32[]{:S(2)}, u32[]{:S(2)}) %collective-permute-start.19) | collective-permute-done | bytes 40992 | tf_op jit(solution)/shard_map/ppermute | solution.py:23
  238.6 1.9 collective-permute-start.21
  240.5 2.0 fusion.62
  242.5 2.5 copy.243
  246.0 2.5 copy.245
  249.0 3.1 %copy.251 = f32[5,32,16,128]{3,2,1,0:T(8,128)} copy(f32[5,32,16,128]{3,1,0,2:T(8,128)} %get-tuple-element.12) | data formatting | bytes 2621440
  253.2 2.4 copy.244
  255.7 2.4 copy.246
  260.2 3.3 %collective-permute-done.20 = f32[5,34,1,128]{3,1,0,2:T(8,128)S(1)} collective-permute-done((f32[5,34,1,128]{3,1,0,2:T(8,128)S(1)}, f32[5,34,1,128]{3,1,0,2:T(8,128)S(1)}, u32[]{:S(2)}, u32[]{:S(2)}) %collective-permute-start.20) | collective-permute-done | bytes 87072 | tf_op jit(solution)/shard_map/ppermute | solution.py:23
  263.6 3.6 %subtract_multiply_fusion.2 = (f32[5,32,16,128]{3,1,0,2:T(8,128)S(1)}, f32[5,32,16,128]{3,1,0,2:T(8,128)S(1)}, f32[5,32,16,128]{3,1,0,2:T(8,128)S(1)}) fusion(f32[5,32,15,128]{3,1,0,2:T(8,128)} %slice.266, f32[5,32,1,128]{3,1,0,2:T(8,128)S(1)} %slice_select_fusion, f32[5,34,1,128]{3,1,0,2:T(8,128)S(1)} %collective-permute-done.20, ...), kind=kLoop, calls=%fused_computation.78 | loop fusion | flops 4587520 | bytes 6743040 | tf_op jit(solution)/shard_map/mul | solution.py:45
  267.2 2.8 %fusion.2 = f32[32,16,128,5]{2,3,1,0:T(8,128)S(1)} fusion(f32[5,32,16,128]{3,1,0,2:T(8,128)S(1)} %get-tuple-element.16, f32[1,5,5]{2,0,1:T(1,128)S(1)} %get-tuple-element.55), kind=kOutput, calls=%fused_computation.4 | convolution fusion | flops 19660800 | bytes 2621540 | tf_op jit(solution)/shard_map/uv,vsat->usat/dot_general | solution.py:39
  270.1 2.8 fusion.4
  272.9 2.8 fusion
  275.7 4.6 %fusion.25 = f32[5,32,16,128]{3,1,0,2:T(8,128)S(1)} fusion(f32[32,16,128,5]{2,3,1,0:T(8,128)S(1)} %fusion, f32[32,16,128,5]{2,3,1,0:T(8,128)S(1)} %fusion.2, f32[32,16,128,5]{2,3,1,0:T(8,128)S(1)} %fusion.4, f32[5,32,16,128]{3,1,0,2:T(8,128)S(1)} %fusion.27, f32[5,32,15,128]{3,1,0,2:T(8,128)S(1)} %copy-done.15, f32[5,32,1,128]{3,1,0,2:T(8,128)S(1)} %slice_select_fusion, ...), kind=kLoop, calls=%fused_computation.60 | loop fusion | flops 6881280 | bytes 9626624 | tf_op jit(solution)/shard_map/sub | solution.py:121
  280.3 1.8 copy.250
  (141 shorter events, 34.7 us)
Async XLA Ops:
  2.1 32.0 %collective-permute-start = (f32[5,1,16,128]{3,1,0,2:T(1,128)}, f32[5,1,16,128]{3,1,0,2:T(1,128)S(1)}, u32[]{:S(2)}, u32[]{:S(2)}) collective-permute-start(f32[5,1,16,128]{3,1,0,2:T(1,128)} %copy.186), channel_id=1, source_target_pairs={{0,2},{2,4},{4,6},{1,3},{3,5},{5,7},{8,10},{10,12},{12,14},{9,11},... | collective-permute-start | bytes 122888 | tf_op jit(solution)/shard_map/ppermute | solution.py:21
  7.3 26.8 %collective-permute-start.1 = (f32[5,1,16,128]{3,1,0,2:T(1,128)}, f32[5,1,16,128]{3,1,0,2:T(1,128)S(1)}, u32[]{:S(2)}, u32[]{:S(2)}) collective-permute-start(f32[5,1,16,128]{3,1,0,2:T(1,128)} %copy.187), channel_id=1, source_target_pairs={{2,0},{4,2},{6,4},{3,1},{5,3},{7,5},{10,8},{12,10},{14,12},{11,9},... | collective-permute-start | bytes 122888 | tf_op jit(solution)/shard_map/ppermute | solution.py:23
  10.5 23.5 %all-to-all-start = ((f32[5,8,128]{2,0,1:T(8,128)}), f32[5,8,128]{2,0,1:T(8,128)S(1)}, u32[]{:S(2)}, u32[]{:S(2)}) async-start(f32[5,8,128]{2,0,1:T(8,128)} %copy.189), calls=%async_computation | async-start | bytes 65536 | tf_op jit(solution)/shard_map/all_to_all | solution.py:98
  17.5 5.8 %copy-start.32 = (s32[32]{0:T(128)S(1)}, s32[32]{0:T(128)}, u32[]{:S(2)}) copy-start(s32[32]{0:T(128)} %param.13) | copy-start | bytes 388
  17.5 6.9 %copy-start.33 = (s32[8]{0:T(128)S(1)}, s32[8]{0:T(128)}, u32[]{:S(2)}) copy-start(s32[8]{0:T(128)} %param.12) | copy-start | bytes 100
  17.5 7.8 %copy-start.31 = (f32[32]{0:T(128)S(1)}, f32[32]{0:T(128)}, u32[]{:S(2)}) copy-start(f32[32]{0:T(128)} %param.14) | copy-start | bytes 388
  17.5 8.4 %copy-start.30 = (f32[3,5,5]{2,0,1:T(4,128)S(1)}, f32[3,5,5]{2,0,1:T(4,128)}, u32[]{:S(2)}) copy-start(f32[3,5,5]{2,0,1:T(4,128)} %param.17) | copy-start | bytes 904
  17.5 8.4 %copy-start.19 = (f32[32,16,128]{2,1,0:T(8,128)S(1)}, f32[32,16,128]{2,1,0:T(8,128)}, u32[]{:S(2)}) copy-start(f32[32,16,128]{2,1,0:T(8,128)} %param.16) | copy-start | bytes 786436
  18.7 8.0 %copy-start = (f32[5,32,16,128]{3,2,1,0:T(8,128)S(1)}, f32[5,32,16,128]{3,2,1,0:T(8,128)}, u32[]{:S(2)}) copy-start(f32[5,32,16,128]{3,2,1,0:T(8,128)} %param.15) | copy-start | bytes 3932164
  18.7 10.4 %collective-permute-start.4 = (f32[5,32,16,1]{1,2,3,0:T(8,128)}, f32[5,32,16,1]{1,2,3,0:T(8,128)}, u32[]{:S(2)}, u32[]{:S(2)}) collective-permute-start(f32[5,32,16,1]{1,2,3,0:T(8,128)} %copy.257), channel_id=1, source_target_pairs={{8,0},{16,8},{24,16},{0,24},{9,1},{17,9},{25,17},{1,25},{10,2},{18... | collective-permute-start | bytes 30728 | tf_op jit(solution)/shard_map/ppermute | solution.py:23
  23.2 8.4 %collective-permute-start.5 = (f32[5,32,16,1]{1,2,3,0:T(8,128)}, f32[5,32,16,1]{1,2,3,0:T(8,128)}, u32[]{:S(2)}, u32[]{:S(2)}) collective-permute-start(f32[5,32,16,1]{1,2,3,0:T(8,128)} %copy.258), channel_id=1, source_target_pairs={{0,8},{8,16},{16,24},{24,0},{1,9},{9,17},{17,25},{25,1},{2,10},{10... | collective-permute-start | bytes 30728 | tf_op jit(solution)/shard_map/ppermute | solution.py:21
  27.2 85.1 %copy-start.5 = (f32[5,32,16,128]{3,1,0,2:T(8,128)}, f32[5,32,16,128]{3,1,0,2:T(8,128)S(1)}, u32[]{:S(2)}) copy-start(f32[5,32,16,128]{3,1,0,2:T(8,128)S(1)} %copy.249) | copy-start | bytes 3932164
  31.6 7.0 %copy-start.28 = (f32[8,512]{1,0:T(8,128)S(1)}, f32[8,512]{1,0:T(8,128)}, u32[]{:S(2)}) copy-start(f32[8,512]{1,0:T(8,128)} %get-tuple-element.60) | copy-start | bytes 49156
  31.6 7.0 %copy-start.29 = (f32[8,512]{1,0:T(8,128)S(1)}, f32[8,512]{1,0:T(8,128)}, u32[]{:S(2)}) copy-start(f32[8,512]{1,0:T(8,128)} %get-tuple-element.61) | copy-start | bytes 49156
  34.1 78.2 %copy-start.25 = (f32[5,1,16,128]{3,1,0,2:T(1,128)}, f32[5,1,16,128]{3,1,0,2:T(1,128)S(1)}, u32[]{:S(2)}) copy-start(f32[5,1,16,128]{3,1,0,2:T(1,128)S(1)} %collective-permute-done.1) | copy-start | bytes 122884
  34.8 73.3 %collective-permute-start.3 = (f32[5,34,1,128]{3,1,0,2:T(8,128)}, f32[5,34,1,128]{3,1,0,2:T(8,128)}, u32[]{:S(2)}, u32[]{:S(2)}) collective-permute-start(f32[5,34,1,128]{3,1,0,2:T(8,128)} %get-tuple-element.30), channel_id=1, source_target_pairs={{0,1},{2,3},{4,5},{6,7},{8,9},{10,11},{12,13},{14,15},{16,17},{18,... | collective-permute-start | bytes 261128 | tf_op jit(solution)/shard_map/ppermute | solution.py:21
  106.6 5.6 %collective-permute-start.2 = (f32[5,34,1,128]{3,1,0,2:T(8,128)}, f32[5,34,1,128]{3,1,0,2:T(8,128)S(1)}, u32[]{:S(2)}, u32[]{:S(2)}) collective-permute-start(f32[5,34,1,128]{3,1,0,2:T(8,128)} %get-tuple-element.29), channel_id=1, source_target_pairs={{1,0},{3,2},{5,4},{7,6},{9,8},{11,10},{13,12},{15,14},{17,16},{19,... | collective-permute-start | bytes 261128 | tf_op jit(solution)/shard_map/ppermute | solution.py:23
  118.7 5.7 %copy-start.18 = (f32[5,32,15,128]{3,1,0,2:T(8,128)S(1)}, f32[5,32,15,128]{3,1,0,2:T(8,128)}, u32[]{:S(2)}) copy-start(f32[5,32,15,128]{3,1,0,2:T(8,128)} %slice.250) | copy-start | bytes 3686404
  118.7 5.7 %copy-start.26 = (f32[5,1,16,128]{3,1,0,2:T(1,128)S(1)}, f32[5,1,16,128]{3,1,0,2:T(1,128)}, u32[]{:S(2)}) copy-start(f32[5,1,16,128]{3,1,0,2:T(1,128)} %copy-done.25) | copy-start | bytes 122884
  121.5 2.9 %copy-start.6 = (f32[5,32,16,128]{3,1,0,2:T(8,128)S(1)}, f32[5,32,16,128]{3,1,0,2:T(8,128)}, u32[]{:S(2)}) copy-start(f32[5,32,16,128]{3,1,0,2:T(8,128)} %copy-done.5) | copy-start | bytes 3932164
  121.5 2.9 %copy-start.13 = (f32[5,32,16,1]{3,1,0,2:T(8,128)S(1)}, f32[5,32,16,1]{3,1,0,2:T(8,128)}, u32[]{:S(2)}) copy-start(f32[5,32,16,1]{3,1,0,2:T(8,128)} %copy.208) | copy-start | bytes 30724
  121.5 2.9 %copy-start.14 = (f32[5,32,16,1]{3,1,0,2:T(8,128)S(1)}, f32[5,32,16,1]{3,1,0,2:T(8,128)}, u32[]{:S(2)}) copy-start(f32[5,32,16,1]{3,1,0,2:T(8,128)} %copy.210) | copy-start | bytes 30724
  121.5 2.9 %copy-start.20 = (f32[32,16,128]{2,0,1:T(8,128)S(1)}, f32[32,16,128]{2,0,1:T(8,128)}, u32[]{:S(2)}) copy-start(f32[32,16,128]{2,0,1:T(8,128)} %copy.185) | copy-start | bytes 786436
  130.3 32.3 %copy-start.3 = (f32[5,32,16,128]{3,1,0,2:T(8,128)}, f32[5,32,16,128]{3,1,0,2:T(8,128)S(1)}, u32[]{:S(2)}) copy-start(f32[5,32,16,128]{3,1,0,2:T(8,128)S(1)} %get-tuple-element.11) | copy-start | bytes 3932164
  130.4 7.8 %collective-permute-start.6 = (f32[5,1,16,128]{3,1,0,2:T(1,128)S(1)}, f32[5,1,16,128]{3,1,0,2:T(1,128)S(1)}, u32[]{:S(2)}, u32[]{:S(2)}) collective-permute-start(f32[5,1,16,128]{3,1,0,2:T(1,128)S(1)} %get-tuple-element.42), channel_id=1, source_target_pairs={{0,2},{2,4},{4,6},{1,3},{3,5},{5,7},{8,10},{10,12},{12,14},{9,11},... | collective-permute-start | bytes 122888 | tf_op jit(solution)/shard_map/ppermute | solution.py:21
  132.3 6.7 %collective-permute-start.7 = (f32[5,1,16,128]{3,1,0,2:T(1,128)S(1)}, f32[5,1,16,128]{3,1,0,2:T(1,128)S(1)}, u32[]{:S(2)}, u32[]{:S(2)}) collective-permute-start(f32[5,1,16,128]{3,1,0,2:T(1,128)S(1)} %get-tuple-element.43), channel_id=1, source_target_pairs={{2,0},{4,2},{6,4},{3,1},{5,3},{7,5},{10,8},{12,10},{14,12},{11,9},... | collective-permute-start | bytes 122888 | tf_op jit(solution)/shard_map/ppermute | solution.py:23
  139.0 4.7 %copy-start.21 = (f32[5,1,16,128]{3,1,0,2:T(1,128)}, f32[5,1,16,128]{3,1,0,2:T(1,128)S(1)}, u32[]{:S(2)}) copy-start(f32[5,1,16,128]{3,1,0,2:T(1,128)S(1)} %collective-permute-done.7) | copy-start | bytes 122884
  139.7 18.6 %collective-permute-start.9 = (f32[5,34,1,128]{3,1,0,2:T(8,128)}, f32[5,34,1,128]{3,1,0,2:T(8,128)}, u32[]{:S(2)}, u32[]{:S(2)}) collective-permute-start(f32[5,34,1,128]{3,1,0,2:T(8,128)} %get-tuple-element.26), channel_id=1, source_target_pairs={{0,1},{2,3},{4,5},{6,7},{8,9},{10,11},{12,13},{14,15},{16,17},{18,... | collective-permute-start | bytes 261128 | tf_op jit(solution)/shard_map/ppermute | solution.py:21
  146.1 6.1 %collective-permute-start.10 = (f32[5,32,16,1]{1,2,3,0:T(8,128)}, f32[5,32,16,1]{1,2,3,0:T(8,128)}, u32[]{:S(2)}, u32[]{:S(2)}) collective-permute-start(f32[5,32,16,1]{1,2,3,0:T(8,128)} %copy.221), channel_id=1, source_target_pairs={{8,0},{16,8},{24,16},{0,24},{9,1},{17,9},{25,17},{1,25},{10,2},{18... | collective-permute-start | bytes 30728 | tf_op jit(solution)/shard_map/ppermute | solution.py:23
  148.6 6.0 %collective-permute-start.11 = (f32[5,32,16,1]{1,2,3,0:T(8,128)}, f32[5,32,16,1]{1,2,3,0:T(8,128)}, u32[]{:S(2)}, u32[]{:S(2)}) collective-permute-start(f32[5,32,16,1]{1,2,3,0:T(8,128)} %copy.223), channel_id=1, source_target_pairs={{0,8},{8,16},{16,24},{24,0},{1,9},{9,17},{17,25},{25,1},{2,10},{10... | collective-permute-start | bytes 30728 | tf_op jit(solution)/shard_map/ppermute | solution.py:21
  157.0 5.6 %collective-permute-start.8 = (f32[5,34,1,128]{3,1,0,2:T(8,128)}, f32[5,34,1,128]{3,1,0,2:T(8,128)S(1)}, u32[]{:S(2)}, u32[]{:S(2)}) collective-permute-start(f32[5,34,1,128]{3,1,0,2:T(8,128)} %get-tuple-element.25), channel_id=1, source_target_pairs={{1,0},{3,2},{5,4},{7,6},{9,8},{11,10},{13,12},{15,14},{17,16},{19,... | collective-permute-start | bytes 261128 | tf_op jit(solution)/shard_map/ppermute | solution.py:23
  169.1 5.7 %copy-start.16 = (f32[5,32,15,128]{3,1,0,2:T(8,128)S(1)}, f32[5,32,15,128]{3,1,0,2:T(8,128)}, u32[]{:S(2)}) copy-start(f32[5,32,15,128]{3,1,0,2:T(8,128)} %slice.254) | copy-start | bytes 3686404
  171.9 2.9 %copy-start.4 = (f32[5,32,16,128]{3,1,0,2:T(8,128)S(1)}, f32[5,32,16,128]{3,1,0,2:T(8,128)}, u32[]{:S(2)}) copy-start(f32[5,32,16,128]{3,1,0,2:T(8,128)} %copy-done.3) | copy-start | bytes 3932164
  172.0 2.9 %copy-start.8 = (f32[5,32,16,1]{3,1,0,2:T(8,128)S(1)}, f32[5,32,16,1]{3,1,0,2:T(8,128)}, u32[]{:S(2)}) copy-start(f32[5,32,16,1]{3,1,0,2:T(8,128)} %copy.222) | copy-start | bytes 30724
  172.0 2.9 %copy-start.11 = (f32[5,32,16,1]{3,1,0,2:T(8,128)S(1)}, f32[5,32,16,1]{3,1,0,2:T(8,128)}, u32[]{:S(2)}) copy-start(f32[5,32,16,1]{3,1,0,2:T(8,128)} %copy.224) | copy-start | bytes 30724
  172.0 2.9 %copy-start.22 = (f32[5,1,16,128]{3,1,0,2:T(1,128)S(1)}, f32[5,1,16,128]{3,1,0,2:T(1,128)}, u32[]{:S(2)}) copy-start(f32[5,1,16,128]{3,1,0,2:T(1,128)} %copy-done.21) | copy-start | bytes 122884
  179.4 32.7 %copy-start.1 = (f32[5,32,16,128]{3,1,0,2:T(8,128)}, f32[5,32,16,128]{3,1,0,2:T(8,128)S(1)}, u32[]{:S(2)}) copy-start(f32[5,32,16,128]{3,1,0,2:T(8,128)S(1)} %fusion.29) | copy-start | bytes 3932164
  179.5 5.6 %collective-permute-start.12 = (f32[5,1,16,128]{3,1,0,2:T(1,128)S(1)}, f32[5,1,16,128]{3,1,0,2:T(1,128)S(1)}, u32[]{:S(2)}, u32[]{:S(2)}) collective-permute-start(f32[5,1,16,128]{3,1,0,2:T(1,128)S(1)} %get-tuple-element.37), channel_id=1, source_target_pairs={{0,2},{2,4},{4,6},{1,3},{3,5},{5,7},{8,10},{10,12},{12,14},{9,11},... | collective-permute-start | bytes 122888 | tf_op jit(solution)/shard_map/ppermute | solution.py:21
  182.3 5.3 %collective-permute-start.13 = (f32[5,1,16,128]{3,1,0,2:T(1,128)S(1)}, f32[5,1,16,128]{3,1,0,2:T(1,128)S(1)}, u32[]{:S(2)}, u32[]{:S(2)}) collective-permute-start(f32[5,1,16,128]{3,1,0,2:T(1,128)S(1)} %get-tuple-element.38), channel_id=1, source_target_pairs={{2,0},{4,2},{6,4},{3,1},{5,3},{7,5},{10,8},{12,10},{14,12},{11,9},... | collective-permute-start | bytes 122888 | tf_op jit(solution)/shard_map/ppermute | solution.py:23
  187.6 4.7 %copy-start.23 = (f32[5,1,16,128]{3,1,0,2:T(1,128)}, f32[5,1,16,128]{3,1,0,2:T(1,128)S(1)}, u32[]{:S(2)}) copy-start(f32[5,1,16,128]{3,1,0,2:T(1,128)S(1)} %collective-permute-done.13) | copy-start | bytes 122884
  188.4 19.1 %collective-permute-start.15 = (f32[5,34,1,128]{3,1,0,2:T(8,128)}, f32[5,34,1,128]{3,1,0,2:T(8,128)}, u32[]{:S(2)}, u32[]{:S(2)}) collective-permute-start(f32[5,34,1,128]{3,1,0,2:T(8,128)} %get-tuple-element.22), channel_id=1, source_target_pairs={{0,1},{2,3},{4,5},{6,7},{8,9},{10,11},{12,13},{14,15},{16,17},{18,... | collective-permute-start | bytes 261128 | tf_op jit(solution)/shard_map/ppermute | solution.py:21
  194.8 5.2 %collective-permute-start.16 = (f32[5,32,16,1]{1,2,3,0:T(8,128)}, f32[5,32,16,1]{1,2,3,0:T(8,128)}, u32[]{:S(2)}, u32[]{:S(2)}) collective-permute-start(f32[5,32,16,1]{1,2,3,0:T(8,128)} %copy.232), channel_id=1, source_target_pairs={{8,0},{16,8},{24,16},{0,24},{9,1},{17,9},{25,17},{1,25},{10,2},{18... | collective-permute-start | bytes 30728 | tf_op jit(solution)/shard_map/ppermute | solution.py:23
  198.8 5.1 %collective-permute-start.17 = (f32[5,32,16,1]{1,2,3,0:T(8,128)}, f32[5,32,16,1]{1,2,3,0:T(8,128)}, u32[]{:S(2)}, u32[]{:S(2)}) collective-permute-start(f32[5,32,16,1]{1,2,3,0:T(8,128)} %copy.234), channel_id=1, source_target_pairs={{0,8},{8,16},{16,24},{24,0},{1,9},{9,17},{17,25},{25,1},{2,10},{10... | collective-permute-start | bytes 30728 | tf_op jit(solution)/shard_map/ppermute | solution.py:21
  200.0 6.2 %copy-start.27 = (f32[5,34,1,128]{3,1,0,2:T(8,128)S(1)}, f32[5,34,1,128]{3,1,0,2:T(8,128)}, u32[]{:S(2)}) copy-start(f32[5,34,1,128]{3,1,0,2:T(8,128)} %get-tuple-element.21) | copy-start | bytes 261124
  200.0 12.2 %copy-start.24 = (f32[5,1,16,128]{3,1,0,2:T(1,128)S(1)}, f32[5,1,16,128]{3,1,0,2:T(1,128)}, u32[]{:S(2)}) copy-start(f32[5,1,16,128]{3,1,0,2:T(1,128)} %copy-done.23) | copy-start | bytes 122884
  206.2 6.0 %collective-permute-start.14 = (f32[5,34,1,128]{3,1,0,2:T(8,128)S(1)}, f32[5,34,1,128]{3,1,0,2:T(8,128)S(1)}, u32[]{:S(2)}, u32[]{:S(2)}) collective-permute-start(f32[5,34,1,128]{3,1,0,2:T(8,128)S(1)} %copy-done.27), channel_id=1, source_target_pairs={{1,0},{3,2},{5,4},{7,6},{9,8},{11,10},{13,12},{15,14},{17,16},{19,... | collective-permute-start | bytes 261128 | tf_op jit(solution)/shard_map/ppermute | solution.py:23
  218.6 5.7 %copy-start.17 = (f32[5,32,15,128]{3,1,0,2:T(8,128)S(1)}, f32[5,32,15,128]{3,1,0,2:T(8,128)}, u32[]{:S(2)}) copy-start(f32[5,32,15,128]{3,1,0,2:T(8,128)} %slice.260) | copy-start | bytes 3686404
  221.5 2.8 %copy-start.2 = (f32[5,32,16,128]{3,1,0,2:T(8,128)S(1)}, f32[5,32,16,128]{3,1,0,2:T(8,128)}, u32[]{:S(2)}) copy-start(f32[5,32,16,128]{3,1,0,2:T(8,128)} %copy-done.1) | copy-start | bytes 3932164
  221.5 2.8 %copy-start.9 = (f32[5,32,16,1]{3,1,0,2:T(8,128)S(1)}, f32[5,32,16,1]{3,1,0,2:T(8,128)}, u32[]{:S(2)}) copy-start(f32[5,32,16,1]{3,1,0,2:T(8,128)} %copy.233) | copy-start | bytes 30724
  221.5 2.8 %copy-start.12 = (f32[5,32,16,1]{3,1,0,2:T(8,128)S(1)}, f32[5,32,16,1]{3,1,0,2:T(8,128)}, u32[]{:S(2)}) copy-start(f32[5,32,16,1]{3,1,0,2:T(8,128)} %copy.235) | copy-start | bytes 30724
  229.1 6.0 %collective-permute-start.18 = (f32[5,1,16,128]{3,1,0,2:T(1,128)S(1)}, f32[5,1,16,128]{3,1,0,2:T(1,128)S(1)}, u32[]{:S(2)}, u32[]{:S(2)}) collective-permute-start(f32[5,1,16,128]{3,1,0,2:T(1,128)S(1)} %get-tuple-element.32), channel_id=1, source_target_pairs={{0,2},{2,4},{4,6},{1,3},{3,5},{5,7},{8,10},{10,12},{12,14},{9,11},... | collective-permute-start | bytes 122888 | tf_op jit(solution)/shard_map/ppermute | solution.py:21
  233.2 5.3 %collective-permute-start.19 = (f32[5,1,16,128]{3,1,0,2:T(1,128)S(1)}, f32[5,1,16,128]{3,1,0,2:T(1,128)S(1)}, u32[]{:S(2)}, u32[]{:S(2)}) collective-permute-start(f32[5,1,16,128]{3,1,0,2:T(1,128)S(1)} %get-tuple-element.33), channel_id=1, source_target_pairs={{2,0},{4,2},{6,4},{3,1},{5,3},{7,5},{10,8},{12,10},{14,12},{11,9},... | collective-permute-start | bytes 122888 | tf_op jit(solution)/shard_map/ppermute | solution.py:23
  238.6 20.7 %collective-permute-start.21 = (f32[5,34,1,128]{3,1,0,2:T(8,128)S(1)}, f32[5,34,1,128]{3,1,0,2:T(8,128)}, u32[]{:S(2)}, u32[]{:S(2)}) collective-permute-start(f32[5,34,1,128]{3,1,0,2:T(8,128)S(1)} %get-tuple-element.18), channel_id=1, source_target_pairs={{0,1},{2,3},{4,5},{6,7},{8,9},{10,11},{12,13},{14,15},{16,17},{18,... | collective-permute-start | bytes 261128 | tf_op jit(solution)/shard_map/ppermute | solution.py:21
  244.9 8.3 %collective-permute-start.22 = (f32[5,32,16,1]{1,2,3,0:T(8,128)}, f32[5,32,16,1]{1,2,3,0:T(8,128)}, u32[]{:S(2)}, u32[]{:S(2)}) collective-permute-start(f32[5,32,16,1]{1,2,3,0:T(8,128)} %copy.243), channel_id=1, source_target_pairs={{8,0},{16,8},{24,16},{0,24},{9,1},{17,9},{25,17},{1,25},{10,2},{18... | collective-permute-start | bytes 30728 | tf_op jit(solution)/shard_map/ppermute | solution.py:23
  248.5 7.2 %collective-permute-start.23 = (f32[5,32,16,1]{1,2,3,0:T(8,128)}, f32[5,32,16,1]{1,2,3,0:T(8,128)}, u32[]{:S(2)}, u32[]{:S(2)}) collective-permute-start(f32[5,32,16,1]{1,2,3,0:T(8,128)} %copy.245), channel_id=1, source_target_pairs={{0,8},{8,16},{16,24},{24,0},{1,9},{9,17},{17,25},{25,1},{2,10},{10... | collective-permute-start | bytes 30728 | tf_op jit(solution)/shard_map/ppermute | solution.py:21
  258.0 5.5 %collective-permute-start.20 = (f32[5,34,1,128]{3,1,0,2:T(8,128)S(1)}, f32[5,34,1,128]{3,1,0,2:T(8,128)S(1)}, u32[]{:S(2)}, u32[]{:S(2)}) collective-permute-start(f32[5,34,1,128]{3,1,0,2:T(8,128)S(1)} %get-tuple-element.17), channel_id=1, source_target_pairs={{1,0},{3,2},{5,4},{7,6},{9,8},{11,10},{13,12},{15,14},{17,16},{19,... | collective-permute-start | bytes 261128 | tf_op jit(solution)/shard_map/ppermute | solution.py:23
  272.9 2.8 %copy-start.7 = (f32[5,32,16,1]{3,1,0,2:T(8,128)S(1)}, f32[5,32,16,1]{3,1,0,2:T(8,128)}, u32[]{:S(2)}) copy-start(f32[5,32,16,1]{3,1,0,2:T(8,128)} %copy.244) | copy-start | bytes 30724
  272.9 2.8 %copy-start.10 = (f32[5,32,16,1]{3,1,0,2:T(8,128)S(1)}, f32[5,32,16,1]{3,1,0,2:T(8,128)}, u32[]{:S(2)}) copy-start(f32[5,32,16,1]{3,1,0,2:T(8,128)} %copy.246) | copy-start | bytes 30724
  272.9 2.8 %copy-start.15 = (f32[5,32,15,128]{3,1,0,2:T(8,128)S(1)}, f32[5,32,15,128]{3,1,0,2:T(8,128)}, u32[]{:S(2)}) copy-start(f32[5,32,15,128]{3,1,0,2:T(8,128)} %slice.266) | copy-start | bytes 3686404
where the time goes:
time: 288 us; the launch traced here: 283 us
  local copies, waits for them, and re-layouts  65.1 us (23%)
  blocking collectives  63.2 us (22%)
  starting transfers between devices  53.1 us (18%)
  other arithmetic  42 us (15%)
  matrix products  35.1 us (12%)
  waiting for transfers between devices  21.5 us (7%)
    all_gather x1, blocking collectives, local(): lax.all_gather(coef, ('circ', 'span', 'axial'), axis=1, tiled=True)  63.2 us
    dot_general x12, matrix products, apply_jac(): jnp.einsum('uv,vsat->usat', matrix, field, precision=lax.Precision.HIGHEST)  33.7 us
    ppermute x12, starting transfers between devices, padded_2(): lax.ppermute(tail, axis, [(i, (i + 1) % count) for i in range(ends)])  24.8 us
    ppermute x12, starting transfers between devices, padded_2(): lax.ppermute(head, axis, [((i + 1) % count, i) for i in range(ends)])  23.6 us
    ppermute x12, waiting for transfers between devices, padded_2(): lax.ppermute(head, axis, [((i + 1) % count, i) for i in range(ends)])  20.1 us
    mul x4, other arithmetic, combine_terms(): total = apply_jac(flux_jacobian[0], (axial_plus - axial_minus) * 0.5)  14.5 us
    slice x10, local copies, waits for them, and re-layouts, padded_2(): lax.slice_in_dim(cells, cells.shape[dim] - width, cells.shape[dim], axis=...  14.1 us
    sub x3, other arithmetic, local(): state - SEGMENT_COEF[segment] * time_step[None] * operate(field, ghost, i...  13.9 us
  transfers between devices with their start and end apart: 25, of which 8 were waited for; matrix products, arithmetic and copies ran while one was open for 24% of the time, Pallas kernels for 0%

commit v1 on v0

v1 whole, which is shorter than its diff:
```python
import functools

import jax
import jax.numpy as jnp
import numpy as np
from jax import lax
from jax.experimental import pallas as pl
from jax.experimental.pallas import tpu as pltpu
from jax.sharding import PartitionSpec as P

SEGMENT_COEF = (0.25, 1.0 / 3.0, 0.5, 1.0)
DISSIP = 0.2
W = 4
HIGH = lax.Precision.HIGHEST
VMEM = pl.BlockSpec(memory_space=pltpu.VMEM)
SMEM = pl.BlockSpec(memory_space=pltpu.SMEM)
HBM = pl.BlockSpec(memory_space=pltpu.HBM)
ANY = pl.BlockSpec(memory_space=pl.ANY)
AXES = ("circ", "span", "axial")


def make_basis(harm, blade, nh, cells, ncells):
    width = cells.shape[1]
    row = lax.broadcasted_iota(jnp.int32, (nh, width), 0)
    waves = jnp.zeros((nh, width), jnp.int32)
    for k in range(nh):
        waves = jnp.where(row == k, harm[k] * blade[0], waves)
    phase = waves * cells
    phase = phase & (ncells - 1) if ncells & (ncells - 1) == 0 else phase % ncells
    angle = (2.0 * np.pi) * phase.astype(jnp.float32) / ncells
    return jnp.concatenate([jnp.cos(angle), jnp.sin(angle)], axis=0)


def dot(a, b, dims):
    return lax.dot_general(a, b, (dims, ((), ())), precision=HIGH, preferred_element_type=jnp.float32)


def axial_kernel(dims, state, dt, rotor, blade, harm, edge, bulk, part, *scratch):
    nv, sl, al, cl, nh = (dims[k] for k in ("nv", "sl", "al", "cl", "nh"))
    cells, dt_cells, rotor_v, blade_s, harm_s, sems = scratch
    axial = lax.axis_index("axial")
    circ = lax.axis_index("circ")
    swap = dims["n_axial"] == 2
    size = cells.shape[2]
    at = pl.multiple_of(jnp.where(axial == 0, al - size, 0), 8) if swap else 0
    copies = [
        pltpu.make_async_copy(state.at[:, :, pl.ds(at, size), :], cells, sems.at[0]),
        pltpu.make_async_copy(dt.at[:, pl.ds(at, size), :], dt_cells, sems.at[1]),
        pltpu.make_async_copy(rotor, rotor_v, sems.at[2]),
        pltpu.make_async_copy(blade, blade_s, sems.at[3]),
        pltpu.make_async_copy(harm, harm_s, sems.at[4]),
    ]
    for copy in copies:
        copy.start()
    for copy in copies[2:]:
        copy.wait()
    ncells = cl * dims["n_circ"]
    here = circ * cl + lax.broadcasted_iota(jnp.int32, (1, cl), 1)
    basis = make_basis(harm_s, blade_s, nh, here, ncells)
    rl = rotor_v.shape[1]
    flat = rotor_v[...].reshape(nv * rl, cl)
    part[...] = jnp.zeros_like(part)
    part[:, : nv * rl] = dot(basis, flat, ((1,), (1,))) * (2.0 / ncells)
    for copy in copies[:2]:
        copy.wait()

    def put(side, base):
        for f in range(nv + 1):
            for i in range(W):
                ref = cells.at[f] if f < nv else dt_cells
                rows = ref[:, base + i, :]
                edge[side, f, i, 0:W] = rows[0:W]
                edge[side, f, i, W:] = rows[sl - W :]
                bulk[side, f, i] = rows[W : sl - W]

    if swap:

        @pl.when(axial == 0)
        def _():
            put(0, size - W)

        @pl.when(axial != 0)
        def _():
            put(0, 0)

    else:
        put(0, size - W)
        put(1, 0)


def inter_rows(dims, parts, firsts, donor, weight):
    nv = dims["nv"]
    rl = dims["rl"]
    table = jnp.concatenate([p[:, : nv * rl] for p in parts], axis=1)
    rows = table.shape[1]
    row = lax.broadcasted_iota(jnp.int32, (rows, 128), 0)
    station = row % rl
    for i, first in enumerate(firsts):
        station = station + jnp.where(row // (nv * rl) == i, first, 0)
    mix = jnp.where(station == donor, 1.0 - weight, jnp.where(station == donor + 1, weight, 0.0))
    var = row // rl % nv
    return [dot(table, jnp.where(var == v, mix, 0.0), ((1,), (0,))) for v in range(nv)]


def span_kernel(dims, s_head, s_tail, d_head, d_tail, lo, hi, part, other, before, donor, weight, down, up, inter):
    nv, sl, al, cl, br, nh = (dims[k] for k in ("nv", "sl", "al", "cl", "br", "nh"))
    span = lax.axis_index("span")
    faces = (lo,) if dims["n_axial"] == 2 else (lo, hi)
    rows_of = (nv + 1) * W * (al + W * len(faces))
    for out, s_ref, d_ref, at in ((down, s_head, d_head, 0), (up, s_tail, d_tail, W)):
        for f in range(nv + 1):
            rows = slice(f * W * al, (f + 1) * W * al)
            out[rows, :] = s_ref[f] if f < nv else d_ref[...]
            for side, src in enumerate(faces):
                for i in range(W):
                    to = (nv + 1) * W * al + ((side * (nv + 1) + f) * W + i) * W
                    out[to : to + W, :] = src[f, i, at : at + W, :]

    if not dims["ride"]:
        return
    rl = dims["rl"]
    first = span * 2 * rl
    shares = inter_rows(
        dims, [part[...], other[...], before[...]], [first, first + rl, first - rl], donor[...], weight[...]
    )
    lane = lax.broadcasted_iota(jnp.int32, (2 * nh, 128), 1)
    head = tail = jnp.zeros((2 * nh, 128), jnp.float32)
    for v in range(nv):
        inter[v] = shares[v]
        mine = lane // W == v
        head = jnp.where(mine, pltpu.roll(shares[v], W * v, 1), head)
        tail = jnp.where(mine, pltpu.roll(shares[v], (W * v - (sl - W)) % 128, 1), tail)
    down[rows_of:, :] = head
    up[rows_of:, :] = tail


def lane_ids(rows=8):
    return lax.broadcasted_iota(jnp.int32, (rows, 128), 1)


def gather_strips(dims, load, store, tiles):
    nb, ng, br = dims["nb"], dims["ng"], dims["br"]
    group = lane_ids() // 8
    for g in range(ng):
        for t in tiles:
            acc = jnp.zeros((8, 128), jnp.float32)
            for r in range((nb - 1 - g) // ng + 1):
                part = pltpu.roll(load((ng * r + g) * br + 8 * t), (8 * r + 4) % 128, 1)
                acc = jnp.where(group == r, part, acc)
            store(g * br + 8 * t, acc)


def circ_kernel(
    dims, state, dt, lo_edge, hi_edge, lo, hi, below, above, inter, ext, left, right, share, strips
):
    nv, sl, al, cl, br, nb, ng, nh = (dims[k] for k in ("nv", "sl", "al", "cl", "br", "nb", "ng", "nh"))
    axial = lax.axis_index("axial")
    zero = jnp.zeros((8, cl), jnp.float32)
    for f in range(nv + 1):
        ext[f, 0:8, :] = zero
        ext[f, nb * br - br : nb * br - br + 8, :] = zero
        for s in range(sl):
            rows = slice(s * al, (s + 1) * al)
            at = (s + W) * br + 8
            ext[f, at : at + al, :] = state[f, rows, :] if f < nv else dt[rows, :]

    swap = dims["n_axial"] == 2
    for side, (edge, bulk, valid) in enumerate(
        ((lo_edge, lo, axial > 0), (hi_edge, hi, axial < dims["n_axial"] - 1))
    ):
        base = br if side else W

        def fill(edge, bulk, side, base):
            for f in range(nv + 1):
                for i in range(W):
                    part = (nv + 1) * W * al + (((0 if swap else side) * (nv + 1) + f) * W + i) * W
                    pieces = (
                        (0, W, lambda: below[part : part + W, :]),
                        (W, W, lambda: edge[f, i, 0:W]),
                        (2 * W, sl - 2 * W, lambda: bulk[f, i]),
                        (sl, W, lambda: edge[f, i, W:]),
                        (sl + W, W, lambda: above[part : part + W, :]),
                    )
                    for at, n, read in pieces:
                        val = jnp.zeros((n, cl), jnp.float32) if edge is None else read()
                        ext[f, pl.ds(base + at * br + i, n, stride=br), :] = val

        @pl.when(valid)
        def _(edge=edge, bulk=bulk, side=side, base=base):
            fill(edge, bulk, side, base)

        @pl.when(jnp.logical_not(valid))
        def _(side=side, base=base):
            fill(None, None, side, base)

    for f in range(nv + 1):
        for j in range(W):
            rows = slice((f * W + j) * al, (f * W + j + 1) * al)
            for src, b in ((below, j), (above, sl + W + j)):
                ext[f, b * br + 8 : b * br + 8 + al, :] = src[rows, :]

    def each(f, carry):
        def store(row, val):
            strips[f, row : row + 8, :] = val

        gather_strips(dims, lambda row: ext[f, row : row + 8, :], store, range(br // 8))
        return carry

    lax.fori_loop(0, nv + 1, each, 0)
    half = (nv + 1) // 2
    low = lane_ids(ng * br) % 8 < 4
    for f in range(half):
        one, two = strips[f], strips[f + half]
        rows = slice(f * ng * br, (f + 1) * ng * br)
        right[rows, :] = jnp.where(low, one, pltpu.roll(two, 4, 1))
        left[rows, :] = jnp.where(low, pltpu.roll(one, 124, 1), two)

    if not dims["ride"]:
        return
    wide = sl + 2 * W
    lane = lax.broadcasted_iota(jnp.int32, (2 * nh, 128), 1)
    rows = slice((nv + 1) * W * (al + W * (1 if swap else 2)), None)
    packed = [jnp.zeros((2 * nh, 128), jnp.float32)] * dims["packs"]
    for v in range(nv):
        whole = pltpu.roll(inter[v], W, 1)
        whole = jnp.where(lane < W, pltpu.roll(below[rows, :], (-W * v) % 128, 1), whole)
        whole = jnp.where(lane >= sl + W, pltpu.roll(above[rows, :], sl + W - W * v, 1), whole)
        pack, first = divmod(v, 128 // wide)
        first = first * wide
        packed[pack] = jnp.where(
            (lane >= first) & (lane < first + wide), pltpu.roll(whole, first, 1), packed[pack]
        )
    for i in range(dims["packs"]):
        at = half * ng * br + i * 2 * nh
        left[at : at + 2 * nh, :] = packed[i]
        right[at : at + 2 * nh, :] = packed[i]
        share[i * 2 * nh : (i + 1) * 2 * nh, :] = packed[i]


def ghost_table(dims, table, span):
    nv, sl, nh = (dims[k] for k in ("nv", "sl", "nh"))
    rows, width = table.shape
    donors = pltpu.roll(table[rows - 8 :, :], lax.rem(width - span * sl + W, width), 1)[:, :128]
    lane = lax.broadcasted_iota(jnp.int32, (1, 128), 1)
    where = span * sl - W + lane
    inside = (where >= 0) & (where < sl * dims["n_span"]) & (lane < sl + 2 * W)
    station = lax.broadcasted_iota(jnp.int32, (width, 128), 0)
    donor = (donors[0:1, :] + 0.5).astype(jnp.int32)
    weight = donors[1:2, :]
    mix = jnp.where(station == donor, 1.0 - weight, jnp.where(station == donor + 1, weight, 0.0))
    mix = jnp.where(inside, mix, 0.0)
    inter = dot(table[0 : rows - 8, :], mix, ((1,), (0,)))
    return [inter[v * 2 * nh : (v + 1) * 2 * nh, :] for v in range(nv)]


def step_kernel(
    dims, jac, harm, blade, shares, _, from_left, from_right, new, res, ext, new_v, res_v, q_a, q_b, p_0, p_a, p_b, edge, coef, sem
):
    nv, sl, al, cl, br, nb, ng, nh = (dims[k] for k in ("nv", "sl", "al", "cl", "br", "nb", "ng", "nh"))
    axial = lax.axis_index("axial")
    span = lax.axis_index("span")
    circ = lax.axis_index("circ")
    spare = (W - 1) * al
    parts = 4 if sl % 8 == 0 else 1
    for d in range(3):
        for u in range(nv):
            for v in range(nv):
                value = jac[d, u, v] * 0.5 - (DISSIP if u == v else 0.0)
                coef[(d * nv + u) * nv + v] = jnp.full((8, 128), value, jnp.float32)

    half = (nv + 1) // 2
    low = lane_ids(ng * br) % 8 < 4
    for f in range(half):
        rows = slice(f * ng * br, (f + 1) * ng * br)
        one, two = from_left[rows, :], from_right[rows, :]
        p_0[f, br : (ng + 1) * br, :] = jnp.where(low, one, pltpu.roll(two, 4, 1))
        p_0[f + half, br : (ng + 1) * br, :] = jnp.where(low, pltpu.roll(one, 124, 1), two)

    ncells = cl * dims["n_circ"]
    lane = lax.broadcasted_iota(jnp.int32, (1, 128), 1)
    wide = sl + 2 * W
    if dims["ride"]:
        rows = slice(half * ng * br, None)
        packed = from_left[rows, :] + from_right[rows, :] + shares[0][...] + shares[1][...]
        inter = []
        for v in range(nv):
            pack, first = divmod(v, 128 // wide)
            part = pltpu.roll(packed[pack * 2 * nh : (pack + 1) * 2 * nh, :], (-first * wide) % 128, 1)
            inter.append(jnp.where(lane < wide, part, 0.0))
    else:
        inter = ghost_table(dims, shares, span)
    start = circ * cl
    own = make_basis(harm, blade, nh, start + lax.broadcasted_iota(jnp.int32, (1, cl), 1), ncells)
    pos = lane % 8
    halo_cells = lax.rem(start + jnp.where(pos < 4, pos - 4, pos + cl - 4) + ncells, ncells)
    halo = make_basis(harm, blade, nh, halo_cells, ncells)
    s_id = lax.broadcasted_iota(jnp.int32, (128, 128), 0)
    r_id = lax.broadcasted_iota(jnp.int32, (128, 128), 1) // 8

    @pl.when(axial == 0)
    def _():
        for v in range(nv):
            part = inter[v]
            ghost = dot(part, own, ((0,), (0,)))
            ext[v, pl.ds(7, sl + 2 * W, stride=br), :] = ghost[: sl + 2 * W, :]
            ghost = dot(part, halo, ((0,), (0,)))
            for g in range(ng):
                picked = jnp.where(s_id == ng * r_id + g, ghost, 0.0)
                at = (g + 1) * br + 7
                p_0[v, at : at + 1, :] = jnp.sum(picked, axis=0, keepdims=True)

    lanes = lane_ids()
    first_lane, last_lane = lanes == 0, lanes == 127
    pos3, pos4 = lanes % 8 == 3, lanes % 8 == 4
    last = (ng + 1) * br

    def apply(cells):
        for c in cells:
            c["diff"] = [
                [plus - minus for plus, minus in zip(c[d + "+"], c[d + "-"])] for d in ("axial", "span", "theta")
            ]
            c["rest"] = [
                (2.0 * DISSIP) * (3.0 * q - (x + y + z))
                for q, x, y, z in zip(c["q"], c["axial-"], c["span-"], c["theta-"])
            ]
        out = [[] for _ in cells]
        for u in range(nv):
            acc = [c["rest"][u] for c in cells]
            for d in range(3):
                for v in range(nv):
                    k = coef[(d * nv + u) * nv + v]
                    for i, c in enumerate(cells):
                        acc[i] = acc[i] + k * c["diff"][d][v]
            for i in range(len(cells)):
                out[i].append(acc[i])
        return out

    def gather(view, at):
        def load(off):
            return [view[v, at + off : at + off + 8, :] for v in range(nv)]

        return {"q": load(0), "axial-": load(-1), "axial+": load(1), "span-": load(-br), "span+": load(br)}

    def turn(cell, beyond, at_plus, at_minus):
        cell["theta+"] = [
            pltpu.roll(jnp.where(at_plus, z, q), 127, 1) for z, q in zip(beyond, cell["q"])
        ]
        cell["theta-"] = [pltpu.roll(jnp.where(at_minus, z, q), 1, 1) for z, q in zip(beyond, cell["q"])]

    writes = [pltpu.make_async_copy(res_v.at[:, pl.ds(spare, sl * al), :], res, sem.at[0])]

    def stage(number, src, p_src, dst, p_dst):
        width = W - 1 - number
        factor = SEGMENT_COEF[number]
        final = number == len(SEGMENT_COEF) - 1
        for v in range(nv):
            p_src[v, 0:br, :] = pltpu.roll(p_src[v, last - br : last, :], 8, 1)
            p_src[v, last : last + br, :] = pltpu.roll(p_src[v, br : 2 * br, :], 120, 1)

        def blocks(b, count, tiles):
            around = pl.multiple_of((b - 1) * br, 8)
            rows = (count + 1) * br + (8 if tiles == [0] else br)
            view = src.at[:, pl.ds(around, rows), :]
            for t in tiles:
                cells = []
                for i in range(count):
                    r = (b + i) // ng
                    g = b + i - r * ng
                    p_row = pl.multiple_of((g + 1) * br, 8) + 8 * t
                    cell = gather(view, (i + 1) * br + 8 * t)
                    beyond = [pltpu.roll(p_src[v, pl.ds(p_row, 8), :], 124 - 8 * r, 1) for v in range(nv)]
                    turn(cell, beyond, first_lane, last_lane)
                    cells.append(cell)
                for i, result in enumerate(apply(cells)):
                    row = pl.multiple_of((b + i) * br, 8) + 8 * t
                    step = factor * ext[nv, pl.ds(row, 8), :]
                    out = pl.multiple_of((b + i - W) * al, 8) + 8 * (t - 1)
                    for u in range(nv):
                        value = ext[u, pl.ds(row, 8), :] - step * result[u]
                        if final:
                            new_v[u, pl.ds(out, 8), :] = value
                        else:
                            dst[u, pl.ds(row, 8), :] = value
                            if t > 0 and number == 0:
                                res_v[u, pl.ds(out + spare, 8), :] = result[u]

        def run(first, count, tiles):
            def loop(j, carry):
                blocks(first + 2 * j, 2, tiles)
                return carry

            lax.fori_loop(0, count // 2, loop, 0)
            if count % 2:
                blocks(first + count - 1, 1, tiles)

        if final:
            tiles = list(range(1, br // 8))
            for i in range(parts):
                run(W + i * (sl // parts), sl // parts, tiles)
                rows = pl.ds(i * (sl // parts) * al, sl // parts * al)
                copy = pltpu.make_async_copy(new_v.at[:, rows, :], new.at[:, rows, :], sem.at[i + 1])
                copy.start()
                writes.append(copy)
        else:
            run(W - width, sl + 2 * width, list(range(br // 8)))
            blocks(sl + W + width, 1, [0])
        if number == 0:
            writes[0].start()
        if final:
            return

        def edges(v, carry):
            def store(row, val):
                edge[v, row : row + 8, :] = val

            gather_strips(dims, lambda row: src[v, row : row + 8, :], store, range(br // 8))
            return carry

        lax.fori_loop(0, nv, edges, 0)

        def strip(g, carry):
            base = pl.multiple_of((g + 1) * br, 8)
            around = pl.multiple_of(g * br, 8)
            view = p_src.at[:, pl.ds(around, 3 * br), :]

            for t in range(br // 8):
                cell = gather(view, br + 8 * t)
                turn(cell, [edge[v, pl.ds(around + 8 * t, 8), :] for v in range(nv)], pos4, pos3)
                (result,) = apply([cell])
                step = factor * p_0[nv, pl.ds(base + 8 * t, 8), :]
                for u in range(nv):
                    p_dst[u, pl.ds(base + 8 * t, 8), :] = p_0[u, pl.ds(base + 8 * t, 8), :] - step * result[u]
            return carry

        lax.fori_loop(0, ng, strip, 0)

    stage(0, ext, p_0, q_a, p_a)
    stage(1, q_a, p_a, q_b, p_b)
    stage(2, q_b, p_b, q_a, p_a)
    stage(3, q_a, p_a, None, None)
    for copy in writes:
        copy.wait()


def shift_pairs(count, step, closed):
    return [(i, (i + step) % count) for i in range(count) if closed or 0 <= i + step < count]


def coef_table(part, donor_index, donor_weight, rl, nv, sizes):
    n_circ, n_span, n_axial = sizes
    modes, sl = part.shape[0], donor_index.shape[0]
    width = -(-max(rl * n_span * n_axial, sl * n_span) // 128) * 128
    circ, span, axial = (lax.axis_index(a) for a in AXES)
    rows = part[:, : nv * rl].reshape(modes, nv, rl).transpose(1, 0, 2).reshape(nv * modes, rl)
    table = jnp.zeros((nv * modes + 8, width), jnp.float32)
    table = lax.dynamic_update_slice(table, rows, (0, (span * n_axial + axial) * rl))
    donors = jnp.stack([donor_index.astype(jnp.float32), donor_weight])
    donors = jnp.where((circ == 0) & (axial == 0), donors, 0.0)
    table = lax.dynamic_update_slice(table, donors, (nv * modes, span * sl))
    return lax.psum(table, AXES)


def local(rotor_outlet, blade_count, harmonic_list, donor_index, donor_weight, state, time_step, flux_jacobian):
    f32 = jnp.float32
    n_circ, n_span, n_axial = (lax.axis_size(a) for a in AXES)
    nv, sl, al, cl = state.shape
    br = al + 2 * W
    nb = sl + 2 * W + 1
    ng = -(-nb // 16)
    nh = harmonic_list.shape[0]
    dims = dict(
        nv=nv, sl=sl, al=al, cl=cl, br=br, nb=nb, ng=ng, nh=nh, n_circ=n_circ, n_span=n_span, n_axial=n_axial
    )
    rl = rotor_outlet.shape[1]
    packs = -(-nv // (128 // (sl + 2 * W)))
    ride = n_axial == 2 and n_circ == 4 and nv * rl <= 128
    dims.update(rl=rl, packs=packs, ride=ride)
    params = pltpu.CompilerParams(vmem_limit_bytes=48 * 2**20)
    sides = 1 if n_axial == 2 else 2
    deep = 8 if n_axial == 2 else al

    edge, bulk, part = pl.pallas_call(
        functools.partial(axial_kernel, dims),
        out_shape=[
            jax.ShapeDtypeStruct((sides, nv + 1, W, 2 * W, cl), f32),
            jax.ShapeDtypeStruct((sides, nv + 1, W, sl - 2 * W, cl), f32),
            jax.ShapeDtypeStruct((2 * nh, -(-nv * rl // 128) * 128), f32),
        ],
        in_specs=[HBM] * 5,
        out_specs=[VMEM] * 3,
        scratch_shapes=[
            pltpu.VMEM((nv, sl, deep, cl), f32),
            pltpu.VMEM((sl, deep, cl), f32),
            pltpu.VMEM(rotor_outlet.shape, f32),
            pltpu.SMEM(blade_count.shape, jnp.int32),
            pltpu.SMEM(harmonic_list.shape, jnp.int32),
            pltpu.SemaphoreType.DMA((5,)),
        ],
        compiler_params=pltpu.CompilerParams(vmem_limit_bytes=63 * 2**20),
        name="axial_faces",
    )(state, time_step, rotor_outlet, blade_count, harmonic_list)
    state = state.reshape(nv, sl * al, cl)
    time_step = time_step.reshape(sl * al, cl)

    def axial_move(faces):
        if n_axial == 2:
            moved = lax.ppermute(faces[0], "axial", [(0, 1), (1, 0)])
            return moved, moved
        lo = lax.ppermute(faces[0], "axial", shift_pairs(n_axial, 1, False))
        hi = lax.ppermute(faces[1], "axial", shift_pairs(n_axial, -1, False))
        return lo, hi

    lo_edge, hi_edge = axial_move(edge)
    if ride:
        other = lax.ppermute(part, "axial", [(0, 1), (1, 0)])
        before = lax.ppermute(part, ("span", "axial"), shift_pairs(n_span * n_axial, 1, False))
        shares = None
    else:
        other = before = part
        shares = coef_table(part, donor_index, donor_weight, rl, nv, (n_circ, n_span, n_axial))
    lo, hi = axial_move(bulk)

    def spec(shape, *index):
        index = index or (0,) * len(shape)
        return pl.BlockSpec(shape, lambda i: index)

    faces = (nv + 1, W, 2 * W, cl)
    message = ((nv + 1) * W * (al + W * sides) + (2 * nh if ride else 0), cl)
    end = sl // W - 1
    pad = lambda x: jnp.pad(x, (0, 128 - sl))[None]
    down, up, inter = pl.pallas_call(
        functools.partial(span_kernel, dims),
        grid=(1,),
        out_shape=[jax.ShapeDtypeStruct(message, f32)] * 2 + [jax.ShapeDtypeStruct((nv, 2 * nh, 128), f32)],
        in_specs=[
            spec((nv, W * al, cl)),
            spec((nv, W * al, cl), 0, end, 0),
            spec((W * al, cl)),
            spec((W * al, cl), end, 0),
            spec(faces),
            spec(faces),
            spec(part.shape),
            spec(part.shape),
            spec(part.shape),
            spec((1, 128)),
            spec((1, 128)),
        ],
        out_specs=[spec(message), spec(message), spec((nv, 2 * nh, 128))],
        compiler_params=params,
        name="span_faces",
    )(
        state, state, time_step, time_step, lo_edge, hi_edge, part, other, before, pad(donor_index), pad(donor_weight)
    )
    below = lax.ppermute(up, "span", shift_pairs(n_span, 1, False))
    above = lax.ppermute(down, "span", shift_pairs(n_span, -1, False))

    strip = jax.ShapeDtypeStruct(((nv + 1) // 2 * ng * br + (packs * 2 * nh if ride else 0), 128), f32)
    ext, left, right, share = pl.pallas_call(
        functools.partial(circ_kernel, dims),
        out_shape=[
            jax.ShapeDtypeStruct((nv + 1, nb * br, cl), f32),
            strip,
            strip,
            jax.ShapeDtypeStruct((packs * 2 * nh, 128), f32),
        ],
        in_specs=[VMEM] * 9,
        out_specs=[VMEM] * 4,
        scratch_shapes=[pltpu.VMEM((nv + 1, ng * br, 128), f32)],
        compiler_params=params,
        name="circ_faces",
    )(state, time_step, lo_edge, hi_edge, lo, hi, below, above, inter)
    from_left = lax.ppermute(right, "circ", shift_pairs(n_circ, 1, True))
    from_right = lax.ppermute(left, "circ", shift_pairs(n_circ, -1, True))
    if ride:
        shares = [share, lax.ppermute(share, "circ", shift_pairs(n_circ, 2, True))]

    block = jax.ShapeDtypeStruct((nv, sl * al, cl), f32)
    field = pltpu.VMEM((nv, nb * br, cl), f32)
    strips = pltpu.VMEM((nv, (ng + 2) * br, 128), f32)
    new, res, _ = pl.pallas_call(
        functools.partial(step_kernel, dims),
        out_shape=[block, block, jax.ShapeDtypeStruct(ext.shape, f32)],
        in_specs=[SMEM, SMEM, SMEM, [VMEM, VMEM] if ride else VMEM, VMEM, VMEM, VMEM],
        out_specs=[HBM, HBM, VMEM],
        input_output_aliases={(5 if ride else 4): 2},
        scratch_shapes=[
            pltpu.VMEM((nv, sl * al, cl), f32),
            pltpu.VMEM((nv, (sl + 2 * W - 2) * al, cl), f32),
            field,
            field,
            pltpu.VMEM((nv + 1, (ng + 2) * br, 128), f32),
            strips,
            strips,
            pltpu.VMEM((nv, ng * br, 128), f32),
            pltpu.VMEM((3 * nv * nv, 8, 128), f32),
            pltpu.SemaphoreType.DMA((5,)),
        ],
        compiler_params=params,
        name="segments",
    )(flux_jacobian, harmonic_list, blade_count, shares, ext, from_left, from_right)
    return new.reshape(nv, sl, al, cl), res.reshape(nv, sl, al, cl)


def solution(mesh):
    return jax.shard_map(
        local,
        mesh=mesh,
        in_specs=(
            P(None, ("span", "axial"), "circ"),
            P(),
            P(),
            P("span"),
            P("span"),
            P(None, "span", "axial", "circ"),
            P("span", "axial", "circ"),
            P(),
        ),
        out_specs=(P(None, "span", "axial", "circ"), P(None, "span", "axial", "circ")),
        check_vma=False,
    )
```

time: 288 us -> 65.6 us (0.23); the launches traced: 283 us -> 65.3 us
  blocking collectives: 63.2 us -> 0 us
  local copies, waits for them, and re-layouts: 65.1 us -> 2.04 us
  other arithmetic: 42 us -> 0 us
  starting transfers between devices: 53.1 us -> 16.4 us
  matrix products: 35.1 us -> 0 us
  Pallas kernels: 0 us -> 33.1 us
  waiting for transfers between devices: 21.5 us -> 12.5 us
    all_gather x1 -> x0, blocking collectives: 63.2 us -> none  [local(): lax.all_gather(coef, ('circ', 'span', 'axial'), axis=1, tiled=True)]
    dot_general x14 -> x0, matrix products: 35.1 us -> none  [the longest x12 33.7 us: apply_jac(): jnp.einsum('uv,vsat->usat', matrix, field, precision=lax.Precision.HIGHEST)]
    pallas_call x0 -> x4, Pallas kernels: none -> 33.1 us  [the longest x1 28.6 us: local(): pl.pallas_call(functools.partial(step_kernel, dims), out_shape=[block, bl...]
    ppermute x24 -> x9, starting transfers between devices: 48.5 us -> 16.4 us  [the longest x1 3.98 us: local(): lax.ppermute(part, ('span', 'axial'), shift_pairs(n_span * n_axial, 1, Fa...]
    slice x21 -> x0, local copies, waits for them, and re-layouts: 30 us -> none  [the longest x10 14.1 us: padded_2(): lax.slice_in_dim(cells, cells.shape[dim] - width, cells.shape[dim], axis=...]
    sub x5 -> x0, other arithmetic: 20.4 us -> none  [the longest x3 13.9 us: local(): state - SEGMENT_COEF[segment] * time_step[None] * operate(field, ghost, i...]
    ppermute x8 -> x0, local copies, waits for them, and re-layouts: 19.2 us -> none  [the longest x4 9.64 us: padded_2(): lax.ppermute(head, axis, [((i + 1) % count, i) for i in range(ends)])]
    mul x6 -> x0, other arithmetic: 15.3 us -> none  [the longest x4 14.5 us: combine_terms(): total = apply_jac(flux_jacobian[0], (axial_plus - axial_minus) * 0.5)]
  transfers between devices with their start and end apart: 25 -> 9, of which waited for: 8 -> 4; matrix products, arithmetic and copies ran while one was open for 24% -> 0% of each run, Pallas kernels for 0% -> 1%
where the time goes in v1:
time: 65.6 us; the launch traced here: 65.3 us
  Pallas kernels  33.1 us (50%)
  starting transfers between devices  16.4 us (25%)
  waiting for transfers between devices  12.5 us (19%)
  local copies, waits for them, and re-layouts  2.04 us (3%)
  between operations  1.43 us (2%)
    pallas_call x1, Pallas kernels, local(): pl.pallas_call(functools.partial(step_kernel, dims), out_shape=[block, bl...  28.6 us
    ppermute x1, waiting for transfers between devices, local(): above = lax.ppermute(down, 'span', shift_pairs(n_span, -1, False))  4.4 us
    ppermute x1, starting transfers between devices, local(): lax.ppermute(part, ('span', 'axial'), shift_pairs(n_span * n_axial, 1, Fa...  3.98 us
    ppermute x1, waiting for transfers between devices, local(): shares = [share, lax.ppermute(share, 'circ', shift_pairs(n_circ, 2, True))]  3.4 us
    ppermute x2, waiting for transfers between devices, axial_move(): moved = lax.ppermute(faces[0], 'axial', [(0, 1), (1, 0)])  3.38 us
    ppermute x1, starting transfers between devices, local(): below = lax.ppermute(up, 'span', shift_pairs(n_span, 1, False))  3.37 us
    pallas_call x1, Pallas kernels, local(): pl.pallas_call(functools.partial(axial_kernel, dims), out_shape=[jax.Shap...  2.21 us
    ppermute x1, starting transfers between devices, local(): from_right = lax.ppermute(left, 'circ', shift_pairs(n_circ, -1, True))  2.09 us
  transfers between devices with their start and end apart: 9, of which 4 were waited for; matrix products, arithmetic and copies ran while one was open for 0% of the time, Pallas kernels for 1%

profile of v1, /device:TPU:1, one launch (start us, length us, event | category | flops | bytes accessed | tf_op | source)
XLA Modules:
  0.0 65.3 jit_solution(9436356469013952710)
XLA Ops:
  0.6 0.0 copy-start.1
  0.6 0.0 copy-start.5
  0.7 0.0 copy-start.6
  1.3 2.2 %axial_faces.1 = (f32[1,6,4,8,128]{4,3,2,1,0:T(8,128)}, f32[1,6,4,24,128]{4,3,2,1,0:T(8,128)}, f32[16,128]{1,0:T(8,128)}) custom-call(f32[5,32,16,128]{3,2,1,0:T(8,128)} %state.1, f32[32,16,128]{2,1,0:T(8,128)} %dt.1, f32[5,8,128]{2,1,0:T(8,128)} %rotor.1, s32[1]{0:T(128)S(6)} %copy.13.blade, s32[8]{0:T(128)} %harm.3), custom_call_target="tpu_custom_call" | custom-call | tf_op jit(solution)/shard_map/axial_faces/pallas_call | solution.py:482
  3.6 4.0 %collective-permute-start.3 = (f32[16,128]{1,0:T(8,128)}, f32[16,128]{1,0:T(8,128)S(1)}, u32[]{:S(2)}, u32[]{:S(2)}) collective-permute-start(f32[16,128]{1,0:T(8,128)} %get-tuple-element.16.part), channel_id=1, source_target_pairs={{0,1},{1,2},{2,3},{3,4},{4,5},{5,6},{6,7},{8,9},{9,10},{10,11},{11... | collective-permute-start | bytes 24584 | tf_op jit(solution)/shard_map/ppermute | solution.py:516
  7.6 1.8 %collective-permute-start.2 = (f32[16,128]{1,0:T(8,128)}, f32[16,128]{1,0:T(8,128)S(1)}, u32[]{:S(2)}, u32[]{:S(2)}) collective-permute-start(f32[16,128]{1,0:T(8,128)} %get-tuple-element.16.part), channel_id=1, source_target_pairs={{0,1},{1,0},{2,3},{3,2},{4,5},{5,4},{6,7},{7,6},{8,9},{9,8},{10,11... | collective-permute-start | bytes 24584 | tf_op jit(solution)/shard_map/ppermute | solution.py:515
  9.4 0.1 collective-permute-start
  9.4 1.4 %collective-permute-start.1 = (f32[6,4,24,128]{3,2,1,0:T(8,128)}, f32[6,4,24,128]{3,2,1,0:T(8,128)S(1)}, u32[]{:S(2)}, u32[]{:S(2)}) collective-permute-start(f32[6,4,24,128]{3,2,1,0:T(8,128)} %bitcast.18), channel_id=1, source_target_pairs={{0,1},{1,0},{2,3},{3,2},{4,5},{5,4},{6,7},{7,6},{8,9},{9,8},{10,11... | collective-permute-start | bytes 884744 | tf_op jit(solution)/shard_map/ppermute | solution.py:507
  10.8 0.0 copy-done.5
  10.8 0.0 copy-done.6
  10.8 0.0 collective-permute-done.3.before
  10.9 0.0 collective-permute-done.2.other
  10.9 3.4 %collective-permute-done.lo.hi.lo_edge.hi_edge = f32[6,4,8,128]{3,2,1,0:T(8,128)S(1)} collective-permute-done((f32[6,4,8,128]{3,2,1,0:T(8,128)}, f32[6,4,8,128]{3,2,1,0:T(8,128)S(1)}, u32[]{:S(2)}, u32[]{:S(2)}) %collective-permute-start) | collective-permute-done | bytes 98336 | tf_op jit(solution)/shard_map/ppermute | solution.py:507
  14.2 0.0 copy-done.1
  14.2 0.0 copy-start
  14.2 1.3 %copy-done = f32[5,32,16,128]{3,2,1,0:T(8,128)S(1)} copy-done((f32[5,32,16,128]{3,2,1,0:T(8,128)S(1)}, f32[5,32,16,128]{3,2,1,0:T(8,128)}, u32[]{:S(2)}) %copy-start) | copy-done | bytes 1310744
  15.6 0.0 copy-start.2
  15.6 0.7 %copy-done.2 = f32[16,128]{1,0:T(8,128)S(1)} copy-done((f32[16,128]{1,0:T(8,128)S(1)}, f32[16,128]{1,0:T(8,128)}, u32[]{:S(2)}) %copy-start.2) | copy-done | bytes 8216
  16.3 0.5 span_faces.1
  16.8 3.4 %collective-permute-start.4 = (f32[496,128]{1,0:T(8,128)S(1)}, f32[496,128]{1,0:T(8,128)S(1)}, u32[]{:S(2)}, u32[]{:S(2)}) collective-permute-start(f32[496,128]{1,0:T(8,128)S(1)} %get-tuple-element.17), channel_id=1, source_target_pairs={{0,2},{2,4},{4,6},{1,3},{3,5},{5,7},{8,10},{10,12},{12,14},{9,11},... | collective-permute-start | bytes 761864 | tf_op jit(solution)/shard_map/ppermute | solution.py:554
  20.1 1.9 %collective-permute-start.5 = (f32[496,128]{1,0:T(8,128)S(1)}, f32[496,128]{1,0:T(8,128)S(1)}, u32[]{:S(2)}, u32[]{:S(2)}) collective-permute-start(f32[496,128]{1,0:T(8,128)S(1)} %get-tuple-element.18), channel_id=1, source_target_pairs={{2,0},{4,2},{6,4},{3,1},{5,3},{7,5},{10,8},{12,10},{14,12},{11,9},... | collective-permute-start | bytes 761864 | tf_op jit(solution)/shard_map/ppermute | solution.py:555
  22.1 0.0 collective-permute-done.1.lo.hi
  22.1 1.3 %collective-permute-done.4.below = f32[496,128]{1,0:T(8,128)S(1)} collective-permute-done((f32[496,128]{1,0:T(8,128)S(1)}, f32[496,128]{1,0:T(8,128)S(1)}, u32[]{:S(2)}, u32[]{:S(2)}) %collective-permute-start.4) | collective-permute-done | bytes 253984 | tf_op jit(solution)/shard_map/ppermute | solution.py:554
  23.3 4.4 %collective-permute-done.5.above = f32[496,128]{1,0:T(8,128)S(1)} collective-permute-done((f32[496,128]{1,0:T(8,128)S(1)}, f32[496,128]{1,0:T(8,128)S(1)}, u32[]{:S(2)}, u32[]{:S(2)}) %collective-permute-start.5) | collective-permute-done | bytes 253984 | tf_op jit(solution)/shard_map/ppermute | solution.py:555
  27.7 0.0 copy-start.4
  27.7 0.0 copy-start.3
  27.7 1.7 %circ_faces.1 = (f32[6,984,128]{2,1,0:T(8,128)S(1)}, f32[248,128]{1,0:T(8,128)S(1)}, f32[248,128]{1,0:T(8,128)S(1)}, f32[32,128]{1,0:T(8,128)S(1)}) custom-call(f32[5,512,128]{2,1,0:T(8,128)S(1)} %bitcast.12, f32[512,128]{1,0:T(8,128)S(1)} %bitcast.15, f32[6,4,8,128]{3,2,1,0:T(8,128)S(1)} %collective-permute-done.lo.hi.lo_edge.hi_edge, ...), custom_call_target="tpu_custom_call" | custom-call | tf_op jit(solution)/shard_map/circ_faces/pallas_call | solution.py:558
  29.5 1.3 %collective-permute-start.7 = (f32[248,128]{1,0:T(8,128)S(1)}, f32[248,128]{1,0:T(8,128)S(1)}, u32[]{:S(2)}, u32[]{:S(2)}) collective-permute-start(f32[248,128]{1,0:T(8,128)S(1)} %get-tuple-element.22), channel_id=1, source_target_pairs={{0,8},{8,16},{16,24},{24,0},{1,9},{9,17},{17,25},{25,1},{2,10},{10... | collective-permute-start | bytes 380936 | tf_op jit(solution)/shard_map/ppermute | solution.py:572
  30.8 2.1 %collective-permute-start.8 = (f32[248,128]{1,0:T(8,128)S(1)}, f32[248,128]{1,0:T(8,128)S(1)}, u32[]{:S(2)}, u32[]{:S(2)}) collective-permute-start(f32[248,128]{1,0:T(8,128)S(1)} %get-tuple-element.23), channel_id=1, source_target_pairs={{0,24},{8,0},{16,8},{24,16},{1,25},{9,1},{17,9},{25,17},{2,26},{10... | collective-permute-start | bytes 380936 | tf_op jit(solution)/shard_map/ppermute | solution.py:573
  32.9 0.4 collective-permute-start.6
  33.3 0.0 copy-done.4
  33.3 3.4 %collective-permute-done.6.shares_1_ = f32[32,128]{1,0:T(8,128)S(1)} collective-permute-done((f32[32,128]{1,0:T(8,128)S(1)}, f32[32,128]{1,0:T(8,128)S(1)}, u32[]{:S(2)}, u32[]{:S(2)}) %collective-permute-start.6) | collective-permute-done | bytes 16416 | tf_op jit(solution)/shard_map/ppermute | solution.py:575
  36.7 0.0 collective-permute-done.7.from_left
  36.7 0.0 collective-permute-done.8.from_right
  36.7 0.0 copy-done.3
  36.7 28.6 %segments.1 = (f32[5,512,128]{2,1,0:T(8,128)}, f32[5,512,128]{2,1,0:T(8,128)}, f32[6,984,128]{2,1,0:T(8,128)S(1)}) custom-call(f32[3,5,5]{2,1,0:T(8,128)S(1)} %copy.11.jac, s32[8]{0:T(128)S(1)} %copy-done.3, s32[1]{0:T(128)S(6)} %copy.13.blade, f32[32,128]{1,0:T(8,128)S(1)} %get-tuple-element.20.shares_0_, ...), custom_call_target="tpu_custom_call", output_to_operand_aliasing={{2}: (5, {})} | custom-call | tf_op jit(solution)/shard_map/segments/pallas_call | solution.py:580
  (3 shorter events, 0.0 us)
Async XLA Ops:
  0.6 13.6 %copy-start.1 = (f32[32,16,128]{2,1,0:T(8,128)S(1)}, f32[32,16,128]{2,1,0:T(8,128)}, u32[]{:S(2)}) copy-start(f32[32,16,128]{2,1,0:T(8,128)} %dt.1) | copy-start | bytes 786436
  0.6 10.2 %copy-start.5 = (s32[32]{0:T(128)S(1)}, s32[32]{0:T(128)}, u32[]{:S(2)}) copy-start(s32[32]{0:T(128)} %param.11) | copy-start | bytes 388
  0.7 10.2 %copy-start.6 = (f32[32]{0:T(128)S(1)}, f32[32]{0:T(128)}, u32[]{:S(2)}) copy-start(f32[32]{0:T(128)} %param.12) | copy-start | bytes 388
  3.6 7.3 %collective-permute-start.3 = (f32[16,128]{1,0:T(8,128)}, f32[16,128]{1,0:T(8,128)S(1)}, u32[]{:S(2)}, u32[]{:S(2)}) collective-permute-start(f32[16,128]{1,0:T(8,128)} %get-tuple-element.16.part), channel_id=1, source_target_pairs={{0,1},{1,2},{2,3},{3,4},{4,5},{5,6},{6,7},{8,9},{9,10},{10,11},{11... | collective-permute-start | bytes 24584 | tf_op jit(solution)/shard_map/ppermute | solution.py:516
  7.6 3.3 %collective-permute-start.2 = (f32[16,128]{1,0:T(8,128)}, f32[16,128]{1,0:T(8,128)S(1)}, u32[]{:S(2)}, u32[]{:S(2)}) collective-permute-start(f32[16,128]{1,0:T(8,128)} %get-tuple-element.16.part), channel_id=1, source_target_pairs={{0,1},{1,0},{2,3},{3,2},{4,5},{5,4},{6,7},{7,6},{8,9},{9,8},{10,11... | collective-permute-start | bytes 24584 | tf_op jit(solution)/shard_map/ppermute | solution.py:515
  9.4 4.9 %collective-permute-start = (f32[6,4,8,128]{3,2,1,0:T(8,128)}, f32[6,4,8,128]{3,2,1,0:T(8,128)S(1)}, u32[]{:S(2)}, u32[]{:S(2)}) collective-permute-start(f32[6,4,8,128]{3,2,1,0:T(8,128)} %bitcast.19), channel_id=1, source_target_pairs={{0,1},{1,0},{2,3},{3,2},{4,5},{5,4},{6,7},{7,6},{8,9},{9,8},{10,11... | collective-permute-start | bytes 294920 | tf_op jit(solution)/shard_map/ppermute | solution.py:507
  9.4 12.6 %collective-permute-start.1 = (f32[6,4,24,128]{3,2,1,0:T(8,128)}, f32[6,4,24,128]{3,2,1,0:T(8,128)S(1)}, u32[]{:S(2)}, u32[]{:S(2)}) collective-permute-start(f32[6,4,24,128]{3,2,1,0:T(8,128)} %bitcast.18), channel_id=1, source_target_pairs={{0,1},{1,0},{2,3},{3,2},{4,5},{5,4},{6,7},{7,6},{8,9},{9,8},{10,11... | collective-permute-start | bytes 884744 | tf_op jit(solution)/shard_map/ppermute | solution.py:507
  14.2 1.3 %copy-start = (f32[5,32,16,128]{3,2,1,0:T(8,128)S(1)}, f32[5,32,16,128]{3,2,1,0:T(8,128)}, u32[]{:S(2)}) copy-start(f32[5,32,16,128]{3,2,1,0:T(8,128)} %state.1) | copy-start | bytes 3932164
  15.6 0.7 %copy-start.2 = (f32[16,128]{1,0:T(8,128)S(1)}, f32[16,128]{1,0:T(8,128)}, u32[]{:S(2)}) copy-start(f32[16,128]{1,0:T(8,128)} %get-tuple-element.16.part) | copy-start | bytes 24580
  16.8 6.6 %collective-permute-start.4 = (f32[496,128]{1,0:T(8,128)S(1)}, f32[496,128]{1,0:T(8,128)S(1)}, u32[]{:S(2)}, u32[]{:S(2)}) collective-permute-start(f32[496,128]{1,0:T(8,128)S(1)} %get-tuple-element.17), channel_id=1, source_target_pairs={{0,2},{2,4},{4,6},{1,3},{3,5},{5,7},{8,10},{10,12},{12,14},{9,11},... | collective-permute-start | bytes 761864 | tf_op jit(solution)/shard_map/ppermute | solution.py:554
  20.1 7.6 %collective-permute-start.5 = (f32[496,128]{1,0:T(8,128)S(1)}, f32[496,128]{1,0:T(8,128)S(1)}, u32[]{:S(2)}, u32[]{:S(2)}) collective-permute-start(f32[496,128]{1,0:T(8,128)S(1)} %get-tuple-element.18), channel_id=1, source_target_pairs={{2,0},{4,2},{6,4},{3,1},{5,3},{7,5},{10,8},{12,10},{14,12},{11,9},... | collective-permute-start | bytes 761864 | tf_op jit(solution)/shard_map/ppermute | solution.py:555
  27.7 5.6 %copy-start.4 = (f32[3,5,5]{2,0,1:T(4,128)S(1)}, f32[3,5,5]{2,0,1:T(4,128)}, u32[]{:S(2)}) copy-start(f32[3,5,5]{2,0,1:T(4,128)} %param.15) | copy-start | bytes 904
  27.7 9.0 %copy-start.3 = (s32[8]{0:T(128)S(1)}, s32[8]{0:T(128)}, u32[]{:S(2)}) copy-start(s32[8]{0:T(128)} %harm.3) | copy-start | bytes 100
  29.5 7.2 %collective-permute-start.7 = (f32[248,128]{1,0:T(8,128)S(1)}, f32[248,128]{1,0:T(8,128)S(1)}, u32[]{:S(2)}, u32[]{:S(2)}) collective-permute-start(f32[248,128]{1,0:T(8,128)S(1)} %get-tuple-element.22), channel_id=1, source_target_pairs={{0,8},{8,16},{16,24},{24,0},{1,9},{9,17},{17,25},{25,1},{2,10},{10... | collective-permute-start | bytes 380936 | tf_op jit(solution)/shard_map/ppermute | solution.py:572
  30.8 5.9 %collective-permute-start.8 = (f32[248,128]{1,0:T(8,128)S(1)}, f32[248,128]{1,0:T(8,128)S(1)}, u32[]{:S(2)}, u32[]{:S(2)}) collective-permute-start(f32[248,128]{1,0:T(8,128)S(1)} %get-tuple-element.23), channel_id=1, source_target_pairs={{0,24},{8,0},{16,8},{24,16},{1,25},{9,1},{17,9},{25,17},{2,26},{10... | collective-permute-start | bytes 380936 | tf_op jit(solution)/shard_map/ppermute | solution.py:573
  32.9 3.8 %collective-permute-start.6 = (f32[32,128]{1,0:T(8,128)S(1)}, f32[32,128]{1,0:T(8,128)S(1)}, u32[]{:S(2)}, u32[]{:S(2)}) collective-permute-start(f32[32,128]{1,0:T(8,128)S(1)} %get-tuple-element.20.shares_0_), channel_id=1, source_target_pairs={{0,16},{8,24},{16,0},{24,8},{1,17},{9,25},{17,1},{25,9},{2,18},{10... | collective-permute-start | bytes 49160 | tf_op jit(solution)/shard_map/ppermute | solution.py:575

commit v2 on v1

--- a/solution.py
+++ b/solution.py
@@ -155,20 +155,19 @@
 ):
     nv, sl, al, cl, br, nb, ng, nh = (dims[k] for k in ("nv", "sl", "al", "cl", "br", "nb", "ng", "nh"))
     axial = lax.axis_index("axial")
-    zero = jnp.zeros((8, cl), jnp.float32)
+    turns = al // 8
     for f in range(nv + 1):
-        ext[f, 0:8, :] = zero
-        ext[f, nb * br - br : nb * br - br + 8, :] = zero
         for s in range(sl):
-            rows = slice(s * al, (s + 1) * al)
-            at = (s + W) * br + 8
-            ext[f, at : at + al, :] = state[f, rows, :] if f < nv else dt[rows, :]
+            for t in range(turns):
+                rows = pl.ds(s * al + t, 8, stride=turns)
+                at = (s + W) * br + 8 * (t + 1)
+                ext[f, at : at + 8, :] = state[f, rows, :] if f < nv else dt[rows, :]
 
     swap = dims["n_axial"] == 2
     for side, (edge, bulk, valid) in enumerate(
         ((lo_edge, lo, axial > 0), (hi_edge, hi, axial < dims["n_axial"] - 1))
     ):
-        base = br if side else W
+        base = 0 if side else W
 
         def fill(edge, bulk, side, base):
             for f in range(nv + 1):
@@ -195,9 +194,10 @@
 
     for f in range(nv + 1):
         for j in range(W):
-            rows = slice((f * W + j) * al, (f * W + j + 1) * al)
             for src, b in ((below, j), (above, sl + W + j)):
-                ext[f, b * br + 8 : b * br + 8 + al, :] = src[rows, :]
+                for t in range(turns):
+                    at = b * br + 8 * (t + 1)
+                    ext[f, at : at + 8, :] = src[pl.ds((f * W + j) * al + t, 8, stride=turns), :]
 
     def each(f, carry):
         def store(row, val):
@@ -335,11 +335,37 @@
                 out[i].append(acc[i])
         return out
 
-    def gather(view, at):
-        def load(off):
-            return [view[v, at + off : at + off + 8, :] for v in range(nv)]
-
-        return {"q": load(0), "axial-": load(-1), "axial+": load(1), "span-": load(-br), "span+": load(br)}
+    turns = al // 8
+    sub = lax.broadcasted_iota(jnp.int32, (8, 128), 0)
+    top, bottom = sub == 0, sub == 7
+
+    def block_cells(view, at):
+        memo = {}
+
+        def load(t, off=0):
+            if (t, off) not in memo:
+                row = at + off + 8 * t
+                memo[t, off] = [view[v, row : row + 8, :] for v in range(nv)]
+            return memo[t, off]
+
+        def rolled(t, amount):
+            if (t, "roll", amount) not in memo:
+                memo[t, "roll", amount] = [pltpu.roll(x, amount, 0) for x in load(t)]
+            return memo[t, "roll", amount]
+
+        def choose(mask, one, two):
+            return [jnp.where(mask, x, y) for x, y in zip(one, two)]
+
+        def values(t):
+            if t == 0:
+                plus = choose(bottom, rolled(1, 7), rolled(0, 7))
+                minus = choose(top, rolled(turns, 1), rolled(0, 1))
+            else:
+                plus = load(t + 1) if t < turns else choose(bottom, rolled(0, 7), rolled(1, 7))
+                minus = load(t - 1) if t > 1 else choose(top, rolled(0, 1), rolled(turns, 1))
+            return {"q": load(t), "axial-": minus, "axial+": plus, "span-": load(t, -br), "span+": load(t, br)}
+
+        return values
 
     def turn(cell, beyond, at_plus, at_minus):
         cell["theta+"] = [
@@ -357,53 +383,55 @@
             p_src[v, 0:br, :] = pltpu.roll(p_src[v, last - br : last, :], 8, 1)
             p_src[v, last : last + br, :] = pltpu.roll(p_src[v, br : 2 * br, :], 120, 1)
 
-        def blocks(b, count, tiles):
+        def blocks(b, count, first):
             around = pl.multiple_of((b - 1) * br, 8)
-            rows = (count + 1) * br + (8 if tiles == [0] else br)
-            view = src.at[:, pl.ds(around, rows), :]
-            for t in tiles:
+            view = src.at[:, pl.ds(around, (count + 2) * br), :]
+            values = [block_cells(view, (i + 1) * br) for i in range(count)]
+            groups = [[(i, t) for t in range(1, turns + 1)] for i in range(count)]
+            if first == 0:
+                groups.append([(i, 0) for i in range(count)])
+            for group in groups:
                 cells = []
-                for i in range(count):
+                for i, t in group:
                     r = (b + i) // ng
                     g = b + i - r * ng
                     p_row = pl.multiple_of((g + 1) * br, 8) + 8 * t
-                    cell = gather(view, (i + 1) * br + 8 * t)
+                    cell = values[i](t)
                     beyond = [pltpu.roll(p_src[v, pl.ds(p_row, 8), :], 124 - 8 * r, 1) for v in range(nv)]
                     turn(cell, beyond, first_lane, last_lane)
                     cells.append(cell)
-                for i, result in enumerate(apply(cells)):
+                for (i, t), result in zip(group, apply(cells)):
                     row = pl.multiple_of((b + i) * br, 8) + 8 * t
                     step = factor * ext[nv, pl.ds(row, 8), :]
-                    out = pl.multiple_of((b + i - W) * al, 8) + 8 * (t - 1)
                     for u in range(nv):
                         value = ext[u, pl.ds(row, 8), :] - step * result[u]
                         if final:
-                            new_v[u, pl.ds(out, 8), :] = value
+                            rows = pl.ds(pl.multiple_of((b + i - W) * al, 8) + t - 1, 8, stride=turns)
+                            new_v[u, rows, :] = value
                         else:
                             dst[u, pl.ds(row, 8), :] = value
                             if t > 0 and number == 0:
-                                res_v[u, pl.ds(out + spare, 8), :] = result[u]
-
-        def run(first, count, tiles):
+                                rows = pl.ds(pl.multiple_of((b + i - 1) * al, 8) + t - 1, 8, stride=turns)
+                                res_v[u, rows, :] = result[u]
+
+        def run(start, count, first):
             def loop(j, carry):
-                blocks(first + 2 * j, 2, tiles)
+                blocks(start + 2 * j, 2, first)
                 return carry
 
             lax.fori_loop(0, count // 2, loop, 0)
             if count % 2:
-                blocks(first + count - 1, 1, tiles)
+                blocks(start + count - 1, 1, first)
 
         if final:
-            tiles = list(range(1, br // 8))
             for i in range(parts):
-                run(W + i * (sl // parts), sl // parts, tiles)
+                run(W + i * (sl // parts), sl // parts, 1)
                 rows = pl.ds(i * (sl // parts) * al, sl // parts * al)
                 copy = pltpu.make_async_copy(new_v.at[:, rows, :], new.at[:, rows, :], sem.at[i + 1])
                 copy.start()
                 writes.append(copy)
         else:
-            run(W - width, sl + 2 * width, list(range(br // 8)))
-            blocks(sl + W + width, 1, [0])
+            run(W - width, sl + 2 * width, 0)
         if number == 0:
             writes[0].start()
         if final:
@@ -423,8 +451,9 @@
             around = pl.multiple_of(g * br, 8)
             view = p_src.at[:, pl.ds(around, 3 * br), :]
 
+            values = block_cells(view, br)
             for t in range(br // 8):
-                cell = gather(view, br + 8 * t)
+                cell = values(t)
                 turn(cell, [edge[v, pl.ds(around + 8 * t, 8), :] for v in range(nv)], pos4, pos3)
                 (result,) = apply([cell])
                 step = factor * p_0[nv, pl.ds(base + 8 * t, 8), :]
@@ -465,7 +494,7 @@
     n_circ, n_span, n_axial = (lax.axis_size(a) for a in AXES)
     nv, sl, al, cl = state.shape
     br = al + 2 * W
-    nb = sl + 2 * W + 1
+    nb = sl + 2 * W
     ng = -(-nb // 16)
     nh = harmonic_list.shape[0]
     dims = dict(

time: 65.6 us -> 64.9 us (0.989)
  Pallas kernels: 33.1 us -> 32.3 us
    pallas_call x1, Pallas kernels: 28.6 us -> 27.9 us  [local(): pl.pallas_call(functools.partial(step_kernel, dims), out_shape=[block, bl...]
where the time goes in v2:
time: 64.9 us; the launch traced here: 64.6 us
  Pallas kernels  32.3 us (50%)
  starting transfers between devices  16.4 us (25%)
  waiting for transfers between devices  12.5 us (19%)
  local copies, waits for them, and re-layouts  2.04 us (3%)
  between operations  1.43 us (2%)
    pallas_call x1, Pallas kernels, local(): pl.pallas_call(functools.partial(step_kernel, dims), out_shape=[block, bl...  27.9 us
    ppermute x1, waiting for transfers between devices, local(): above = lax.ppermute(down, 'span', shift_pairs(n_span, -1, False))  4.4 us
    ppermute x1, starting transfers between devices, local(): lax.ppermute(part, ('span', 'axial'), shift_pairs(n_span * n_axial, 1, Fa...  3.98 us
    ppermute x1, waiting for transfers between devices, local(): shares = [share, lax.ppermute(share, 'circ', shift_pairs(n_circ, 2, True))]  3.4 us
    ppermute x2, waiting for transfers between devices, axial_move(): moved = lax.ppermute(faces[0], 'axial', [(0, 1), (1, 0)])  3.38 us
    ppermute x1, starting transfers between devices, local(): below = lax.ppermute(up, 'span', shift_pairs(n_span, 1, False))  3.37 us
    pallas_call x1, Pallas kernels, local(): pl.pallas_call(functools.partial(axial_kernel, dims), out_shape=[jax.Shap...  2.21 us
    ppermute x1, starting transfers between devices, local(): from_right = lax.ppermute(left, 'circ', shift_pairs(n_circ, -1, True))  2.09 us
  transfers between devices with their start and end apart: 9, of which 4 were waited for; matrix products, arithmetic and copies ran while one was open for 0% of the time, Pallas kernels for 1%

profile of v2, /device:TPU:1, one launch (start us, length us, event | category | flops | bytes accessed | tf_op | source)
XLA Modules:
  0.0 64.6 jit_solution(17517946811103523692)
XLA Ops:
  0.6 0.0 copy-start.1
  0.6 0.0 copy-start.5
  0.7 0.0 copy-start.6
  1.3 2.2 %axial_faces.1 = (f32[1,6,4,8,128]{4,3,2,1,0:T(8,128)}, f32[1,6,4,24,128]{4,3,2,1,0:T(8,128)}, f32[16,128]{1,0:T(8,128)}) custom-call(f32[5,32,16,128]{3,2,1,0:T(8,128)} %state.1, f32[32,16,128]{2,1,0:T(8,128)} %dt.1, f32[5,8,128]{2,1,0:T(8,128)} %rotor.1, s32[1]{0:T(128)S(6)} %copy.13.blade, s32[8]{0:T(128)} %harm.3), custom_call_target="tpu_custom_call" | custom-call | tf_op jit(solution)/shard_map/axial_faces/pallas_call | solution.py:511
  3.6 4.0 %collective-permute-start.3 = (f32[16,128]{1,0:T(8,128)}, f32[16,128]{1,0:T(8,128)S(1)}, u32[]{:S(2)}, u32[]{:S(2)}) collective-permute-start(f32[16,128]{1,0:T(8,128)} %get-tuple-element.16.part), channel_id=1, source_target_pairs={{0,1},{1,2},{2,3},{3,4},{4,5},{5,6},{6,7},{8,9},{9,10},{10,11},{11... | collective-permute-start | bytes 24584 | tf_op jit(solution)/shard_map/ppermute | solution.py:545
  7.6 1.8 %collective-permute-start.2 = (f32[16,128]{1,0:T(8,128)}, f32[16,128]{1,0:T(8,128)S(1)}, u32[]{:S(2)}, u32[]{:S(2)}) collective-permute-start(f32[16,128]{1,0:T(8,128)} %get-tuple-element.16.part), channel_id=1, source_target_pairs={{0,1},{1,0},{2,3},{3,2},{4,5},{5,4},{6,7},{7,6},{8,9},{9,8},{10,11... | collective-permute-start | bytes 24584 | tf_op jit(solution)/shard_map/ppermute | solution.py:544
  9.4 0.1 collective-permute-start
  9.4 1.4 %collective-permute-start.1 = (f32[6,4,24,128]{3,2,1,0:T(8,128)}, f32[6,4,24,128]{3,2,1,0:T(8,128)S(1)}, u32[]{:S(2)}, u32[]{:S(2)}) collective-permute-start(f32[6,4,24,128]{3,2,1,0:T(8,128)} %bitcast.18), channel_id=1, source_target_pairs={{0,1},{1,0},{2,3},{3,2},{4,5},{5,4},{6,7},{7,6},{8,9},{9,8},{10,11... | collective-permute-start | bytes 884744 | tf_op jit(solution)/shard_map/ppermute | solution.py:536
  10.8 0.0 copy-done.5
  10.8 0.0 copy-done.6
  10.8 0.0 collective-permute-done.3.before
  10.9 0.0 collective-permute-done.2.other
  10.9 3.4 %collective-permute-done.lo.hi.lo_edge.hi_edge = f32[6,4,8,128]{3,2,1,0:T(8,128)S(1)} collective-permute-done((f32[6,4,8,128]{3,2,1,0:T(8,128)}, f32[6,4,8,128]{3,2,1,0:T(8,128)S(1)}, u32[]{:S(2)}, u32[]{:S(2)}) %collective-permute-start) | collective-permute-done | bytes 98336 | tf_op jit(solution)/shard_map/ppermute | solution.py:536
  14.2 0.0 copy-done.1
  14.2 0.0 copy-start
  14.2 1.3 %copy-done = f32[5,32,16,128]{3,2,1,0:T(8,128)S(1)} copy-done((f32[5,32,16,128]{3,2,1,0:T(8,128)S(1)}, f32[5,32,16,128]{3,2,1,0:T(8,128)}, u32[]{:S(2)}) %copy-start) | copy-done | bytes 1310744
  15.6 0.0 copy-start.2
  15.6 0.7 %copy-done.2 = f32[16,128]{1,0:T(8,128)S(1)} copy-done((f32[16,128]{1,0:T(8,128)S(1)}, f32[16,128]{1,0:T(8,128)}, u32[]{:S(2)}) %copy-start.2) | copy-done | bytes 8216
  16.3 0.5 span_faces.1
  16.8 3.4 %collective-permute-start.4 = (f32[496,128]{1,0:T(8,128)S(1)}, f32[496,128]{1,0:T(8,128)S(1)}, u32[]{:S(2)}, u32[]{:S(2)}) collective-permute-start(f32[496,128]{1,0:T(8,128)S(1)} %get-tuple-element.17), channel_id=1, source_target_pairs={{0,2},{2,4},{4,6},{1,3},{3,5},{5,7},{8,10},{10,12},{12,14},{9,11},... | collective-permute-start | bytes 761864 | tf_op jit(solution)/shard_map/ppermute | solution.py:583
  20.1 1.9 %collective-permute-start.5 = (f32[496,128]{1,0:T(8,128)S(1)}, f32[496,128]{1,0:T(8,128)S(1)}, u32[]{:S(2)}, u32[]{:S(2)}) collective-permute-start(f32[496,128]{1,0:T(8,128)S(1)} %get-tuple-element.18), channel_id=1, source_target_pairs={{2,0},{4,2},{6,4},{3,1},{5,3},{7,5},{10,8},{12,10},{14,12},{11,9},... | collective-permute-start | bytes 761864 | tf_op jit(solution)/shard_map/ppermute | solution.py:584
  22.1 0.0 collective-permute-done.1.lo.hi
  22.1 1.3 %collective-permute-done.4.below = f32[496,128]{1,0:T(8,128)S(1)} collective-permute-done((f32[496,128]{1,0:T(8,128)S(1)}, f32[496,128]{1,0:T(8,128)S(1)}, u32[]{:S(2)}, u32[]{:S(2)}) %collective-permute-start.4) | collective-permute-done | bytes 253984 | tf_op jit(solution)/shard_map/ppermute | solution.py:583
  23.3 4.4 %collective-permute-done.5.above = f32[496,128]{1,0:T(8,128)S(1)} collective-permute-done((f32[496,128]{1,0:T(8,128)S(1)}, f32[496,128]{1,0:T(8,128)S(1)}, u32[]{:S(2)}, u32[]{:S(2)}) %collective-permute-start.5) | collective-permute-done | bytes 253984 | tf_op jit(solution)/shard_map/ppermute | solution.py:584
  27.7 0.0 copy-start.4
  27.7 0.0 copy-start.3
  27.7 1.7 %circ_faces.1 = (f32[6,960,128]{2,1,0:T(8,128)S(1)}, f32[248,128]{1,0:T(8,128)S(1)}, f32[248,128]{1,0:T(8,128)S(1)}, f32[32,128]{1,0:T(8,128)S(1)}) custom-call(f32[5,512,128]{2,1,0:T(8,128)S(1)} %bitcast.12, f32[512,128]{1,0:T(8,128)S(1)} %bitcast.15, f32[6,4,8,128]{3,2,1,0:T(8,128)S(1)} %collective-permute-done.lo.hi.lo_edge.hi_edge, ...), custom_call_target="tpu_custom_call" | custom-call | tf_op jit(solution)/shard_map/circ_faces/pallas_call | solution.py:587
  29.4 1.3 %collective-permute-start.7 = (f32[248,128]{1,0:T(8,128)S(1)}, f32[248,128]{1,0:T(8,128)S(1)}, u32[]{:S(2)}, u32[]{:S(2)}) collective-permute-start(f32[248,128]{1,0:T(8,128)S(1)} %get-tuple-element.22), channel_id=1, source_target_pairs={{0,8},{8,16},{16,24},{24,0},{1,9},{9,17},{17,25},{25,1},{2,10},{10... | collective-permute-start | bytes 380936 | tf_op jit(solution)/shard_map/ppermute | solution.py:601
  30.8 2.1 %collective-permute-start.8 = (f32[248,128]{1,0:T(8,128)S(1)}, f32[248,128]{1,0:T(8,128)S(1)}, u32[]{:S(2)}, u32[]{:S(2)}) collective-permute-start(f32[248,128]{1,0:T(8,128)S(1)} %get-tuple-element.23), channel_id=1, source_target_pairs={{0,24},{8,0},{16,8},{24,16},{1,25},{9,1},{17,9},{25,17},{2,26},{10... | collective-permute-start | bytes 380936 | tf_op jit(solution)/shard_map/ppermute | solution.py:602
  32.9 0.4 collective-permute-start.6
  33.3 0.0 copy-done.4
  33.3 3.4 %collective-permute-done.6.shares_1_ = f32[32,128]{1,0:T(8,128)S(1)} collective-permute-done((f32[32,128]{1,0:T(8,128)S(1)}, f32[32,128]{1,0:T(8,128)S(1)}, u32[]{:S(2)}, u32[]{:S(2)}) %collective-permute-start.6) | collective-permute-done | bytes 16416 | tf_op jit(solution)/shard_map/ppermute | solution.py:604
  36.7 0.0 collective-permute-done.7.from_left
  36.7 0.0 collective-permute-done.8.from_right
  36.7 0.0 copy-done.3
  36.7 27.9 %segments.1 = (f32[5,512,128]{2,1,0:T(8,128)}, f32[5,512,128]{2,1,0:T(8,128)}, f32[6,960,128]{2,1,0:T(8,128)S(1)}) custom-call(f32[3,5,5]{2,1,0:T(8,128)S(1)} %copy.11.jac, s32[8]{0:T(128)S(1)} %copy-done.3, s32[1]{0:T(128)S(6)} %copy.13.blade, f32[32,128]{1,0:T(8,128)S(1)} %get-tuple-element.20.shares_0_, ...), custom_call_target="tpu_custom_call", output_to_operand_aliasing={{2}: (5, {})} | custom-call | tf_op jit(solution)/shard_map/segments/pallas_call | solution.py:609
  (3 shorter events, 0.0 us)
Async XLA Ops:
  0.6 13.6 %copy-start.1 = (f32[32,16,128]{2,1,0:T(8,128)S(1)}, f32[32,16,128]{2,1,0:T(8,128)}, u32[]{:S(2)}) copy-start(f32[32,16,128]{2,1,0:T(8,128)} %dt.1) | copy-start | bytes 786436
  0.6 10.2 %copy-start.5 = (s32[32]{0:T(128)S(1)}, s32[32]{0:T(128)}, u32[]{:S(2)}) copy-start(s32[32]{0:T(128)} %param.11) | copy-start | bytes 388
  0.7 10.2 %copy-start.6 = (f32[32]{0:T(128)S(1)}, f32[32]{0:T(128)}, u32[]{:S(2)}) copy-start(f32[32]{0:T(128)} %param.12) | copy-start | bytes 388
  3.6 7.3 %collective-permute-start.3 = (f32[16,128]{1,0:T(8,128)}, f32[16,128]{1,0:T(8,128)S(1)}, u32[]{:S(2)}, u32[]{:S(2)}) collective-permute-start(f32[16,128]{1,0:T(8,128)} %get-tuple-element.16.part), channel_id=1, source_target_pairs={{0,1},{1,2},{2,3},{3,4},{4,5},{5,6},{6,7},{8,9},{9,10},{10,11},{11... | collective-permute-start | bytes 24584 | tf_op jit(solution)/shard_map/ppermute | solution.py:545
  7.6 3.3 %collective-permute-start.2 = (f32[16,128]{1,0:T(8,128)}, f32[16,128]{1,0:T(8,128)S(1)}, u32[]{:S(2)}, u32[]{:S(2)}) collective-permute-start(f32[16,128]{1,0:T(8,128)} %get-tuple-element.16.part), channel_id=1, source_target_pairs={{0,1},{1,0},{2,3},{3,2},{4,5},{5,4},{6,7},{7,6},{8,9},{9,8},{10,11... | collective-permute-start | bytes 24584 | tf_op jit(solution)/shard_map/ppermute | solution.py:544
  9.4 4.9 %collective-permute-start = (f32[6,4,8,128]{3,2,1,0:T(8,128)}, f32[6,4,8,128]{3,2,1,0:T(8,128)S(1)}, u32[]{:S(2)}, u32[]{:S(2)}) collective-permute-start(f32[6,4,8,128]{3,2,1,0:T(8,128)} %bitcast.19), channel_id=1, source_target_pairs={{0,1},{1,0},{2,3},{3,2},{4,5},{5,4},{6,7},{7,6},{8,9},{9,8},{10,11... | collective-permute-start | bytes 294920 | tf_op jit(solution)/shard_map/ppermute | solution.py:536
  9.4 12.6 %collective-permute-start.1 = (f32[6,4,24,128]{3,2,1,0:T(8,128)}, f32[6,4,24,128]{3,2,1,0:T(8,128)S(1)}, u32[]{:S(2)}, u32[]{:S(2)}) collective-permute-start(f32[6,4,24,128]{3,2,1,0:T(8,128)} %bitcast.18), channel_id=1, source_target_pairs={{0,1},{1,0},{2,3},{3,2},{4,5},{5,4},{6,7},{7,6},{8,9},{9,8},{10,11... | collective-permute-start | bytes 884744 | tf_op jit(solution)/shard_map/ppermute | solution.py:536
  14.2 1.3 %copy-start = (f32[5,32,16,128]{3,2,1,0:T(8,128)S(1)}, f32[5,32,16,128]{3,2,1,0:T(8,128)}, u32[]{:S(2)}) copy-start(f32[5,32,16,128]{3,2,1,0:T(8,128)} %state.1) | copy-start | bytes 3932164
  15.6 0.7 %copy-start.2 = (f32[16,128]{1,0:T(8,128)S(1)}, f32[16,128]{1,0:T(8,128)}, u32[]{:S(2)}) copy-start(f32[16,128]{1,0:T(8,128)} %get-tuple-element.16.part) | copy-start | bytes 24580
  16.8 6.6 %collective-permute-start.4 = (f32[496,128]{1,0:T(8,128)S(1)}, f32[496,128]{1,0:T(8,128)S(1)}, u32[]{:S(2)}, u32[]{:S(2)}) collective-permute-start(f32[496,128]{1,0:T(8,128)S(1)} %get-tuple-element.17), channel_id=1, source_target_pairs={{0,2},{2,4},{4,6},{1,3},{3,5},{5,7},{8,10},{10,12},{12,14},{9,11},... | collective-permute-start | bytes 761864 | tf_op jit(solution)/shard_map/ppermute | solution.py:583
  20.1 7.6 %collective-permute-start.5 = (f32[496,128]{1,0:T(8,128)S(1)}, f32[496,128]{1,0:T(8,128)S(1)}, u32[]{:S(2)}, u32[]{:S(2)}) collective-permute-start(f32[496,128]{1,0:T(8,128)S(1)} %get-tuple-element.18), channel_id=1, source_target_pairs={{2,0},{4,2},{6,4},{3,1},{5,3},{7,5},{10,8},{12,10},{14,12},{11,9},... | collective-permute-start | bytes 761864 | tf_op jit(solution)/shard_map/ppermute | solution.py:584
  27.7 5.5 %copy-start.4 = (f32[3,5,5]{2,0,1:T(4,128)S(1)}, f32[3,5,5]{2,0,1:T(4,128)}, u32[]{:S(2)}) copy-start(f32[3,5,5]{2,0,1:T(4,128)} %param.15) | copy-start | bytes 904
  27.7 8.9 %copy-start.3 = (s32[8]{0:T(128)S(1)}, s32[8]{0:T(128)}, u32[]{:S(2)}) copy-start(s32[8]{0:T(128)} %harm.3) | copy-start | bytes 100
  29.4 7.2 %collective-permute-start.7 = (f32[248,128]{1,0:T(8,128)S(1)}, f32[248,128]{1,0:T(8,128)S(1)}, u32[]{:S(2)}, u32[]{:S(2)}) collective-permute-start(f32[248,128]{1,0:T(8,128)S(1)} %get-tuple-element.22), channel_id=1, source_target_pairs={{0,8},{8,16},{16,24},{24,0},{1,9},{9,17},{17,25},{25,1},{2,10},{10... | collective-permute-start | bytes 380936 | tf_op jit(solution)/shard_map/ppermute | solution.py:601
  30.8 5.9 %collective-permute-start.8 = (f32[248,128]{1,0:T(8,128)S(1)}, f32[248,128]{1,0:T(8,128)S(1)}, u32[]{:S(2)}, u32[]{:S(2)}) collective-permute-start(f32[248,128]{1,0:T(8,128)S(1)} %get-tuple-element.23), channel_id=1, source_target_pairs={{0,24},{8,0},{16,8},{24,16},{1,25},{9,1},{17,9},{25,17},{2,26},{10... | collective-permute-start | bytes 380936 | tf_op jit(solution)/shard_map/ppermute | solution.py:602
  32.9 3.8 %collective-permute-start.6 = (f32[32,128]{1,0:T(8,128)S(1)}, f32[32,128]{1,0:T(8,128)S(1)}, u32[]{:S(2)}, u32[]{:S(2)}) collective-permute-start(f32[32,128]{1,0:T(8,128)S(1)} %get-tuple-element.20.shares_0_), channel_id=1, source_target_pairs={{0,16},{8,24},{16,0},{24,8},{1,17},{9,25},{17,1},{25,9},{2,18},{10... | collective-permute-start | bytes 49160 | tf_op jit(solution)/shard_map/ppermute | solution.py:604

commit v3 on v2

--- a/solution.py
+++ b/solution.py
@@ -323,16 +323,20 @@
                 (2.0 * DISSIP) * (3.0 * q - (x + y + z))
                 for q, x, y, z in zip(c["q"], c["axial-"], c["span-"], c["theta-"])
             ]
-        out = [[] for _ in cells]
-        for u in range(nv):
-            acc = [c["rest"][u] for c in cells]
-            for d in range(3):
-                for v in range(nv):
-                    k = coef[(d * nv + u) * nv + v]
-                    for i, c in enumerate(cells):
-                        acc[i] = acc[i] + k * c["diff"][d][v]
-            for i in range(len(cells)):
-                out[i].append(acc[i])
+        out = [[None] * nv for _ in cells]
+        for first in range(0, nv, 2):
+            some = range(first, min(first + 2, nv))
+            sums = {}
+            for v in range(nv):
+                for d in range(3):
+                    for u in some:
+                        k = coef[(d * nv + u) * nv + v]
+                        for i, c in enumerate(cells):
+                            term = k * c["diff"][d][v]
+                            sums[i, u, d] = sums[i, u, d] + term if v else term
+            for u in some:
+                for i, c in enumerate(cells):
+                    out[i][u] = (sums[i, u, 0] + sums[i, u, 1]) + (sums[i, u, 2] + c["rest"][u])
         return out
 
     turns = al // 8
@@ -390,21 +394,30 @@
             groups = [[(i, t) for t in range(1, turns + 1)] for i in range(count)]
             if first == 0:
                 groups.append([(i, 0) for i in range(count)])
-            for group in groups:
+
+            def prepare(group):
                 cells = []
                 for i, t in group:
                     r = (b + i) // ng
                     g = b + i - r * ng
                     p_row = pl.multiple_of((g + 1) * br, 8) + 8 * t
+                    row = pl.multiple_of((b + i) * br, 8) + 8 * t
                     cell = values[i](t)
                     beyond = [pltpu.roll(p_src[v, pl.ds(p_row, 8), :], 124 - 8 * r, 1) for v in range(nv)]
                     turn(cell, beyond, first_lane, last_lane)
+                    cell["base"] = [ext[u, pl.ds(row, 8), :] for u in range(nv)] if number else cell["q"]
+                    cell["step"] = factor * ext[nv, pl.ds(row, 8), :]
                     cells.append(cell)
-                for (i, t), result in zip(group, apply(cells)):
+                return cells
+
+            cells = prepare(groups[0])
+            for n, group in enumerate(groups):
+                following = prepare(groups[n + 1]) if n + 1 < len(groups) else None
+                results = apply(cells)
+                for (i, t), cell, result in zip(group, cells, results):
                     row = pl.multiple_of((b + i) * br, 8) + 8 * t
-                    step = factor * ext[nv, pl.ds(row, 8), :]
                     for u in range(nv):
-                        value = ext[u, pl.ds(row, 8), :] - step * result[u]
+                        value = cell["base"][u] - cell["step"] * result[u]
                         if final:
                             rows = pl.ds(pl.multiple_of((b + i - W) * al, 8) + t - 1, 8, stride=turns)
                             new_v[u, rows, :] = value
@@ -413,6 +426,7 @@
                             if t > 0 and number == 0:
                                 rows = pl.ds(pl.multiple_of((b + i - 1) * al, 8) + t - 1, 8, stride=turns)
                                 res_v[u, rows, :] = result[u]
+                cells = following
 
         def run(start, count, first):
             def loop(j, carry):

time: 64.9 us -> 62.9 us (0.969)
  Pallas kernels: 32.3 us -> 30.3 us
    pallas_call x1, Pallas kernels: 27.9 us -> 25.9 us  [local(): pl.pallas_call(functools.partial(step_kernel, dims), out_shape=[block, bl...]
where the time goes in v3:
time: 62.9 us; the launch traced here: 62.6 us
  Pallas kernels  30.3 us (48%)
  starting transfers between devices  16.4 us (26%)
  waiting for transfers between devices  12.5 us (20%)
  local copies, waits for them, and re-layouts  2.04 us (3%)
  between operations  1.43 us (2%)
    pallas_call x1, Pallas kernels, local(): pl.pallas_call(functools.partial(step_kernel, dims), out_shape=[block, bl...  25.9 us
    ppermute x1, waiting for transfers between devices, local(): above = lax.ppermute(down, 'span', shift_pairs(n_span, -1, False))  4.4 us
    ppermute x1, starting transfers between devices, local(): lax.ppermute(part, ('span', 'axial'), shift_pairs(n_span * n_axial, 1, Fa...  3.98 us
    ppermute x1, waiting for transfers between devices, local(): shares = [share, lax.ppermute(share, 'circ', shift_pairs(n_circ, 2, True))]  3.4 us
    ppermute x2, waiting for transfers between devices, axial_move(): moved = lax.ppermute(faces[0], 'axial', [(0, 1), (1, 0)])  3.38 us
    ppermute x1, starting transfers between devices, local(): below = lax.ppermute(up, 'span', shift_pairs(n_span, 1, False))  3.37 us
    pallas_call x1, Pallas kernels, local(): pl.pallas_call(functools.partial(axial_kernel, dims), out_shape=[jax.Shap...  2.21 us
    ppermute x1, starting transfers between devices, local(): from_right = lax.ppermute(left, 'circ', shift_pairs(n_circ, -1, True))  2.09 us
  transfers between devices with their start and end apart: 9, of which 4 were waited for; matrix products, arithmetic and copies ran while one was open for 0% of the time, Pallas kernels for 1%

profile of v3, /device:TPU:1, one launch (start us, length us, event | category | flops | bytes accessed | tf_op | source)
XLA Modules:
  0.0 62.6 jit_solution(10664587979998500057)
XLA Ops:
  0.6 0.0 copy-start.1
  0.6 0.0 copy-start.5
  0.7 0.0 copy-start.6
  1.3 2.2 %axial_faces.1 = (f32[1,6,4,8,128]{4,3,2,1,0:T(8,128)}, f32[1,6,4,24,128]{4,3,2,1,0:T(8,128)}, f32[16,128]{1,0:T(8,128)}) custom-call(f32[5,32,16,128]{3,2,1,0:T(8,128)} %state.1, f32[32,16,128]{2,1,0:T(8,128)} %dt.1, f32[5,8,128]{2,1,0:T(8,128)} %rotor.1, s32[1]{0:T(128)S(6)} %copy.13.blade, s32[8]{0:T(128)} %harm.3), custom_call_target="tpu_custom_call" | custom-call | tf_op jit(solution)/shard_map/axial_faces/pallas_call | solution.py:525
  3.6 4.0 %collective-permute-start.3 = (f32[16,128]{1,0:T(8,128)}, f32[16,128]{1,0:T(8,128)S(1)}, u32[]{:S(2)}, u32[]{:S(2)}) collective-permute-start(f32[16,128]{1,0:T(8,128)} %get-tuple-element.16.part), channel_id=1, source_target_pairs={{0,1},{1,2},{2,3},{3,4},{4,5},{5,6},{6,7},{8,9},{9,10},{10,11},{11... | collective-permute-start | bytes 24584 | tf_op jit(solution)/shard_map/ppermute | solution.py:559
  7.6 1.8 %collective-permute-start.2 = (f32[16,128]{1,0:T(8,128)}, f32[16,128]{1,0:T(8,128)S(1)}, u32[]{:S(2)}, u32[]{:S(2)}) collective-permute-start(f32[16,128]{1,0:T(8,128)} %get-tuple-element.16.part), channel_id=1, source_target_pairs={{0,1},{1,0},{2,3},{3,2},{4,5},{5,4},{6,7},{7,6},{8,9},{9,8},{10,11... | collective-permute-start | bytes 24584 | tf_op jit(solution)/shard_map/ppermute | solution.py:558
  9.4 0.1 collective-permute-start
  9.4 1.4 %collective-permute-start.1 = (f32[6,4,24,128]{3,2,1,0:T(8,128)}, f32[6,4,24,128]{3,2,1,0:T(8,128)S(1)}, u32[]{:S(2)}, u32[]{:S(2)}) collective-permute-start(f32[6,4,24,128]{3,2,1,0:T(8,128)} %bitcast.18), channel_id=1, source_target_pairs={{0,1},{1,0},{2,3},{3,2},{4,5},{5,4},{6,7},{7,6},{8,9},{9,8},{10,11... | collective-permute-start | bytes 884744 | tf_op jit(solution)/shard_map/ppermute | solution.py:550
  10.8 0.0 copy-done.5
  10.8 0.0 copy-done.6
  10.8 0.0 collective-permute-done.3.before
  10.9 0.0 collective-permute-done.2.other
  10.9 3.4 %collective-permute-done.lo.hi.lo_edge.hi_edge = f32[6,4,8,128]{3,2,1,0:T(8,128)S(1)} collective-permute-done((f32[6,4,8,128]{3,2,1,0:T(8,128)}, f32[6,4,8,128]{3,2,1,0:T(8,128)S(1)}, u32[]{:S(2)}, u32[]{:S(2)}) %collective-permute-start) | collective-permute-done | bytes 98336 | tf_op jit(solution)/shard_map/ppermute | solution.py:550
  14.2 0.0 copy-done.1
  14.2 0.0 copy-start
  14.2 1.3 %copy-done = f32[5,32,16,128]{3,2,1,0:T(8,128)S(1)} copy-done((f32[5,32,16,128]{3,2,1,0:T(8,128)S(1)}, f32[5,32,16,128]{3,2,1,0:T(8,128)}, u32[]{:S(2)}) %copy-start) | copy-done | bytes 1310744
  15.6 0.0 copy-start.2
  15.6 0.7 %copy-done.2 = f32[16,128]{1,0:T(8,128)S(1)} copy-done((f32[16,128]{1,0:T(8,128)S(1)}, f32[16,128]{1,0:T(8,128)}, u32[]{:S(2)}) %copy-start.2) | copy-done | bytes 8216
  16.3 0.5 span_faces.1
  16.8 3.4 %collective-permute-start.4 = (f32[496,128]{1,0:T(8,128)S(1)}, f32[496,128]{1,0:T(8,128)S(1)}, u32[]{:S(2)}, u32[]{:S(2)}) collective-permute-start(f32[496,128]{1,0:T(8,128)S(1)} %get-tuple-element.17), channel_id=1, source_target_pairs={{0,2},{2,4},{4,6},{1,3},{3,5},{5,7},{8,10},{10,12},{12,14},{9,11},... | collective-permute-start | bytes 761864 | tf_op jit(solution)/shard_map/ppermute | solution.py:597
  20.1 1.9 %collective-permute-start.5 = (f32[496,128]{1,0:T(8,128)S(1)}, f32[496,128]{1,0:T(8,128)S(1)}, u32[]{:S(2)}, u32[]{:S(2)}) collective-permute-start(f32[496,128]{1,0:T(8,128)S(1)} %get-tuple-element.18), channel_id=1, source_target_pairs={{2,0},{4,2},{6,4},{3,1},{5,3},{7,5},{10,8},{12,10},{14,12},{11,9},... | collective-permute-start | bytes 761864 | tf_op jit(solution)/shard_map/ppermute | solution.py:598
  22.1 0.0 collective-permute-done.1.lo.hi
  22.1 1.3 %collective-permute-done.4.below = f32[496,128]{1,0:T(8,128)S(1)} collective-permute-done((f32[496,128]{1,0:T(8,128)S(1)}, f32[496,128]{1,0:T(8,128)S(1)}, u32[]{:S(2)}, u32[]{:S(2)}) %collective-permute-start.4) | collective-permute-done | bytes 253984 | tf_op jit(solution)/shard_map/ppermute | solution.py:597
  23.3 4.4 %collective-permute-done.5.above = f32[496,128]{1,0:T(8,128)S(1)} collective-permute-done((f32[496,128]{1,0:T(8,128)S(1)}, f32[496,128]{1,0:T(8,128)S(1)}, u32[]{:S(2)}, u32[]{:S(2)}) %collective-permute-start.5) | collective-permute-done | bytes 253984 | tf_op jit(solution)/shard_map/ppermute | solution.py:598
  27.7 0.0 copy-start.4
  27.7 0.0 copy-start.3
  27.7 1.7 %circ_faces.1 = (f32[6,960,128]{2,1,0:T(8,128)S(1)}, f32[248,128]{1,0:T(8,128)S(1)}, f32[248,128]{1,0:T(8,128)S(1)}, f32[32,128]{1,0:T(8,128)S(1)}) custom-call(f32[5,512,128]{2,1,0:T(8,128)S(1)} %bitcast.12, f32[512,128]{1,0:T(8,128)S(1)} %bitcast.15, f32[6,4,8,128]{3,2,1,0:T(8,128)S(1)} %collective-permute-done.lo.hi.lo_edge.hi_edge, ...), custom_call_target="tpu_custom_call" | custom-call | tf_op jit(solution)/shard_map/circ_faces/pallas_call | solution.py:601
  29.4 1.3 %collective-permute-start.7 = (f32[248,128]{1,0:T(8,128)S(1)}, f32[248,128]{1,0:T(8,128)S(1)}, u32[]{:S(2)}, u32[]{:S(2)}) collective-permute-start(f32[248,128]{1,0:T(8,128)S(1)} %get-tuple-element.22), channel_id=1, source_target_pairs={{0,8},{8,16},{16,24},{24,0},{1,9},{9,17},{17,25},{25,1},{2,10},{10... | collective-permute-start | bytes 380936 | tf_op jit(solution)/shard_map/ppermute | solution.py:615
  30.8 2.1 %collective-permute-start.8 = (f32[248,128]{1,0:T(8,128)S(1)}, f32[248,128]{1,0:T(8,128)S(1)}, u32[]{:S(2)}, u32[]{:S(2)}) collective-permute-start(f32[248,128]{1,0:T(8,128)S(1)} %get-tuple-element.23), channel_id=1, source_target_pairs={{0,24},{8,0},{16,8},{24,16},{1,25},{9,1},{17,9},{25,17},{2,26},{10... | collective-permute-start | bytes 380936 | tf_op jit(solution)/shard_map/ppermute | solution.py:616
  32.9 0.4 collective-permute-start.6
  33.3 0.0 copy-done.4
  33.3 3.4 %collective-permute-done.6.shares_1_ = f32[32,128]{1,0:T(8,128)S(1)} collective-permute-done((f32[32,128]{1,0:T(8,128)S(1)}, f32[32,128]{1,0:T(8,128)S(1)}, u32[]{:S(2)}, u32[]{:S(2)}) %collective-permute-start.6) | collective-permute-done | bytes 16416 | tf_op jit(solution)/shard_map/ppermute | solution.py:618
  36.7 0.0 collective-permute-done.7.from_left
  36.7 0.0 collective-permute-done.8.from_right
  36.7 0.0 copy-done.3
  36.7 25.9 %segments.1 = (f32[5,512,128]{2,1,0:T(8,128)}, f32[5,512,128]{2,1,0:T(8,128)}, f32[6,960,128]{2,1,0:T(8,128)S(1)}) custom-call(f32[3,5,5]{2,1,0:T(8,128)S(1)} %copy.11.jac, s32[8]{0:T(128)S(1)} %copy-done.3, s32[1]{0:T(128)S(6)} %copy.13.blade, f32[32,128]{1,0:T(8,128)S(1)} %get-tuple-element.20.shares_0_, ...), custom_call_target="tpu_custom_call", output_to_operand_aliasing={{2}: (5, {})} | custom-call | tf_op jit(solution)/shard_map/segments/pallas_call | solution.py:623
  (3 shorter events, 0.0 us)
Async XLA Ops:
  0.6 13.6 %copy-start.1 = (f32[32,16,128]{2,1,0:T(8,128)S(1)}, f32[32,16,128]{2,1,0:T(8,128)}, u32[]{:S(2)}) copy-start(f32[32,16,128]{2,1,0:T(8,128)} %dt.1) | copy-start | bytes 786436
  0.6 10.2 %copy-start.5 = (s32[32]{0:T(128)S(1)}, s32[32]{0:T(128)}, u32[]{:S(2)}) copy-start(s32[32]{0:T(128)} %param.11) | copy-start | bytes 388
  0.7 10.2 %copy-start.6 = (f32[32]{0:T(128)S(1)}, f32[32]{0:T(128)}, u32[]{:S(2)}) copy-start(f32[32]{0:T(128)} %param.12) | copy-start | bytes 388
  3.6 7.3 %collective-permute-start.3 = (f32[16,128]{1,0:T(8,128)}, f32[16,128]{1,0:T(8,128)S(1)}, u32[]{:S(2)}, u32[]{:S(2)}) collective-permute-start(f32[16,128]{1,0:T(8,128)} %get-tuple-element.16.part), channel_id=1, source_target_pairs={{0,1},{1,2},{2,3},{3,4},{4,5},{5,6},{6,7},{8,9},{9,10},{10,11},{11... | collective-permute-start | bytes 24584 | tf_op jit(solution)/shard_map/ppermute | solution.py:559
  7.6 3.3 %collective-permute-start.2 = (f32[16,128]{1,0:T(8,128)}, f32[16,128]{1,0:T(8,128)S(1)}, u32[]{:S(2)}, u32[]{:S(2)}) collective-permute-start(f32[16,128]{1,0:T(8,128)} %get-tuple-element.16.part), channel_id=1, source_target_pairs={{0,1},{1,0},{2,3},{3,2},{4,5},{5,4},{6,7},{7,6},{8,9},{9,8},{10,11... | collective-permute-start | bytes 24584 | tf_op jit(solution)/shard_map/ppermute | solution.py:558
  9.4 4.9 %collective-permute-start = (f32[6,4,8,128]{3,2,1,0:T(8,128)}, f32[6,4,8,128]{3,2,1,0:T(8,128)S(1)}, u32[]{:S(2)}, u32[]{:S(2)}) collective-permute-start(f32[6,4,8,128]{3,2,1,0:T(8,128)} %bitcast.19), channel_id=1, source_target_pairs={{0,1},{1,0},{2,3},{3,2},{4,5},{5,4},{6,7},{7,6},{8,9},{9,8},{10,11... | collective-permute-start | bytes 294920 | tf_op jit(solution)/shard_map/ppermute | solution.py:550
  9.4 12.6 %collective-permute-start.1 = (f32[6,4,24,128]{3,2,1,0:T(8,128)}, f32[6,4,24,128]{3,2,1,0:T(8,128)S(1)}, u32[]{:S(2)}, u32[]{:S(2)}) collective-permute-start(f32[6,4,24,128]{3,2,1,0:T(8,128)} %bitcast.18), channel_id=1, source_target_pairs={{0,1},{1,0},{2,3},{3,2},{4,5},{5,4},{6,7},{7,6},{8,9},{9,8},{10,11... | collective-permute-start | bytes 884744 | tf_op jit(solution)/shard_map/ppermute | solution.py:550
  14.2 1.3 %copy-start = (f32[5,32,16,128]{3,2,1,0:T(8,128)S(1)}, f32[5,32,16,128]{3,2,1,0:T(8,128)}, u32[]{:S(2)}) copy-start(f32[5,32,16,128]{3,2,1,0:T(8,128)} %state.1) | copy-start | bytes 3932164
  15.6 0.7 %copy-start.2 = (f32[16,128]{1,0:T(8,128)S(1)}, f32[16,128]{1,0:T(8,128)}, u32[]{:S(2)}) copy-start(f32[16,128]{1,0:T(8,128)} %get-tuple-element.16.part) | copy-start | bytes 24580
  16.8 6.6 %collective-permute-start.4 = (f32[496,128]{1,0:T(8,128)S(1)}, f32[496,128]{1,0:T(8,128)S(1)}, u32[]{:S(2)}, u32[]{:S(2)}) collective-permute-start(f32[496,128]{1,0:T(8,128)S(1)} %get-tuple-element.17), channel_id=1, source_target_pairs={{0,2},{2,4},{4,6},{1,3},{3,5},{5,7},{8,10},{10,12},{12,14},{9,11},... | collective-permute-start | bytes 761864 | tf_op jit(solution)/shard_map/ppermute | solution.py:597
  20.1 7.6 %collective-permute-start.5 = (f32[496,128]{1,0:T(8,128)S(1)}, f32[496,128]{1,0:T(8,128)S(1)}, u32[]{:S(2)}, u32[]{:S(2)}) collective-permute-start(f32[496,128]{1,0:T(8,128)S(1)} %get-tuple-element.18), channel_id=1, source_target_pairs={{2,0},{4,2},{6,4},{3,1},{5,3},{7,5},{10,8},{12,10},{14,12},{11,9},... | collective-permute-start | bytes 761864 | tf_op jit(solution)/shard_map/ppermute | solution.py:598
  27.7 5.5 %copy-start.4 = (f32[3,5,5]{2,0,1:T(4,128)S(1)}, f32[3,5,5]{2,0,1:T(4,128)}, u32[]{:S(2)}) copy-start(f32[3,5,5]{2,0,1:T(4,128)} %param.15) | copy-start | bytes 904
  27.7 8.9 %copy-start.3 = (s32[8]{0:T(128)S(1)}, s32[8]{0:T(128)}, u32[]{:S(2)}) copy-start(s32[8]{0:T(128)} %harm.3) | copy-start | bytes 100
  29.4 7.2 %collective-permute-start.7 = (f32[248,128]{1,0:T(8,128)S(1)}, f32[248,128]{1,0:T(8,128)S(1)}, u32[]{:S(2)}, u32[]{:S(2)}) collective-permute-start(f32[248,128]{1,0:T(8,128)S(1)} %get-tuple-element.22), channel_id=1, source_target_pairs={{0,8},{8,16},{16,24},{24,0},{1,9},{9,17},{17,25},{25,1},{2,10},{10... | collective-permute-start | bytes 380936 | tf_op jit(solution)/shard_map/ppermute | solution.py:615
  30.8 5.9 %collective-permute-start.8 = (f32[248,128]{1,0:T(8,128)S(1)}, f32[248,128]{1,0:T(8,128)S(1)}, u32[]{:S(2)}, u32[]{:S(2)}) collective-permute-start(f32[248,128]{1,0:T(8,128)S(1)} %get-tuple-element.23), channel_id=1, source_target_pairs={{0,24},{8,0},{16,8},{24,16},{1,25},{9,1},{17,9},{25,17},{2,26},{10... | collective-permute-start | bytes 380936 | tf_op jit(solution)/shard_map/ppermute | solution.py:616
  32.9 3.8 %collective-permute-start.6 = (f32[32,128]{1,0:T(8,128)S(1)}, f32[32,128]{1,0:T(8,128)S(1)}, u32[]{:S(2)}, u32[]{:S(2)}) collective-permute-start(f32[32,128]{1,0:T(8,128)S(1)} %get-tuple-element.20.shares_0_), channel_id=1, source_target_pairs={{0,16},{8,24},{16,0},{24,8},{1,17},{9,25},{17,1},{25,9},{2,18},{10... | collective-permute-start | bytes 49160 | tf_op jit(solution)/shard_map/ppermute | solution.py:618

commit v4 on v3

--- a/solution.py
+++ b/solution.py
@@ -262,11 +262,21 @@
     circ = lax.axis_index("circ")
     spare = (W - 1) * al
     parts = 4 if sl % 8 == 0 else 1
-    for d in range(3):
-        for u in range(nv):
+    blocks_of = -(-3 * nv // 16) * 16
+    lane = lax.broadcasted_iota(jnp.int32, (8, 8 * blocks_of), 1)
+    row = lax.broadcasted_iota(jnp.int32, (8, 8 * blocks_of), 0)
+    matrix = []
+    for u in range(nv):
+        part = jnp.zeros((8, 8 * blocks_of), jnp.float32)
+        for d in range(3):
             for v in range(nv):
-                value = jac[d, u, v] * 0.5 - (DISSIP if u == v else 0.0)
-                coef[(d * nv + u) * nv + v] = jnp.full((8, 128), value, jnp.float32)
+                value = (jac[d, u, v] * 0.5 - (DISSIP if u == v else 0.0)) * (0.5 / DISSIP)
+                part = jnp.where(lane == row + 8 * (d * nv + v), value, part)
+        matrix.append(part)
+    matrix = jnp.concatenate(matrix, axis=0)
+    high = matrix.astype(jnp.bfloat16).astype(jnp.float32)
+    again = jnp.concatenate([matrix - high, jnp.zeros_like(high)], axis=1)
+    coef[...] = jnp.concatenate([jnp.concatenate([high, high], axis=1), again], axis=0).astype(jnp.bfloat16)
 
     half = (nv + 1) // 2
     low = lane_ids(ng * br) % 8 < 4
@@ -315,28 +325,24 @@
     last = (ng + 1) * br
 
     def apply(cells):
-        for c in cells:
-            c["diff"] = [
-                [plus - minus for plus, minus in zip(c[d + "+"], c[d + "-"])] for d in ("axial", "span", "theta")
-            ]
-            c["rest"] = [
-                (2.0 * DISSIP) * (3.0 * q - (x + y + z))
-                for q, x, y, z in zip(c["q"], c["axial-"], c["span-"], c["theta-"])
-            ]
+        def beside(name):
+            return [jnp.concatenate(parts, axis=1) for parts in zip(*(c[name] for c in cells))]
+
+        both = {name: beside(name) for name in cells[0] if name[-1] in "+-q"}
+        diff = [p - m for d in ("axial", "span", "theta") for p, m in zip(both[d + "+"], both[d + "-"])]
+        diff += [jnp.zeros_like(diff[0])] * (blocks_of - len(diff))
+        diff = jnp.concatenate(diff, axis=0)
+        high = diff.astype(jnp.bfloat16)
+        low = (diff - high.astype(jnp.float32)).astype(jnp.bfloat16)
+        product = jnp.dot(
+            coef[...], jnp.concatenate([high, low], axis=0), preferred_element_type=jnp.float32
+        )
         out = [[None] * nv for _ in cells]
-        for first in range(0, nv, 2):
-            some = range(first, min(first + 2, nv))
-            sums = {}
-            for v in range(nv):
-                for d in range(3):
-                    for u in some:
-                        k = coef[(d * nv + u) * nv + v]
-                        for i, c in enumerate(cells):
-                            term = k * c["diff"][d][v]
-                            sums[i, u, d] = sums[i, u, d] + term if v else term
-            for u in some:
-                for i, c in enumerate(cells):
-                    out[i][u] = (sums[i, u, 0] + sums[i, u, 1]) + (sums[i, u, 2] + c["rest"][u])
+        for u in range(nv):
+            rest = 3.0 * both["q"][u] - (both["axial-"][u] + both["span-"][u] + both["theta-"][u])
+            total = product[8 * u : 8 * u + 8] + (product[8 * (nv + u) : 8 * (nv + u) + 8] + rest)
+            for i in range(len(cells)):
+                out[i][u] = total[:, 128 * i : 128 * i + 128]
         return out
 
     turns = al // 8
@@ -406,7 +412,7 @@
                     beyond = [pltpu.roll(p_src[v, pl.ds(p_row, 8), :], 124 - 8 * r, 1) for v in range(nv)]
                     turn(cell, beyond, first_lane, last_lane)
                     cell["base"] = [ext[u, pl.ds(row, 8), :] for u in range(nv)] if number else cell["q"]
-                    cell["step"] = factor * ext[nv, pl.ds(row, 8), :]
+                    cell["step"] = (2.0 * DISSIP * factor) * ext[nv, pl.ds(row, 8), :]
                     cells.append(cell)
                 return cells
 
@@ -425,7 +431,7 @@
                             dst[u, pl.ds(row, 8), :] = value
                             if t > 0 and number == 0:
                                 rows = pl.ds(pl.multiple_of((b + i - 1) * al, 8) + t - 1, 8, stride=turns)
-                                res_v[u, rows, :] = result[u]
+                                res_v[u, rows, :] = (2.0 * DISSIP) * result[u]
                 cells = following
 
         def run(start, count, first):
@@ -470,7 +476,7 @@
                 cell = values(t)
                 turn(cell, [edge[v, pl.ds(around + 8 * t, 8), :] for v in range(nv)], pos4, pos3)
                 (result,) = apply([cell])
-                step = factor * p_0[nv, pl.ds(base + 8 * t, 8), :]
+                step = (2.0 * DISSIP * factor) * p_0[nv, pl.ds(base + 8 * t, 8), :]
                 for u in range(nv):
                     p_dst[u, pl.ds(base + 8 * t, 8), :] = p_0[u, pl.ds(base + 8 * t, 8), :] - step * result[u]
             return carry
@@ -635,7 +641,7 @@
             strips,
             strips,
             pltpu.VMEM((nv, ng * br, 128), f32),
-            pltpu.VMEM((3 * nv * nv, 8, 128), f32),
+            pltpu.VMEM((16 * nv, 16 * (-(-3 * nv // 16) * 16)), jnp.bfloat16),
             pltpu.SemaphoreType.DMA((5,)),
         ],
         compiler_params=params,

time: 62.9 us -> 71 us (1.13)
  Pallas kernels: 30.3 us -> 38.4 us
    pallas_call x1, Pallas kernels: 25.9 us -> 34 us  [local(): pl.pallas_call(functools.partial(step_kernel, dims), out_shape=[block, bl...]
where the time goes in v4:
time: 71 us; the launch traced here: 70.7 us
  Pallas kernels  38.4 us (54%)
  starting transfers between devices  16.4 us (23%)
  waiting for transfers between devices  12.5 us (18%)
  local copies, waits for them, and re-layouts  2.04 us (3%)
  between operations  1.43 us (2%)
    pallas_call x1, Pallas kernels, local(): pl.pallas_call(functools.partial(step_kernel, dims), out_shape=[block, bl...  34 us
    ppermute x1, waiting for transfers between devices, local(): above = lax.ppermute(down, 'span', shift_pairs(n_span, -1, False))  4.4 us
    ppermute x1, starting transfers between devices, local(): lax.ppermute(part, ('span', 'axial'), shift_pairs(n_span * n_axial, 1, Fa...  3.98 us
    ppermute x1, waiting for transfers between devices, local(): shares = [share, lax.ppermute(share, 'circ', shift_pairs(n_circ, 2, True))]  3.4 us
    ppermute x2, waiting for transfers between devices, axial_move(): moved = lax.ppermute(faces[0], 'axial', [(0, 1), (1, 0)])  3.38 us
    ppermute x1, starting transfers between devices, local(): below = lax.ppermute(up, 'span', shift_pairs(n_span, 1, False))  3.37 us
    pallas_call x1, Pallas kernels, local(): pl.pallas_call(functools.partial(axial_kernel, dims), out_shape=[jax.Shap...  2.21 us
    ppermute x1, starting transfers between devices, local(): from_right = lax.ppermute(left, 'circ', shift_pairs(n_circ, -1, True))  2.09 us
  transfers between devices with their start and end apart: 9, of which 4 were waited for; matrix products, arithmetic and copies ran while one was open for 0% of the time, Pallas kernels for 1%

profile of v4, /device:TPU:1, one launch (start us, length us, event | category | flops | bytes accessed | tf_op | source)
XLA Modules:
  0.0 70.7 jit_solution(10228063703529632343)
XLA Ops:
  0.6 0.0 copy-start.1
  0.6 0.0 copy-start.5
  0.7 0.0 copy-start.6
  1.3 2.2 %axial_faces.1 = (f32[1,6,4,8,128]{4,3,2,1,0:T(8,128)}, f32[1,6,4,24,128]{4,3,2,1,0:T(8,128)}, f32[16,128]{1,0:T(8,128)}) custom-call(f32[5,32,16,128]{3,2,1,0:T(8,128)} %state.1, f32[32,16,128]{2,1,0:T(8,128)} %dt.1, f32[5,8,128]{2,1,0:T(8,128)} %rotor.1, s32[1]{0:T(128)S(6)} %copy.13.blade, s32[8]{0:T(128)} %harm.3), custom_call_target="tpu_custom_call" | custom-call | tf_op jit(solution)/shard_map/axial_faces/pallas_call | solution.py:531
  3.6 4.0 %collective-permute-start.3 = (f32[16,128]{1,0:T(8,128)}, f32[16,128]{1,0:T(8,128)S(1)}, u32[]{:S(2)}, u32[]{:S(2)}) collective-permute-start(f32[16,128]{1,0:T(8,128)} %get-tuple-element.16.part), channel_id=1, source_target_pairs={{0,1},{1,2},{2,3},{3,4},{4,5},{5,6},{6,7},{8,9},{9,10},{10,11},{11... | collective-permute-start | bytes 24584 | tf_op jit(solution)/shard_map/ppermute | solution.py:565
  7.6 1.8 %collective-permute-start.2 = (f32[16,128]{1,0:T(8,128)}, f32[16,128]{1,0:T(8,128)S(1)}, u32[]{:S(2)}, u32[]{:S(2)}) collective-permute-start(f32[16,128]{1,0:T(8,128)} %get-tuple-element.16.part), channel_id=1, source_target_pairs={{0,1},{1,0},{2,3},{3,2},{4,5},{5,4},{6,7},{7,6},{8,9},{9,8},{10,11... | collective-permute-start | bytes 24584 | tf_op jit(solution)/shard_map/ppermute | solution.py:564
  9.4 0.1 collective-permute-start
  9.4 1.4 %collective-permute-start.1 = (f32[6,4,24,128]{3,2,1,0:T(8,128)}, f32[6,4,24,128]{3,2,1,0:T(8,128)S(1)}, u32[]{:S(2)}, u32[]{:S(2)}) collective-permute-start(f32[6,4,24,128]{3,2,1,0:T(8,128)} %bitcast.18), channel_id=1, source_target_pairs={{0,1},{1,0},{2,3},{3,2},{4,5},{5,4},{6,7},{7,6},{8,9},{9,8},{10,11... | collective-permute-start | bytes 884744 | tf_op jit(solution)/shard_map/ppermute | solution.py:556
  10.8 0.0 copy-done.5
  10.8 0.0 copy-done.6
  10.8 0.0 collective-permute-done.3.before
  10.9 0.0 collective-permute-done.2.other
  10.9 3.4 %collective-permute-done.lo.hi.lo_edge.hi_edge = f32[6,4,8,128]{3,2,1,0:T(8,128)S(1)} collective-permute-done((f32[6,4,8,128]{3,2,1,0:T(8,128)}, f32[6,4,8,128]{3,2,1,0:T(8,128)S(1)}, u32[]{:S(2)}, u32[]{:S(2)}) %collective-permute-start) | collective-permute-done | bytes 98336 | tf_op jit(solution)/shard_map/ppermute | solution.py:556
  14.2 0.0 copy-done.1
  14.2 0.0 copy-start
  14.2 1.3 %copy-done = f32[5,32,16,128]{3,2,1,0:T(8,128)S(1)} copy-done((f32[5,32,16,128]{3,2,1,0:T(8,128)S(1)}, f32[5,32,16,128]{3,2,1,0:T(8,128)}, u32[]{:S(2)}) %copy-start) | copy-done | bytes 1310744
  15.6 0.0 copy-start.2
  15.6 0.7 copy-done.2
  16.3 0.5 span_faces.1
  16.8 3.4 %collective-permute-start.4 = (f32[496,128]{1,0:T(8,128)S(1)}, f32[496,128]{1,0:T(8,128)S(1)}, u32[]{:S(2)}, u32[]{:S(2)}) collective-permute-start(f32[496,128]{1,0:T(8,128)S(1)} %get-tuple-element.17), channel_id=1, source_target_pairs={{0,2},{2,4},{4,6},{1,3},{3,5},{5,7},{8,10},{10,12},{12,14},{9,11},... | collective-permute-start | bytes 761864 | tf_op jit(solution)/shard_map/ppermute | solution.py:603
  20.1 1.9 %collective-permute-start.5 = (f32[496,128]{1,0:T(8,128)S(1)}, f32[496,128]{1,0:T(8,128)S(1)}, u32[]{:S(2)}, u32[]{:S(2)}) collective-permute-start(f32[496,128]{1,0:T(8,128)S(1)} %get-tuple-element.18), channel_id=1, source_target_pairs={{2,0},{4,2},{6,4},{3,1},{5,3},{7,5},{10,8},{12,10},{14,12},{11,9},... | collective-permute-start | bytes 761864 | tf_op jit(solution)/shard_map/ppermute | solution.py:604
  22.1 0.0 collective-permute-done.1.lo.hi
  22.1 1.3 %collective-permute-done.4.below = f32[496,128]{1,0:T(8,128)S(1)} collective-permute-done((f32[496,128]{1,0:T(8,128)S(1)}, f32[496,128]{1,0:T(8,128)S(1)}, u32[]{:S(2)}, u32[]{:S(2)}) %collective-permute-start.4) | collective-permute-done | bytes 253984 | tf_op jit(solution)/shard_map/ppermute | solution.py:603
  23.3 4.4 %collective-permute-done.5.above = f32[496,128]{1,0:T(8,128)S(1)} collective-permute-done((f32[496,128]{1,0:T(8,128)S(1)}, f32[496,128]{1,0:T(8,128)S(1)}, u32[]{:S(2)}, u32[]{:S(2)}) %collective-permute-start.5) | collective-permute-done | bytes 253984 | tf_op jit(solution)/shard_map/ppermute | solution.py:604
  27.7 0.0 copy-start.4
  27.7 0.0 copy-start.3
  27.7 1.7 %circ_faces.1 = (f32[6,960,128]{2,1,0:T(8,128)S(1)}, f32[248,128]{1,0:T(8,128)S(1)}, f32[248,128]{1,0:T(8,128)S(1)}, f32[32,128]{1,0:T(8,128)S(1)}) custom-call(f32[5,512,128]{2,1,0:T(8,128)S(1)} %bitcast.12, f32[512,128]{1,0:T(8,128)S(1)} %bitcast.15, f32[6,4,8,128]{3,2,1,0:T(8,128)S(1)} %collective-permute-done.lo.hi.lo_edge.hi_edge, ...), custom_call_target="tpu_custom_call" | custom-call | tf_op jit(solution)/shard_map/circ_faces/pallas_call | solution.py:607
  29.4 1.3 %collective-permute-start.7 = (f32[248,128]{1,0:T(8,128)S(1)}, f32[248,128]{1,0:T(8,128)S(1)}, u32[]{:S(2)}, u32[]{:S(2)}) collective-permute-start(f32[248,128]{1,0:T(8,128)S(1)} %get-tuple-element.22), channel_id=1, source_target_pairs={{0,8},{8,16},{16,24},{24,0},{1,9},{9,17},{17,25},{25,1},{2,10},{10... | collective-permute-start | bytes 380936 | tf_op jit(solution)/shard_map/ppermute | solution.py:621
  30.8 2.1 %collective-permute-start.8 = (f32[248,128]{1,0:T(8,128)S(1)}, f32[248,128]{1,0:T(8,128)S(1)}, u32[]{:S(2)}, u32[]{:S(2)}) collective-permute-start(f32[248,128]{1,0:T(8,128)S(1)} %get-tuple-element.23), channel_id=1, source_target_pairs={{0,24},{8,0},{16,8},{24,16},{1,25},{9,1},{17,9},{25,17},{2,26},{10... | collective-permute-start | bytes 380936 | tf_op jit(solution)/shard_map/ppermute | solution.py:622
  32.9 0.4 collective-permute-start.6
  33.3 0.0 copy-done.4
  33.3 3.4 %collective-permute-done.6.shares_1_ = f32[32,128]{1,0:T(8,128)S(1)} collective-permute-done((f32[32,128]{1,0:T(8,128)S(1)}, f32[32,128]{1,0:T(8,128)S(1)}, u32[]{:S(2)}, u32[]{:S(2)}) %collective-permute-start.6) | collective-permute-done | bytes 16416 | tf_op jit(solution)/shard_map/ppermute | solution.py:624
  36.7 0.0 collective-permute-done.7.from_left
  36.7 0.0 collective-permute-done.8.from_right
  36.7 0.0 copy-done.3
  36.7 34.0 %segments.1 = (f32[5,512,128]{2,1,0:T(8,128)}, f32[5,512,128]{2,1,0:T(8,128)}, f32[6,960,128]{2,1,0:T(8,128)S(1)}) custom-call(f32[3,5,5]{2,1,0:T(8,128)S(1)} %copy.11.jac, s32[8]{0:T(128)S(1)} %copy-done.3, s32[1]{0:T(128)S(6)} %copy.13.blade, f32[32,128]{1,0:T(8,128)S(1)} %get-tuple-element.20.shares_0_, ...), custom_call_target="tpu_custom_call", output_to_operand_aliasing={{2}: (5, {})} | custom-call | tf_op jit(solution)/shard_map/segments/pallas_call | solution.py:629
  (3 shorter events, 0.0 us)
Async XLA Ops:
  0.6 13.6 %copy-start.1 = (f32[32,16,128]{2,1,0:T(8,128)S(1)}, f32[32,16,128]{2,1,0:T(8,128)}, u32[]{:S(2)}) copy-start(f32[32,16,128]{2,1,0:T(8,128)} %dt.1) | copy-start | bytes 786436
  0.6 10.2 %copy-start.5 = (s32[32]{0:T(128)S(1)}, s32[32]{0:T(128)}, u32[]{:S(2)}) copy-start(s32[32]{0:T(128)} %param.11) | copy-start | bytes 388
  0.7 10.2 %copy-start.6 = (f32[32]{0:T(128)S(1)}, f32[32]{0:T(128)}, u32[]{:S(2)}) copy-start(f32[32]{0:T(128)} %param.12) | copy-start | bytes 388
  3.6 7.3 %collective-permute-start.3 = (f32[16,128]{1,0:T(8,128)}, f32[16,128]{1,0:T(8,128)S(1)}, u32[]{:S(2)}, u32[]{:S(2)}) collective-permute-start(f32[16,128]{1,0:T(8,128)} %get-tuple-element.16.part), channel_id=1, source_target_pairs={{0,1},{1,2},{2,3},{3,4},{4,5},{5,6},{6,7},{8,9},{9,10},{10,11},{11... | collective-permute-start | bytes 24584 | tf_op jit(solution)/shard_map/ppermute | solution.py:565
  7.6 3.3 %collective-permute-start.2 = (f32[16,128]{1,0:T(8,128)}, f32[16,128]{1,0:T(8,128)S(1)}, u32[]{:S(2)}, u32[]{:S(2)}) collective-permute-start(f32[16,128]{1,0:T(8,128)} %get-tuple-element.16.part), channel_id=1, source_target_pairs={{0,1},{1,0},{2,3},{3,2},{4,5},{5,4},{6,7},{7,6},{8,9},{9,8},{10,11... | collective-permute-start | bytes 24584 | tf_op jit(solution)/shard_map/ppermute | solution.py:564
  9.4 4.9 %collective-permute-start = (f32[6,4,8,128]{3,2,1,0:T(8,128)}, f32[6,4,8,128]{3,2,1,0:T(8,128)S(1)}, u32[]{:S(2)}, u32[]{:S(2)}) collective-permute-start(f32[6,4,8,128]{3,2,1,0:T(8,128)} %bitcast.19), channel_id=1, source_target_pairs={{0,1},{1,0},{2,3},{3,2},{4,5},{5,4},{6,7},{7,6},{8,9},{9,8},{10,11... | collective-permute-start | bytes 294920 | tf_op jit(solution)/shard_map/ppermute | solution.py:556
  9.4 12.6 %collective-permute-start.1 = (f32[6,4,24,128]{3,2,1,0:T(8,128)}, f32[6,4,24,128]{3,2,1,0:T(8,128)S(1)}, u32[]{:S(2)}, u32[]{:S(2)}) collective-permute-start(f32[6,4,24,128]{3,2,1,0:T(8,128)} %bitcast.18), channel_id=1, source_target_pairs={{0,1},{1,0},{2,3},{3,2},{4,5},{5,4},{6,7},{7,6},{8,9},{9,8},{10,11... | collective-permute-start | bytes 884744 | tf_op jit(solution)/shard_map/ppermute | solution.py:556
  14.2 1.3 %copy-start = (f32[5,32,16,128]{3,2,1,0:T(8,128)S(1)}, f32[5,32,16,128]{3,2,1,0:T(8,128)}, u32[]{:S(2)}) copy-start(f32[5,32,16,128]{3,2,1,0:T(8,128)} %state.1) | copy-start | bytes 3932164
  15.6 0.7 copy-start.2
  16.8 6.6 %collective-permute-start.4 = (f32[496,128]{1,0:T(8,128)S(1)}, f32[496,128]{1,0:T(8,128)S(1)}, u32[]{:S(2)}, u32[]{:S(2)}) collective-permute-start(f32[496,128]{1,0:T(8,128)S(1)} %get-tuple-element.17), channel_id=1, source_target_pairs={{0,2},{2,4},{4,6},{1,3},{3,5},{5,7},{8,10},{10,12},{12,14},{9,11},... | collective-permute-start | bytes 761864 | tf_op jit(solution)/shard_map/ppermute | solution.py:603
  20.1 7.6 %collective-permute-start.5 = (f32[496,128]{1,0:T(8,128)S(1)}, f32[496,128]{1,0:T(8,128)S(1)}, u32[]{:S(2)}, u32[]{:S(2)}) collective-permute-start(f32[496,128]{1,0:T(8,128)S(1)} %get-tuple-element.18), channel_id=1, source_target_pairs={{2,0},{4,2},{6,4},{3,1},{5,3},{7,5},{10,8},{12,10},{14,12},{11,9},... | collective-permute-start | bytes 761864 | tf_op jit(solution)/shard_map/ppermute | solution.py:604
  27.7 5.5 %copy-start.4 = (f32[3,5,5]{2,0,1:T(4,128)S(1)}, f32[3,5,5]{2,0,1:T(4,128)}, u32[]{:S(2)}) copy-start(f32[3,5,5]{2,0,1:T(4,128)} %param.15) | copy-start | bytes 904
  27.7 8.9 %copy-start.3 = (s32[8]{0:T(128)S(1)}, s32[8]{0:T(128)}, u32[]{:S(2)}) copy-start(s32[8]{0:T(128)} %harm.3) | copy-start | bytes 100
  29.4 7.2 %collective-permute-start.7 = (f32[248,128]{1,0:T(8,128)S(1)}, f32[248,128]{1,0:T(8,128)S(1)}, u32[]{:S(2)}, u32[]{:S(2)}) collective-permute-start(f32[248,128]{1,0:T(8,128)S(1)} %get-tuple-element.22), channel_id=1, source_target_pairs={{0,8},{8,16},{16,24},{24,0},{1,9},{9,17},{17,25},{25,1},{2,10},{10... | collective-permute-start | bytes 380936 | tf_op jit(solution)/shard_map/ppermute | solution.py:621
  30.8 5.9 %collective-permute-start.8 = (f32[248,128]{1,0:T(8,128)S(1)}, f32[248,128]{1,0:T(8,128)S(1)}, u32[]{:S(2)}, u32[]{:S(2)}) collective-permute-start(f32[248,128]{1,0:T(8,128)S(1)} %get-tuple-element.23), channel_id=1, source_target_pairs={{0,24},{8,0},{16,8},{24,16},{1,25},{9,1},{17,9},{25,17},{2,26},{10... | collective-permute-start | bytes 380936 | tf_op jit(solution)/shard_map/ppermute | solution.py:622
  32.9 3.8 %collective-permute-start.6 = (f32[32,128]{1,0:T(8,128)S(1)}, f32[32,128]{1,0:T(8,128)S(1)}, u32[]{:S(2)}, u32[]{:S(2)}) collective-permute-start(f32[32,128]{1,0:T(8,128)S(1)} %get-tuple-element.20.shares_0_), channel_id=1, source_target_pairs={{0,16},{8,24},{16,0},{24,8},{1,17},{9,25},{17,1},{25,9},{2,18},{10... | collective-permute-start | bytes 49160 | tf_op jit(solution)/shard_map/ppermute | solution.py:624

commit v5 on v4

--- a/solution.py
+++ b/solution.py
@@ -11,6 +11,7 @@
 SEGMENT_COEF = (0.25, 1.0 / 3.0, 0.5, 1.0)
 DISSIP = 0.2
 W = 4
+SHARE = 8
 HIGH = lax.Precision.HIGHEST
 VMEM = pl.BlockSpec(memory_space=pltpu.VMEM)
 SMEM = pl.BlockSpec(memory_space=pltpu.SMEM)
@@ -254,29 +255,31 @@
 
 
 def step_kernel(
-    dims, jac, harm, blade, shares, _, from_left, from_right, new, res, ext, new_v, res_v, q_a, q_b, p_0, p_a, p_b, edge, coef, sem
+    dims, jac, harm, blade, shares, _, from_left, from_right, new, res, ext, new_v, res_v, q_a, q_b, p_0, p_a, p_b, edge, coef, matrix, sem
 ):
     nv, sl, al, cl, br, nb, ng, nh = (dims[k] for k in ("nv", "sl", "al", "cl", "br", "nb", "ng", "nh"))
     axial = lax.axis_index("axial")
     span = lax.axis_index("span")
     circ = lax.axis_index("circ")
     spare = (W - 1) * al
-    parts = 4 if sl % 8 == 0 else 1
-    blocks_of = -(-3 * nv // 16) * 16
-    lane = lax.broadcasted_iota(jnp.int32, (8, 8 * blocks_of), 1)
-    row = lax.broadcasted_iota(jnp.int32, (8, 8 * blocks_of), 0)
-    matrix = []
+    chunks = 4 if sl % 8 == 0 else 1
+    lane = lax.broadcasted_iota(jnp.int32, (8, 8 * SHARE), 1)
+    row = lax.broadcasted_iota(jnp.int32, (8, 8 * SHARE), 0)
+    parts = []
     for u in range(nv):
-        part = jnp.zeros((8, 8 * blocks_of), jnp.float32)
-        for d in range(3):
-            for v in range(nv):
-                value = (jac[d, u, v] * 0.5 - (DISSIP if u == v else 0.0)) * (0.5 / DISSIP)
-                part = jnp.where(lane == row + 8 * (d * nv + v), value, part)
-        matrix.append(part)
-    matrix = jnp.concatenate(matrix, axis=0)
-    high = matrix.astype(jnp.bfloat16).astype(jnp.float32)
-    again = jnp.concatenate([matrix - high, jnp.zeros_like(high)], axis=1)
-    coef[...] = jnp.concatenate([jnp.concatenate([high, high], axis=1), again], axis=0).astype(jnp.bfloat16)
+        part = jnp.zeros((8, 8 * SHARE), jnp.float32)
+        for k in range(3 * nv):
+            d, v = 2 - k // nv if k // nv != 1 else 1, k % nv
+            value = (jac[d, u, v] * 0.5 - (DISSIP if u == v else 0.0)) * (0.5 / DISSIP)
+            if k < SHARE:
+                part = jnp.where(lane == row + 8 * k, value, part)
+            else:
+                coef[u * 3 * nv + k] = jnp.full((8, 128), value, jnp.float32)
+        parts.append(part)
+    parts = jnp.concatenate(parts, axis=0)
+    high = parts.astype(jnp.bfloat16).astype(jnp.float32)
+    again = jnp.concatenate([parts - high, jnp.zeros_like(high)], axis=1)
+    matrix[...] = jnp.concatenate([jnp.concatenate([high, high], axis=1), again], axis=0).astype(jnp.bfloat16)
 
     half = (nv + 1) // 2
     low = lane_ids(ng * br) % 8 < 4
@@ -325,24 +328,34 @@
     last = (ng + 1) * br
 
     def apply(cells):
-        def beside(name):
-            return [jnp.concatenate(parts, axis=1) for parts in zip(*(c[name] for c in cells))]
-
-        both = {name: beside(name) for name in cells[0] if name[-1] in "+-q"}
-        diff = [p - m for d in ("axial", "span", "theta") for p, m in zip(both[d + "+"], both[d + "-"])]
-        diff += [jnp.zeros_like(diff[0])] * (blocks_of - len(diff))
-        diff = jnp.concatenate(diff, axis=0)
+        n = range(len(cells))
+        for c in cells:
+            c["diff"] = [p - m for d in ("theta", "span", "axial") for p, m in zip(c[d + "+"], c[d + "-"])]
+        diff = jnp.concatenate(
+            [jnp.concatenate([c["diff"][k] for c in cells], axis=1) for k in range(SHARE)], axis=0
+        )
         high = diff.astype(jnp.bfloat16)
         low = (diff - high.astype(jnp.float32)).astype(jnp.bfloat16)
         product = jnp.dot(
-            coef[...], jnp.concatenate([high, low], axis=0), preferred_element_type=jnp.float32
+            matrix[...], jnp.concatenate([high, low], axis=0), preferred_element_type=jnp.float32
         )
         out = [[None] * nv for _ in cells]
         for u in range(nv):
-            rest = 3.0 * both["q"][u] - (both["axial-"][u] + both["span-"][u] + both["theta-"][u])
-            total = product[8 * u : 8 * u + 8] + (product[8 * (nv + u) : 8 * (nv + u) + 8] + rest)
-            for i in range(len(cells)):
-                out[i][u] = total[:, 128 * i : 128 * i + 128]
+            odd = even = None
+            for k in range(SHARE, 3 * nv):
+                value = coef[u * 3 * nv + k]
+                terms = [value * c["diff"][k] for c in cells]
+                if (k - SHARE) % 2:
+                    odd = [x + y for x, y in zip(odd, terms)] if odd else terms
+                else:
+                    even = [x + y for x, y in zip(even, terms)] if even else terms
+            for i, c in enumerate(cells):
+                lanes = slice(128 * i, 128 * i + 128)
+                rest = 3.0 * c["q"][u] - (c["axial-"][u] + c["span-"][u] + c["theta-"][u])
+                total = (odd[i] + even[i]) + rest
+                out[i][u] = (
+                    product[8 * u : 8 * u + 8, lanes] + product[8 * (nv + u) : 8 * (nv + u) + 8, lanes]
+                ) + total
         return out
 
     turns = al // 8
@@ -444,9 +457,9 @@
                 blocks(start + count - 1, 1, first)
 
         if final:
-            for i in range(parts):
-                run(W + i * (sl // parts), sl // parts, 1)
-                rows = pl.ds(i * (sl // parts) * al, sl // parts * al)
+            for i in range(chunks):
+                run(W + i * (sl // chunks), sl // chunks, 1)
+                rows = pl.ds(i * (sl // chunks) * al, sl // chunks * al)
                 copy = pltpu.make_async_copy(new_v.at[:, rows, :], new.at[:, rows, :], sem.at[i + 1])
                 copy.start()
                 writes.append(copy)
@@ -641,7 +654,8 @@
             strips,
             strips,
             pltpu.VMEM((nv, ng * br, 128), f32),
-            pltpu.VMEM((16 * nv, 16 * (-(-3 * nv // 16) * 16)), jnp.bfloat16),
+            pltpu.VMEM((3 * nv * nv, 8, 128), f32),
+            pltpu.VMEM((16 * nv, 16 * SHARE), jnp.bfloat16),
             pltpu.SemaphoreType.DMA((5,)),
         ],
         compiler_params=params,

time: 71 us -> 70.5 us (level)
  no operation moved by 1% of the time
where the time goes in v5:
time: 70.5 us; the launch traced here: 70.2 us
  Pallas kernels  38 us (54%)
  starting transfers between devices  16.4 us (23%)
  waiting for transfers between devices  12.5 us (18%)
  local copies, waits for them, and re-layouts  2.04 us (3%)
  between operations  1.43 us (2%)
    pallas_call x1, Pallas kernels, local(): pl.pallas_call(functools.partial(step_kernel, dims), out_shape=[block, bl...  33.6 us
    ppermute x1, waiting for transfers between devices, local(): above = lax.ppermute(down, 'span', shift_pairs(n_span, -1, False))  4.4 us
    ppermute x1, starting transfers between devices, local(): lax.ppermute(part, ('span', 'axial'), shift_pairs(n_span * n_axial, 1, Fa...  3.98 us
    ppermute x1, waiting for transfers between devices, local(): shares = [share, lax.ppermute(share, 'circ', shift_pairs(n_circ, 2, True))]  3.4 us
    ppermute x2, waiting for transfers between devices, axial_move(): moved = lax.ppermute(faces[0], 'axial', [(0, 1), (1, 0)])  3.38 us
    ppermute x1, starting transfers between devices, local(): below = lax.ppermute(up, 'span', shift_pairs(n_span, 1, False))  3.37 us
    pallas_call x1, Pallas kernels, local(): pl.pallas_call(functools.partial(axial_kernel, dims), out_shape=[jax.Shap...  2.21 us
    ppermute x1, starting transfers between devices, local(): from_right = lax.ppermute(left, 'circ', shift_pairs(n_circ, -1, True))  2.09 us
  transfers between devices with their start and end apart: 9, of which 4 were waited for; matrix products, arithmetic and copies ran while one was open for 0% of the time, Pallas kernels for 1%

profile of v5, /device:TPU:1, one launch (start us, length us, event | category | flops | bytes accessed | tf_op | source)
XLA Modules:
  0.0 70.2 jit_solution(1474720303346329959)
XLA Ops:
  0.6 0.0 copy-start.1
  0.6 0.0 copy-start.5
  0.7 0.0 copy-start.6
  1.3 2.2 %axial_faces.1 = (f32[1,6,4,8,128]{4,3,2,1,0:T(8,128)}, f32[1,6,4,24,128]{4,3,2,1,0:T(8,128)}, f32[16,128]{1,0:T(8,128)}) custom-call(f32[5,32,16,128]{3,2,1,0:T(8,128)} %state.1, f32[32,16,128]{2,1,0:T(8,128)} %dt.1, f32[5,8,128]{2,1,0:T(8,128)} %rotor.1, s32[1]{0:T(128)S(6)} %copy.13.blade, s32[8]{0:T(128)} %harm.3), custom_call_target="tpu_custom_call" | custom-call | tf_op jit(solution)/shard_map/axial_faces/pallas_call | solution.py:544
  3.6 4.0 %collective-permute-start.3 = (f32[16,128]{1,0:T(8,128)}, f32[16,128]{1,0:T(8,128)S(1)}, u32[]{:S(2)}, u32[]{:S(2)}) collective-permute-start(f32[16,128]{1,0:T(8,128)} %get-tuple-element.16.part), channel_id=1, source_target_pairs={{0,1},{1,2},{2,3},{3,4},{4,5},{5,6},{6,7},{8,9},{9,10},{10,11},{11... | collective-permute-start | bytes 24584 | tf_op jit(solution)/shard_map/ppermute | solution.py:578
  7.6 1.8 %collective-permute-start.2 = (f32[16,128]{1,0:T(8,128)}, f32[16,128]{1,0:T(8,128)S(1)}, u32[]{:S(2)}, u32[]{:S(2)}) collective-permute-start(f32[16,128]{1,0:T(8,128)} %get-tuple-element.16.part), channel_id=1, source_target_pairs={{0,1},{1,0},{2,3},{3,2},{4,5},{5,4},{6,7},{7,6},{8,9},{9,8},{10,11... | collective-permute-start | bytes 24584 | tf_op jit(solution)/shard_map/ppermute | solution.py:577
  9.4 0.1 collective-permute-start
  9.4 1.4 %collective-permute-start.1 = (f32[6,4,24,128]{3,2,1,0:T(8,128)}, f32[6,4,24,128]{3,2,1,0:T(8,128)S(1)}, u32[]{:S(2)}, u32[]{:S(2)}) collective-permute-start(f32[6,4,24,128]{3,2,1,0:T(8,128)} %bitcast.18), channel_id=1, source_target_pairs={{0,1},{1,0},{2,3},{3,2},{4,5},{5,4},{6,7},{7,6},{8,9},{9,8},{10,11... | collective-permute-start | bytes 884744 | tf_op jit(solution)/shard_map/ppermute | solution.py:569
  10.8 0.0 copy-done.5
  10.8 0.0 copy-done.6
  10.8 0.0 collective-permute-done.3.before
  10.9 0.0 collective-permute-done.2.other
  10.9 3.4 %collective-permute-done.lo.hi.lo_edge.hi_edge = f32[6,4,8,128]{3,2,1,0:T(8,128)S(1)} collective-permute-done((f32[6,4,8,128]{3,2,1,0:T(8,128)}, f32[6,4,8,128]{3,2,1,0:T(8,128)S(1)}, u32[]{:S(2)}, u32[]{:S(2)}) %collective-permute-start) | collective-permute-done | bytes 98336 | tf_op jit(solution)/shard_map/ppermute | solution.py:569
  14.2 0.0 copy-done.1
  14.2 0.0 copy-start
  14.2 1.3 %copy-done = f32[5,32,16,128]{3,2,1,0:T(8,128)S(1)} copy-done((f32[5,32,16,128]{3,2,1,0:T(8,128)S(1)}, f32[5,32,16,128]{3,2,1,0:T(8,128)}, u32[]{:S(2)}) %copy-start) | copy-done | bytes 1310744
  15.6 0.0 copy-start.2
  15.6 0.7 copy-done.2
  16.3 0.5 span_faces.1
  16.8 3.4 %collective-permute-start.4 = (f32[496,128]{1,0:T(8,128)S(1)}, f32[496,128]{1,0:T(8,128)S(1)}, u32[]{:S(2)}, u32[]{:S(2)}) collective-permute-start(f32[496,128]{1,0:T(8,128)S(1)} %get-tuple-element.17), channel_id=1, source_target_pairs={{0,2},{2,4},{4,6},{1,3},{3,5},{5,7},{8,10},{10,12},{12,14},{9,11},... | collective-permute-start | bytes 761864 | tf_op jit(solution)/shard_map/ppermute | solution.py:616
  20.1 1.9 %collective-permute-start.5 = (f32[496,128]{1,0:T(8,128)S(1)}, f32[496,128]{1,0:T(8,128)S(1)}, u32[]{:S(2)}, u32[]{:S(2)}) collective-permute-start(f32[496,128]{1,0:T(8,128)S(1)} %get-tuple-element.18), channel_id=1, source_target_pairs={{2,0},{4,2},{6,4},{3,1},{5,3},{7,5},{10,8},{12,10},{14,12},{11,9},... | collective-permute-start | bytes 761864 | tf_op jit(solution)/shard_map/ppermute | solution.py:617
  22.1 0.0 collective-permute-done.1.lo.hi
  22.1 1.3 %collective-permute-done.4.below = f32[496,128]{1,0:T(8,128)S(1)} collective-permute-done((f32[496,128]{1,0:T(8,128)S(1)}, f32[496,128]{1,0:T(8,128)S(1)}, u32[]{:S(2)}, u32[]{:S(2)}) %collective-permute-start.4) | collective-permute-done | bytes 253984 | tf_op jit(solution)/shard_map/ppermute | solution.py:616
  23.3 4.4 %collective-permute-done.5.above = f32[496,128]{1,0:T(8,128)S(1)} collective-permute-done((f32[496,128]{1,0:T(8,128)S(1)}, f32[496,128]{1,0:T(8,128)S(1)}, u32[]{:S(2)}, u32[]{:S(2)}) %collective-permute-start.5) | collective-permute-done | bytes 253984 | tf_op jit(solution)/shard_map/ppermute | solution.py:617
  27.7 0.0 copy-start.4
  27.7 0.0 copy-start.3
  27.7 1.7 %circ_faces.1 = (f32[6,960,128]{2,1,0:T(8,128)S(1)}, f32[248,128]{1,0:T(8,128)S(1)}, f32[248,128]{1,0:T(8,128)S(1)}, f32[32,128]{1,0:T(8,128)S(1)}) custom-call(f32[5,512,128]{2,1,0:T(8,128)S(1)} %bitcast.12, f32[512,128]{1,0:T(8,128)S(1)} %bitcast.15, f32[6,4,8,128]{3,2,1,0:T(8,128)S(1)} %collective-permute-done.lo.hi.lo_edge.hi_edge, ...), custom_call_target="tpu_custom_call" | custom-call | tf_op jit(solution)/shard_map/circ_faces/pallas_call | solution.py:620
  29.4 1.3 %collective-permute-start.7 = (f32[248,128]{1,0:T(8,128)S(1)}, f32[248,128]{1,0:T(8,128)S(1)}, u32[]{:S(2)}, u32[]{:S(2)}) collective-permute-start(f32[248,128]{1,0:T(8,128)S(1)} %get-tuple-element.22), channel_id=1, source_target_pairs={{0,8},{8,16},{16,24},{24,0},{1,9},{9,17},{17,25},{25,1},{2,10},{10... | collective-permute-start | bytes 380936 | tf_op jit(solution)/shard_map/ppermute | solution.py:634
  30.8 2.1 %collective-permute-start.8 = (f32[248,128]{1,0:T(8,128)S(1)}, f32[248,128]{1,0:T(8,128)S(1)}, u32[]{:S(2)}, u32[]{:S(2)}) collective-permute-start(f32[248,128]{1,0:T(8,128)S(1)} %get-tuple-element.23), channel_id=1, source_target_pairs={{0,24},{8,0},{16,8},{24,16},{1,25},{9,1},{17,9},{25,17},{2,26},{10... | collective-permute-start | bytes 380936 | tf_op jit(solution)/shard_map/ppermute | solution.py:635
  32.9 0.4 collective-permute-start.6
  33.3 0.0 copy-done.4
  33.3 3.4 %collective-permute-done.6.shares_1_ = f32[32,128]{1,0:T(8,128)S(1)} collective-permute-done((f32[32,128]{1,0:T(8,128)S(1)}, f32[32,128]{1,0:T(8,128)S(1)}, u32[]{:S(2)}, u32[]{:S(2)}) %collective-permute-start.6) | collective-permute-done | bytes 16416 | tf_op jit(solution)/shard_map/ppermute | solution.py:637
  36.7 0.0 collective-permute-done.7.from_left
  36.7 0.0 collective-permute-done.8.from_right
  36.7 0.0 copy-done.3
  36.7 33.6 %segments.1 = (f32[5,512,128]{2,1,0:T(8,128)}, f32[5,512,128]{2,1,0:T(8,128)}, f32[6,960,128]{2,1,0:T(8,128)S(1)}) custom-call(f32[3,5,5]{2,1,0:T(8,128)S(1)} %copy.11.jac, s32[8]{0:T(128)S(1)} %copy-done.3, s32[1]{0:T(128)S(6)} %copy.13.blade, f32[32,128]{1,0:T(8,128)S(1)} %get-tuple-element.20.shares_0_, ...), custom_call_target="tpu_custom_call", output_to_operand_aliasing={{2}: (5, {})} | custom-call | tf_op jit(solution)/shard_map/segments/pallas_call | solution.py:642
  (3 shorter events, 0.0 us)
Async XLA Ops:
  0.6 13.6 %copy-start.1 = (f32[32,16,128]{2,1,0:T(8,128)S(1)}, f32[32,16,128]{2,1,0:T(8,128)}, u32[]{:S(2)}) copy-start(f32[32,16,128]{2,1,0:T(8,128)} %dt.1) | copy-start | bytes 786436
  0.6 10.2 %copy-start.5 = (s32[32]{0:T(128)S(1)}, s32[32]{0:T(128)}, u32[]{:S(2)}) copy-start(s32[32]{0:T(128)} %param.11) | copy-start | bytes 388
  0.7 10.2 %copy-start.6 = (f32[32]{0:T(128)S(1)}, f32[32]{0:T(128)}, u32[]{:S(2)}) copy-start(f32[32]{0:T(128)} %param.12) | copy-start | bytes 388
  3.6 7.3 %collective-permute-start.3 = (f32[16,128]{1,0:T(8,128)}, f32[16,128]{1,0:T(8,128)S(1)}, u32[]{:S(2)}, u32[]{:S(2)}) collective-permute-start(f32[16,128]{1,0:T(8,128)} %get-tuple-element.16.part), channel_id=1, source_target_pairs={{0,1},{1,2},{2,3},{3,4},{4,5},{5,6},{6,7},{8,9},{9,10},{10,11},{11... | collective-permute-start | bytes 24584 | tf_op jit(solution)/shard_map/ppermute | solution.py:578
  7.6 3.3 %collective-permute-start.2 = (f32[16,128]{1,0:T(8,128)}, f32[16,128]{1,0:T(8,128)S(1)}, u32[]{:S(2)}, u32[]{:S(2)}) collective-permute-start(f32[16,128]{1,0:T(8,128)} %get-tuple-element.16.part), channel_id=1, source_target_pairs={{0,1},{1,0},{2,3},{3,2},{4,5},{5,4},{6,7},{7,6},{8,9},{9,8},{10,11... | collective-permute-start | bytes 24584 | tf_op jit(solution)/shard_map/ppermute | solution.py:577
  9.4 4.9 %collective-permute-start = (f32[6,4,8,128]{3,2,1,0:T(8,128)}, f32[6,4,8,128]{3,2,1,0:T(8,128)S(1)}, u32[]{:S(2)}, u32[]{:S(2)}) collective-permute-start(f32[6,4,8,128]{3,2,1,0:T(8,128)} %bitcast.19), channel_id=1, source_target_pairs={{0,1},{1,0},{2,3},{3,2},{4,5},{5,4},{6,7},{7,6},{8,9},{9,8},{10,11... | collective-permute-start | bytes 294920 | tf_op jit(solution)/shard_map/ppermute | solution.py:569
  9.4 12.6 %collective-permute-start.1 = (f32[6,4,24,128]{3,2,1,0:T(8,128)}, f32[6,4,24,128]{3,2,1,0:T(8,128)S(1)}, u32[]{:S(2)}, u32[]{:S(2)}) collective-permute-start(f32[6,4,24,128]{3,2,1,0:T(8,128)} %bitcast.18), channel_id=1, source_target_pairs={{0,1},{1,0},{2,3},{3,2},{4,5},{5,4},{6,7},{7,6},{8,9},{9,8},{10,11... | collective-permute-start | bytes 884744 | tf_op jit(solution)/shard_map/ppermute | solution.py:569
  14.2 1.3 %copy-start = (f32[5,32,16,128]{3,2,1,0:T(8,128)S(1)}, f32[5,32,16,128]{3,2,1,0:T(8,128)}, u32[]{:S(2)}) copy-start(f32[5,32,16,128]{3,2,1,0:T(8,128)} %state.1) | copy-start | bytes 3932164
  15.6 0.7 copy-start.2
  16.8 6.6 %collective-permute-start.4 = (f32[496,128]{1,0:T(8,128)S(1)}, f32[496,128]{1,0:T(8,128)S(1)}, u32[]{:S(2)}, u32[]{:S(2)}) collective-permute-start(f32[496,128]{1,0:T(8,128)S(1)} %get-tuple-element.17), channel_id=1, source_target_pairs={{0,2},{2,4},{4,6},{1,3},{3,5},{5,7},{8,10},{10,12},{12,14},{9,11},... | collective-permute-start | bytes 761864 | tf_op jit(solution)/shard_map/ppermute | solution.py:616
  20.1 7.6 %collective-permute-start.5 = (f32[496,128]{1,0:T(8,128)S(1)}, f32[496,128]{1,0:T(8,128)S(1)}, u32[]{:S(2)}, u32[]{:S(2)}) collective-permute-start(f32[496,128]{1,0:T(8,128)S(1)} %get-tuple-element.18), channel_id=1, source_target_pairs={{2,0},{4,2},{6,4},{3,1},{5,3},{7,5},{10,8},{12,10},{14,12},{11,9},... | collective-permute-start | bytes 761864 | tf_op jit(solution)/shard_map/ppermute | solution.py:617
  27.7 5.5 %copy-start.4 = (f32[3,5,5]{2,0,1:T(4,128)S(1)}, f32[3,5,5]{2,0,1:T(4,128)}, u32[]{:S(2)}) copy-start(f32[3,5,5]{2,0,1:T(4,128)} %param.15) | copy-start | bytes 904
  27.7 8.9 %copy-start.3 = (s32[8]{0:T(128)S(1)}, s32[8]{0:T(128)}, u32[]{:S(2)}) copy-start(s32[8]{0:T(128)} %harm.3) | copy-start | bytes 100
  29.4 7.2 %collective-permute-start.7 = (f32[248,128]{1,0:T(8,128)S(1)}, f32[248,128]{1,0:T(8,128)S(1)}, u32[]{:S(2)}, u32[]{:S(2)}) collective-permute-start(f32[248,128]{1,0:T(8,128)S(1)} %get-tuple-element.22), channel_id=1, source_target_pairs={{0,8},{8,16},{16,24},{24,0},{1,9},{9,17},{17,25},{25,1},{2,10},{10... | collective-permute-start | bytes 380936 | tf_op jit(solution)/shard_map/ppermute | solution.py:634
  30.8 5.9 %collective-permute-start.8 = (f32[248,128]{1,0:T(8,128)S(1)}, f32[248,128]{1,0:T(8,128)S(1)}, u32[]{:S(2)}, u32[]{:S(2)}) collective-permute-start(f32[248,128]{1,0:T(8,128)S(1)} %get-tuple-element.23), channel_id=1, source_target_pairs={{0,24},{8,0},{16,8},{24,16},{1,25},{9,1},{17,9},{25,17},{2,26},{10... | collective-permute-start | bytes 380936 | tf_op jit(solution)/shard_map/ppermute | solution.py:635
  32.9 3.8 %collective-permute-start.6 = (f32[32,128]{1,0:T(8,128)S(1)}, f32[32,128]{1,0:T(8,128)S(1)}, u32[]{:S(2)}, u32[]{:S(2)}) collective-permute-start(f32[32,128]{1,0:T(8,128)S(1)} %get-tuple-element.20.shares_0_), channel_id=1, source_target_pairs={{0,16},{8,24},{16,0},{24,8},{1,17},{9,25},{17,1},{25,9},{2,18},{10... | collective-permute-start | bytes 49160 | tf_op jit(solution)/shard_map/ppermute | solution.py:637

commit v6 on v3

--- a/solution.py
+++ b/solution.py
@@ -265,7 +265,7 @@
     for d in range(3):
         for u in range(nv):
             for v in range(nv):
-                value = jac[d, u, v] * 0.5 - (DISSIP if u == v else 0.0)
+                value = (jac[d, u, v] * 0.5 - (DISSIP if u == v else 0.0)) * (0.5 / DISSIP)
                 coef[(d * nv + u) * nv + v] = jnp.full((8, 128), value, jnp.float32)
 
     half = (nv + 1) // 2
@@ -315,29 +315,19 @@
     last = (ng + 1) * br
 
     def apply(cells):
-        for c in cells:
-            c["diff"] = [
-                [plus - minus for plus, minus in zip(c[d + "+"], c[d + "-"])] for d in ("axial", "span", "theta")
-            ]
-            c["rest"] = [
-                (2.0 * DISSIP) * (3.0 * q - (x + y + z))
-                for q, x, y, z in zip(c["q"], c["axial-"], c["span-"], c["theta-"])
-            ]
-        out = [[None] * nv for _ in cells]
-        for first in range(0, nv, 2):
-            some = range(first, min(first + 2, nv))
-            sums = {}
+        sums = [[3.0 * q for q in c["q"]] for c in cells]
+        for d, name in enumerate(("axial", "span", "theta")):
+            diff = []
+            for c, total in zip(cells, sums):
+                diff.append([p - m for p, m in zip(c[name + "+"], c[name + "-"])])
+                for u in range(nv):
+                    total[u] = total[u] - c[name + "-"][u]
             for v in range(nv):
-                for d in range(3):
-                    for u in some:
-                        k = coef[(d * nv + u) * nv + v]
-                        for i, c in enumerate(cells):
-                            term = k * c["diff"][d][v]
-                            sums[i, u, d] = sums[i, u, d] + term if v else term
-            for u in some:
-                for i, c in enumerate(cells):
-                    out[i][u] = (sums[i, u, 0] + sums[i, u, 1]) + (sums[i, u, 2] + c["rest"][u])
-        return out
+                for u in range(nv):
+                    k = coef[(d * nv + u) * nv + v]
+                    for i in range(len(cells)):
+                        sums[i][u] = sums[i][u] + k * diff[i][v]
+        return sums
 
     turns = al // 8
     sub = lax.broadcasted_iota(jnp.int32, (8, 128), 0)
@@ -391,7 +381,7 @@
             around = pl.multiple_of((b - 1) * br, 8)
             view = src.at[:, pl.ds(around, (count + 2) * br), :]
             values = [block_cells(view, (i + 1) * br) for i in range(count)]
-            groups = [[(i, t) for t in range(1, turns + 1)] for i in range(count)]
+            groups = [[(i, t) for i in range(count) for t in range(1, turns + 1)]]
             if first == 0:
                 groups.append([(i, 0) for i in range(count)])
 
@@ -406,7 +396,7 @@
                     beyond = [pltpu.roll(p_src[v, pl.ds(p_row, 8), :], 124 - 8 * r, 1) for v in range(nv)]
                     turn(cell, beyond, first_lane, last_lane)
                     cell["base"] = [ext[u, pl.ds(row, 8), :] for u in range(nv)] if number else cell["q"]
-                    cell["step"] = factor * ext[nv, pl.ds(row, 8), :]
+                    cell["step"] = (2.0 * DISSIP * factor) * ext[nv, pl.ds(row, 8), :]
                     cells.append(cell)
                 return cells
 
@@ -425,7 +415,7 @@
                             dst[u, pl.ds(row, 8), :] = value
                             if t > 0 and number == 0:
                                 rows = pl.ds(pl.multiple_of((b + i - 1) * al, 8) + t - 1, 8, stride=turns)
-                                res_v[u, rows, :] = result[u]
+                                res_v[u, rows, :] = (2.0 * DISSIP) * result[u]
                 cells = following
 
         def run(start, count, first):
@@ -470,7 +460,7 @@
                 cell = values(t)
                 turn(cell, [edge[v, pl.ds(around + 8 * t, 8), :] for v in range(nv)], pos4, pos3)
                 (result,) = apply([cell])
-                step = factor * p_0[nv, pl.ds(base + 8 * t, 8), :]
+                step = (2.0 * DISSIP * factor) * p_0[nv, pl.ds(base + 8 * t, 8), :]
                 for u in range(nv):
                     p_dst[u, pl.ds(base + 8 * t, 8), :] = p_0[u, pl.ds(base + 8 * t, 8), :] - step * result[u]
             return carry

time: 62.9 us -> 61.1 us (0.971)
  Pallas kernels: 30.3 us -> 28.5 us
    pallas_call x1, Pallas kernels: 25.9 us -> 24.1 us  [local(): pl.pallas_call(functools.partial(step_kernel, dims), out_shape=[block, bl...]
where the time goes in v6:
time: 61.1 us; the launch traced here: 60.8 us
  Pallas kernels  28.5 us (47%)
  starting transfers between devices  16.4 us (27%)
  waiting for transfers between devices  12.5 us (20%)
  local copies, waits for them, and re-layouts  2.04 us (3%)
  between operations  1.43 us (2%)
    pallas_call x1, Pallas kernels, local(): pl.pallas_call(functools.partial(step_kernel, dims), out_shape=[block, bl...  24.1 us
    ppermute x1, waiting for transfers between devices, local(): above = lax.ppermute(down, 'span', shift_pairs(n_span, -1, False))  4.4 us
    ppermute x1, starting transfers between devices, local(): lax.ppermute(part, ('span', 'axial'), shift_pairs(n_span * n_axial, 1, Fa...  3.98 us
    ppermute x1, waiting for transfers between devices, local(): shares = [share, lax.ppermute(share, 'circ', shift_pairs(n_circ, 2, True))]  3.4 us
    ppermute x2, waiting for transfers between devices, axial_move(): moved = lax.ppermute(faces[0], 'axial', [(0, 1), (1, 0)])  3.38 us
    ppermute x1, starting transfers between devices, local(): below = lax.ppermute(up, 'span', shift_pairs(n_span, 1, False))  3.37 us
    pallas_call x1, Pallas kernels, local(): pl.pallas_call(functools.partial(axial_kernel, dims), out_shape=[jax.Shap...  2.21 us
    ppermute x1, starting transfers between devices, local(): from_right = lax.ppermute(left, 'circ', shift_pairs(n_circ, -1, True))  2.09 us
  transfers between devices with their start and end apart: 9, of which 4 were waited for; matrix products, arithmetic and copies ran while one was open for 0% of the time, Pallas kernels for 1%

profile of v6, /device:TPU:1, one launch (start us, length us, event | category | flops | bytes accessed | tf_op | source)
XLA Modules:
  0.0 60.8 jit_solution(5595455150511455346)
XLA Ops:
  0.6 0.0 copy-start.1
  0.6 0.0 copy-start.5
  0.7 0.0 copy-start.6
  1.3 2.2 %axial_faces.1 = (f32[1,6,4,8,128]{4,3,2,1,0:T(8,128)}, f32[1,6,4,24,128]{4,3,2,1,0:T(8,128)}, f32[16,128]{1,0:T(8,128)}) custom-call(f32[5,32,16,128]{3,2,1,0:T(8,128)} %state.1, f32[32,16,128]{2,1,0:T(8,128)} %dt.1, f32[5,8,128]{2,1,0:T(8,128)} %rotor.1, s32[1]{0:T(128)S(6)} %copy.13.blade, s32[8]{0:T(128)} %harm.3), custom_call_target="tpu_custom_call" | custom-call | tf_op jit(solution)/shard_map/axial_faces/pallas_call | solution.py:515
  3.6 4.0 %collective-permute-start.3 = (f32[16,128]{1,0:T(8,128)}, f32[16,128]{1,0:T(8,128)S(1)}, u32[]{:S(2)}, u32[]{:S(2)}) collective-permute-start(f32[16,128]{1,0:T(8,128)} %get-tuple-element.16.part), channel_id=1, source_target_pairs={{0,1},{1,2},{2,3},{3,4},{4,5},{5,6},{6,7},{8,9},{9,10},{10,11},{11... | collective-permute-start | bytes 24584 | tf_op jit(solution)/shard_map/ppermute | solution.py:549
  7.6 1.8 %collective-permute-start.2 = (f32[16,128]{1,0:T(8,128)}, f32[16,128]{1,0:T(8,128)S(1)}, u32[]{:S(2)}, u32[]{:S(2)}) collective-permute-start(f32[16,128]{1,0:T(8,128)} %get-tuple-element.16.part), channel_id=1, source_target_pairs={{0,1},{1,0},{2,3},{3,2},{4,5},{5,4},{6,7},{7,6},{8,9},{9,8},{10,11... | collective-permute-start | bytes 24584 | tf_op jit(solution)/shard_map/ppermute | solution.py:548
  9.4 0.1 collective-permute-start
  9.4 1.4 %collective-permute-start.1 = (f32[6,4,24,128]{3,2,1,0:T(8,128)}, f32[6,4,24,128]{3,2,1,0:T(8,128)S(1)}, u32[]{:S(2)}, u32[]{:S(2)}) collective-permute-start(f32[6,4,24,128]{3,2,1,0:T(8,128)} %bitcast.18), channel_id=1, source_target_pairs={{0,1},{1,0},{2,3},{3,2},{4,5},{5,4},{6,7},{7,6},{8,9},{9,8},{10,11... | collective-permute-start | bytes 884744 | tf_op jit(solution)/shard_map/ppermute | solution.py:540
  10.8 0.0 copy-done.5
  10.8 0.0 copy-done.6
  10.8 0.0 collective-permute-done.3.before
  10.9 0.0 collective-permute-done.2.other
  10.9 3.4 %collective-permute-done.lo.hi.lo_edge.hi_edge = f32[6,4,8,128]{3,2,1,0:T(8,128)S(1)} collective-permute-done((f32[6,4,8,128]{3,2,1,0:T(8,128)}, f32[6,4,8,128]{3,2,1,0:T(8,128)S(1)}, u32[]{:S(2)}, u32[]{:S(2)}) %collective-permute-start) | collective-permute-done | bytes 98336 | tf_op jit(solution)/shard_map/ppermute | solution.py:540
  14.2 0.0 copy-done.1
  14.2 0.0 copy-start
  14.2 1.3 %copy-done = f32[5,32,16,128]{3,2,1,0:T(8,128)S(1)} copy-done((f32[5,32,16,128]{3,2,1,0:T(8,128)S(1)}, f32[5,32,16,128]{3,2,1,0:T(8,128)}, u32[]{:S(2)}) %copy-start) | copy-done | bytes 1310744
  15.6 0.0 copy-start.2
  15.6 0.7 %copy-done.2 = f32[16,128]{1,0:T(8,128)S(1)} copy-done((f32[16,128]{1,0:T(8,128)S(1)}, f32[16,128]{1,0:T(8,128)}, u32[]{:S(2)}) %copy-start.2) | copy-done | bytes 8216
  16.3 0.5 span_faces.1
  16.8 3.4 %collective-permute-start.4 = (f32[496,128]{1,0:T(8,128)S(1)}, f32[496,128]{1,0:T(8,128)S(1)}, u32[]{:S(2)}, u32[]{:S(2)}) collective-permute-start(f32[496,128]{1,0:T(8,128)S(1)} %get-tuple-element.17), channel_id=1, source_target_pairs={{0,2},{2,4},{4,6},{1,3},{3,5},{5,7},{8,10},{10,12},{12,14},{9,11},... | collective-permute-start | bytes 761864 | tf_op jit(solution)/shard_map/ppermute | solution.py:587
  20.1 1.9 %collective-permute-start.5 = (f32[496,128]{1,0:T(8,128)S(1)}, f32[496,128]{1,0:T(8,128)S(1)}, u32[]{:S(2)}, u32[]{:S(2)}) collective-permute-start(f32[496,128]{1,0:T(8,128)S(1)} %get-tuple-element.18), channel_id=1, source_target_pairs={{2,0},{4,2},{6,4},{3,1},{5,3},{7,5},{10,8},{12,10},{14,12},{11,9},... | collective-permute-start | bytes 761864 | tf_op jit(solution)/shard_map/ppermute | solution.py:588
  22.1 0.0 collective-permute-done.1.lo.hi
  22.1 1.3 %collective-permute-done.4.below = f32[496,128]{1,0:T(8,128)S(1)} collective-permute-done((f32[496,128]{1,0:T(8,128)S(1)}, f32[496,128]{1,0:T(8,128)S(1)}, u32[]{:S(2)}, u32[]{:S(2)}) %collective-permute-start.4) | collective-permute-done | bytes 253984 | tf_op jit(solution)/shard_map/ppermute | solution.py:587
  23.3 4.4 %collective-permute-done.5.above = f32[496,128]{1,0:T(8,128)S(1)} collective-permute-done((f32[496,128]{1,0:T(8,128)S(1)}, f32[496,128]{1,0:T(8,128)S(1)}, u32[]{:S(2)}, u32[]{:S(2)}) %collective-permute-start.5) | collective-permute-done | bytes 253984 | tf_op jit(solution)/shard_map/ppermute | solution.py:588
  27.7 0.0 copy-start.4
  27.7 0.0 copy-start.3
  27.7 1.7 %circ_faces.1 = (f32[6,960,128]{2,1,0:T(8,128)S(1)}, f32[248,128]{1,0:T(8,128)S(1)}, f32[248,128]{1,0:T(8,128)S(1)}, f32[32,128]{1,0:T(8,128)S(1)}) custom-call(f32[5,512,128]{2,1,0:T(8,128)S(1)} %bitcast.12, f32[512,128]{1,0:T(8,128)S(1)} %bitcast.15, f32[6,4,8,128]{3,2,1,0:T(8,128)S(1)} %collective-permute-done.lo.hi.lo_edge.hi_edge, ...), custom_call_target="tpu_custom_call" | custom-call | tf_op jit(solution)/shard_map/circ_faces/pallas_call | solution.py:591
  29.4 1.3 %collective-permute-start.7 = (f32[248,128]{1,0:T(8,128)S(1)}, f32[248,128]{1,0:T(8,128)S(1)}, u32[]{:S(2)}, u32[]{:S(2)}) collective-permute-start(f32[248,128]{1,0:T(8,128)S(1)} %get-tuple-element.22), channel_id=1, source_target_pairs={{0,8},{8,16},{16,24},{24,0},{1,9},{9,17},{17,25},{25,1},{2,10},{10... | collective-permute-start | bytes 380936 | tf_op jit(solution)/shard_map/ppermute | solution.py:605
  30.8 2.1 %collective-permute-start.8 = (f32[248,128]{1,0:T(8,128)S(1)}, f32[248,128]{1,0:T(8,128)S(1)}, u32[]{:S(2)}, u32[]{:S(2)}) collective-permute-start(f32[248,128]{1,0:T(8,128)S(1)} %get-tuple-element.23), channel_id=1, source_target_pairs={{0,24},{8,0},{16,8},{24,16},{1,25},{9,1},{17,9},{25,17},{2,26},{10... | collective-permute-start | bytes 380936 | tf_op jit(solution)/shard_map/ppermute | solution.py:606
  32.9 0.4 collective-permute-start.6
  33.3 0.0 copy-done.4
  33.3 3.4 %collective-permute-done.6.shares_1_ = f32[32,128]{1,0:T(8,128)S(1)} collective-permute-done((f32[32,128]{1,0:T(8,128)S(1)}, f32[32,128]{1,0:T(8,128)S(1)}, u32[]{:S(2)}, u32[]{:S(2)}) %collective-permute-start.6) | collective-permute-done | bytes 16416 | tf_op jit(solution)/shard_map/ppermute | solution.py:608
  36.7 0.0 collective-permute-done.7.from_left
  36.7 0.0 collective-permute-done.8.from_right
  36.7 0.0 copy-done.3
  36.7 24.1 %segments.1 = (f32[5,512,128]{2,1,0:T(8,128)}, f32[5,512,128]{2,1,0:T(8,128)}, f32[6,960,128]{2,1,0:T(8,128)S(1)}) custom-call(f32[3,5,5]{2,1,0:T(8,128)S(1)} %copy.11.jac, s32[8]{0:T(128)S(1)} %copy-done.3, s32[1]{0:T(128)S(6)} %copy.13.blade, f32[32,128]{1,0:T(8,128)S(1)} %get-tuple-element.20.shares_0_, ...), custom_call_target="tpu_custom_call", output_to_operand_aliasing={{2}: (5, {})} | custom-call | tf_op jit(solution)/shard_map/segments/pallas_call | solution.py:613
  (3 shorter events, 0.0 us)
Async XLA Ops:
  0.6 13.6 %copy-start.1 = (f32[32,16,128]{2,1,0:T(8,128)S(1)}, f32[32,16,128]{2,1,0:T(8,128)}, u32[]{:S(2)}) copy-start(f32[32,16,128]{2,1,0:T(8,128)} %dt.1) | copy-start | bytes 786436
  0.6 10.2 %copy-start.5 = (s32[32]{0:T(128)S(1)}, s32[32]{0:T(128)}, u32[]{:S(2)}) copy-start(s32[32]{0:T(128)} %param.11) | copy-start | bytes 388
  0.7 10.2 %copy-start.6 = (f32[32]{0:T(128)S(1)}, f32[32]{0:T(128)}, u32[]{:S(2)}) copy-start(f32[32]{0:T(128)} %param.12) | copy-start | bytes 388
  3.6 7.3 %collective-permute-start.3 = (f32[16,128]{1,0:T(8,128)}, f32[16,128]{1,0:T(8,128)S(1)}, u32[]{:S(2)}, u32[]{:S(2)}) collective-permute-start(f32[16,128]{1,0:T(8,128)} %get-tuple-element.16.part), channel_id=1, source_target_pairs={{0,1},{1,2},{2,3},{3,4},{4,5},{5,6},{6,7},{8,9},{9,10},{10,11},{11... | collective-permute-start | bytes 24584 | tf_op jit(solution)/shard_map/ppermute | solution.py:549
  7.6 3.3 %collective-permute-start.2 = (f32[16,128]{1,0:T(8,128)}, f32[16,128]{1,0:T(8,128)S(1)}, u32[]{:S(2)}, u32[]{:S(2)}) collective-permute-start(f32[16,128]{1,0:T(8,128)} %get-tuple-element.16.part), channel_id=1, source_target_pairs={{0,1},{1,0},{2,3},{3,2},{4,5},{5,4},{6,7},{7,6},{8,9},{9,8},{10,11... | collective-permute-start | bytes 24584 | tf_op jit(solution)/shard_map/ppermute | solution.py:548
  9.4 4.9 %collective-permute-start = (f32[6,4,8,128]{3,2,1,0:T(8,128)}, f32[6,4,8,128]{3,2,1,0:T(8,128)S(1)}, u32[]{:S(2)}, u32[]{:S(2)}) collective-permute-start(f32[6,4,8,128]{3,2,1,0:T(8,128)} %bitcast.19), channel_id=1, source_target_pairs={{0,1},{1,0},{2,3},{3,2},{4,5},{5,4},{6,7},{7,6},{8,9},{9,8},{10,11... | collective-permute-start | bytes 294920 | tf_op jit(solution)/shard_map/ppermute | solution.py:540
  9.4 12.6 %collective-permute-start.1 = (f32[6,4,24,128]{3,2,1,0:T(8,128)}, f32[6,4,24,128]{3,2,1,0:T(8,128)S(1)}, u32[]{:S(2)}, u32[]{:S(2)}) collective-permute-start(f32[6,4,24,128]{3,2,1,0:T(8,128)} %bitcast.18), channel_id=1, source_target_pairs={{0,1},{1,0},{2,3},{3,2},{4,5},{5,4},{6,7},{7,6},{8,9},{9,8},{10,11... | collective-permute-start | bytes 884744 | tf_op jit(solution)/shard_map/ppermute | solution.py:540
  14.2 1.3 %copy-start = (f32[5,32,16,128]{3,2,1,0:T(8,128)S(1)}, f32[5,32,16,128]{3,2,1,0:T(8,128)}, u32[]{:S(2)}) copy-start(f32[5,32,16,128]{3,2,1,0:T(8,128)} %state.1) | copy-start | bytes 3932164
  15.6 0.7 %copy-start.2 = (f32[16,128]{1,0:T(8,128)S(1)}, f32[16,128]{1,0:T(8,128)}, u32[]{:S(2)}) copy-start(f32[16,128]{1,0:T(8,128)} %get-tuple-element.16.part) | copy-start | bytes 24580
  16.8 6.6 %collective-permute-start.4 = (f32[496,128]{1,0:T(8,128)S(1)}, f32[496,128]{1,0:T(8,128)S(1)}, u32[]{:S(2)}, u32[]{:S(2)}) collective-permute-start(f32[496,128]{1,0:T(8,128)S(1)} %get-tuple-element.17), channel_id=1, source_target_pairs={{0,2},{2,4},{4,6},{1,3},{3,5},{5,7},{8,10},{10,12},{12,14},{9,11},... | collective-permute-start | bytes 761864 | tf_op jit(solution)/shard_map/ppermute | solution.py:587
  20.1 7.6 %collective-permute-start.5 = (f32[496,128]{1,0:T(8,128)S(1)}, f32[496,128]{1,0:T(8,128)S(1)}, u32[]{:S(2)}, u32[]{:S(2)}) collective-permute-start(f32[496,128]{1,0:T(8,128)S(1)} %get-tuple-element.18), channel_id=1, source_target_pairs={{2,0},{4,2},{6,4},{3,1},{5,3},{7,5},{10,8},{12,10},{14,12},{11,9},... | collective-permute-start | bytes 761864 | tf_op jit(solution)/shard_map/ppermute | solution.py:588
  27.7 5.5 %copy-start.4 = (f32[3,5,5]{2,0,1:T(4,128)S(1)}, f32[3,5,5]{2,0,1:T(4,128)}, u32[]{:S(2)}) copy-start(f32[3,5,5]{2,0,1:T(4,128)} %param.15) | copy-start | bytes 904
  27.7 8.9 %copy-start.3 = (s32[8]{0:T(128)S(1)}, s32[8]{0:T(128)}, u32[]{:S(2)}) copy-start(s32[8]{0:T(128)} %harm.3) | copy-start | bytes 100
  29.4 7.2 %collective-permute-start.7 = (f32[248,128]{1,0:T(8,128)S(1)}, f32[248,128]{1,0:T(8,128)S(1)}, u32[]{:S(2)}, u32[]{:S(2)}) collective-permute-start(f32[248,128]{1,0:T(8,128)S(1)} %get-tuple-element.22), channel_id=1, source_target_pairs={{0,8},{8,16},{16,24},{24,0},{1,9},{9,17},{17,25},{25,1},{2,10},{10... | collective-permute-start | bytes 380936 | tf_op jit(solution)/shard_map/ppermute | solution.py:605
  30.8 5.9 %collective-permute-start.8 = (f32[248,128]{1,0:T(8,128)S(1)}, f32[248,128]{1,0:T(8,128)S(1)}, u32[]{:S(2)}, u32[]{:S(2)}) collective-permute-start(f32[248,128]{1,0:T(8,128)S(1)} %get-tuple-element.23), channel_id=1, source_target_pairs={{0,24},{8,0},{16,8},{24,16},{1,25},{9,1},{17,9},{25,17},{2,26},{10... | collective-permute-start | bytes 380936 | tf_op jit(solution)/shard_map/ppermute | solution.py:606
  32.9 3.8 %collective-permute-start.6 = (f32[32,128]{1,0:T(8,128)S(1)}, f32[32,128]{1,0:T(8,128)S(1)}, u32[]{:S(2)}, u32[]{:S(2)}) collective-permute-start(f32[32,128]{1,0:T(8,128)S(1)} %get-tuple-element.20.shares_0_), channel_id=1, source_target_pairs={{0,16},{8,24},{16,0},{24,8},{1,17},{9,25},{17,1},{25,9},{2,18},{10... | collective-permute-start | bytes 49160 | tf_op jit(solution)/shard_map/ppermute | solution.py:608

commit v7 on v6

--- a/solution.py
+++ b/solution.py
@@ -10,6 +10,7 @@
 
 SEGMENT_COEF = (0.25, 1.0 / 3.0, 0.5, 1.0)
 DISSIP = 0.2
+STEP = 4
 W = 4
 HIGH = lax.Precision.HIGHEST
 VMEM = pl.BlockSpec(memory_space=pltpu.VMEM)
@@ -381,7 +382,9 @@
             around = pl.multiple_of((b - 1) * br, 8)
             view = src.at[:, pl.ds(around, (count + 2) * br), :]
             values = [block_cells(view, (i + 1) * br) for i in range(count)]
-            groups = [[(i, t) for i in range(count) for t in range(1, turns + 1)]]
+            groups = [
+                [(i, t) for i in range(j, min(j + 2, count)) for t in range(1, turns + 1)] for j in range(0, count, 2)
+            ]
             if first == 0:
                 groups.append([(i, 0) for i in range(count)])
 
@@ -420,12 +423,12 @@
 
         def run(start, count, first):
             def loop(j, carry):
-                blocks(start + 2 * j, 2, first)
+                blocks(start + STEP * j, STEP, first)
                 return carry
 
-            lax.fori_loop(0, count // 2, loop, 0)
-            if count % 2:
-                blocks(start + count - 1, 1, first)
+            lax.fori_loop(0, count // STEP, loop, 0)
+            if count % STEP:
+                blocks(start + count // STEP * STEP, count % STEP, first)
 
         if final:
             for i in range(parts):
@@ -544,6 +547,7 @@
         return lo, hi
 
     lo_edge, hi_edge = axial_move(edge)
+    bulk, lo_edge, hi_edge = lax.optimization_barrier((bulk, lo_edge, hi_edge))
     if ride:
         other = lax.ppermute(part, "axial", [(0, 1), (1, 0)])
         before = lax.ppermute(part, ("span", "axial"), shift_pairs(n_span * n_axial, 1, False))

time: 61.1 us -> 60.7 us (level)
  Pallas kernels: 28.5 us -> 27.2 us
  waiting for transfers between devices: 12.5 us -> 13.5 us
    ppermute x2, starting transfers between devices: 1.47 us -> 0.08 us  [axial_move(): moved = lax.ppermute(faces[0], 'axial', [(0, 1), (1, 0)])]
    pallas_call x1, Pallas kernels: 24.1 us -> 22.8 us  [local(): pl.pallas_call(functools.partial(step_kernel, dims), out_shape=[block, bl...]
    ppermute x1, starting transfers between devices: 3.37 us -> 4.56 us  [local(): below = lax.ppermute(up, 'span', shift_pairs(n_span, 1, False))]
    ppermute x2, waiting for transfers between devices: 3.38 us -> 4.46 us  [axial_move(): moved = lax.ppermute(faces[0], 'axial', [(0, 1), (1, 0)])]
where the time goes in v7:
time: 60.7 us; the launch traced here: 60.4 us
  Pallas kernels  27.2 us (45%)
  starting transfers between devices  16.2 us (27%)
  waiting for transfers between devices  13.5 us (22%)
  local copies, waits for them, and re-layouts  2.04 us (3%)
  between operations  1.43 us (2%)
    pallas_call x1, Pallas kernels, local(): pl.pallas_call(functools.partial(step_kernel, dims), out_shape=[block, bl...  22.8 us
    ppermute x1, starting transfers between devices, local(): below = lax.ppermute(up, 'span', shift_pairs(n_span, 1, False))  4.56 us
    ppermute x2, waiting for transfers between devices, axial_move(): moved = lax.ppermute(faces[0], 'axial', [(0, 1), (1, 0)])  4.46 us
    ppermute x1, waiting for transfers between devices, local(): above = lax.ppermute(down, 'span', shift_pairs(n_span, -1, False))  4.4 us
    ppermute x1, starting transfers between devices, local(): lax.ppermute(part, ('span', 'axial'), shift_pairs(n_span * n_axial, 1, Fa...  3.98 us
    ppermute x1, waiting for transfers between devices, local(): shares = [share, lax.ppermute(share, 'circ', shift_pairs(n_circ, 2, True))]  3.4 us
    pallas_call x1, Pallas kernels, local(): pl.pallas_call(functools.partial(axial_kernel, dims), out_shape=[jax.Shap...  2.21 us
    ppermute x1, starting transfers between devices, local(): from_right = lax.ppermute(left, 'circ', shift_pairs(n_circ, -1, True))  2.09 us
  transfers between devices with their start and end apart: 9, of which 4 were waited for; matrix products, arithmetic and copies ran while one was open for 0% of the time, Pallas kernels for 1%

profile of v7, /device:TPU:1, one launch (start us, length us, event | category | flops | bytes accessed | tf_op | source)
XLA Modules:
  0.0 60.4 jit_solution(4254800054305652270)
XLA Ops:
  0.6 0.0 copy-start.1
  0.6 0.0 copy-start.5
  0.7 0.0 copy-start.6
  1.3 2.2 %axial_faces.1 = (f32[1,6,4,8,128]{4,3,2,1,0:T(8,128)}, f32[1,6,4,24,128]{4,3,2,1,0:T(8,128)}, f32[16,128]{1,0:T(8,128)}) custom-call(f32[5,32,16,128]{3,2,1,0:T(8,128)} %state.1, f32[32,16,128]{2,1,0:T(8,128)} %dt.1, f32[5,8,128]{2,1,0:T(8,128)} %rotor.1, s32[1]{0:T(128)S(6)} %copy.13.blade, s32[8]{0:T(128)} %harm.3), custom_call_target="tpu_custom_call" | custom-call | tf_op jit(solution)/shard_map/axial_faces/pallas_call | solution.py:518
  3.6 4.0 %collective-permute-start.3 = (f32[16,128]{1,0:T(8,128)}, f32[16,128]{1,0:T(8,128)S(1)}, u32[]{:S(2)}, u32[]{:S(2)}) collective-permute-start(f32[16,128]{1,0:T(8,128)} %get-tuple-element.22.part), channel_id=1, source_target_pairs={{0,1},{1,2},{2,3},{3,4},{4,5},{5,6},{6,7},{8,9},{9,10},{10,11},{11... | collective-permute-start | bytes 24584 | tf_op jit(solution)/shard_map/ppermute | solution.py:553
  7.6 1.8 %collective-permute-start.2 = (f32[16,128]{1,0:T(8,128)}, f32[16,128]{1,0:T(8,128)S(1)}, u32[]{:S(2)}, u32[]{:S(2)}) collective-permute-start(f32[16,128]{1,0:T(8,128)} %get-tuple-element.22.part), channel_id=1, source_target_pairs={{0,1},{1,0},{2,3},{3,2},{4,5},{5,4},{6,7},{7,6},{8,9},{9,8},{10,11... | collective-permute-start | bytes 24584 | tf_op jit(solution)/shard_map/ppermute | solution.py:552
  9.4 0.1 collective-permute-start
  9.4 0.0 copy-done.5
  9.4 4.5 %collective-permute-done.lo.hi.lo_edge.hi_edge = f32[6,4,8,128]{3,2,1,0:T(8,128)S(1)} collective-permute-done((f32[6,4,8,128]{3,2,1,0:T(8,128)}, f32[6,4,8,128]{3,2,1,0:T(8,128)S(1)}, u32[]{:S(2)}, u32[]{:S(2)}) %collective-permute-start) | collective-permute-done | bytes 98336 | tf_op jit(solution)/shard_map/ppermute | solution.py:543
  13.9 0.0 collective-permute-start.1
  13.9 0.0 copy-done.6
  13.9 0.0 collective-permute-done.3.before
  13.9 0.0 collective-permute-done.2.other
  13.9 0.0 copy-done.1
  13.9 0.0 copy-start
  14.0 1.3 %copy-done = f32[5,32,16,128]{3,2,1,0:T(8,128)S(1)} copy-done((f32[5,32,16,128]{3,2,1,0:T(8,128)S(1)}, f32[5,32,16,128]{3,2,1,0:T(8,128)}, u32[]{:S(2)}) %copy-start) | copy-done | bytes 1310744
  15.3 0.0 copy-start.2
  15.3 0.7 %copy-done.2 = f32[16,128]{1,0:T(8,128)S(1)} copy-done((f32[16,128]{1,0:T(8,128)S(1)}, f32[16,128]{1,0:T(8,128)}, u32[]{:S(2)}) %copy-start.2) | copy-done | bytes 8216
  16.0 0.5 span_faces.1
  16.5 4.6 %collective-permute-start.4 = (f32[496,128]{1,0:T(8,128)S(1)}, f32[496,128]{1,0:T(8,128)S(1)}, u32[]{:S(2)}, u32[]{:S(2)}) collective-permute-start(f32[496,128]{1,0:T(8,128)S(1)} %get-tuple-element.23), channel_id=1, source_target_pairs={{0,2},{2,4},{4,6},{1,3},{3,5},{5,7},{8,10},{10,12},{12,14},{9,11},... | collective-permute-start | bytes 761864 | tf_op jit(solution)/shard_map/ppermute | solution.py:591
  21.0 1.9 %collective-permute-start.5 = (f32[496,128]{1,0:T(8,128)S(1)}, f32[496,128]{1,0:T(8,128)S(1)}, u32[]{:S(2)}, u32[]{:S(2)}) collective-permute-start(f32[496,128]{1,0:T(8,128)S(1)} %get-tuple-element.24), channel_id=1, source_target_pairs={{2,0},{4,2},{6,4},{3,1},{5,3},{7,5},{10,8},{12,10},{14,12},{11,9},... | collective-permute-start | bytes 761864 | tf_op jit(solution)/shard_map/ppermute | solution.py:592
  23.0 1.3 %collective-permute-done.4.below = f32[496,128]{1,0:T(8,128)S(1)} collective-permute-done((f32[496,128]{1,0:T(8,128)S(1)}, f32[496,128]{1,0:T(8,128)S(1)}, u32[]{:S(2)}, u32[]{:S(2)}) %collective-permute-start.4) | collective-permute-done | bytes 253984 | tf_op jit(solution)/shard_map/ppermute | solution.py:591
  24.2 4.4 %collective-permute-done.5.above = f32[496,128]{1,0:T(8,128)S(1)} collective-permute-done((f32[496,128]{1,0:T(8,128)S(1)}, f32[496,128]{1,0:T(8,128)S(1)}, u32[]{:S(2)}, u32[]{:S(2)}) %collective-permute-start.5) | collective-permute-done | bytes 253984 | tf_op jit(solution)/shard_map/ppermute | solution.py:592
  28.6 0.0 collective-permute-done.1.lo.hi
  28.6 0.0 copy-start.4
  28.6 0.0 copy-start.3
  28.6 1.7 %circ_faces.1 = (f32[6,960,128]{2,1,0:T(8,128)S(1)}, f32[248,128]{1,0:T(8,128)S(1)}, f32[248,128]{1,0:T(8,128)S(1)}, f32[32,128]{1,0:T(8,128)S(1)}) custom-call(f32[5,512,128]{2,1,0:T(8,128)S(1)} %bitcast.12, f32[512,128]{1,0:T(8,128)S(1)} %bitcast.15, f32[6,4,8,128]{3,2,1,0:T(8,128)S(1)} %collective-permute-done.lo.hi.lo_edge.hi_edge, ...), custom_call_target="tpu_custom_call" | custom-call | tf_op jit(solution)/shard_map/circ_faces/pallas_call | solution.py:595
  30.3 1.3 %collective-permute-start.7 = (f32[248,128]{1,0:T(8,128)S(1)}, f32[248,128]{1,0:T(8,128)S(1)}, u32[]{:S(2)}, u32[]{:S(2)}) collective-permute-start(f32[248,128]{1,0:T(8,128)S(1)} %get-tuple-element.28), channel_id=1, source_target_pairs={{0,8},{8,16},{16,24},{24,0},{1,9},{9,17},{17,25},{25,1},{2,10},{10... | collective-permute-start | bytes 380936 | tf_op jit(solution)/shard_map/ppermute | solution.py:609
  31.7 2.1 %collective-permute-start.8 = (f32[248,128]{1,0:T(8,128)S(1)}, f32[248,128]{1,0:T(8,128)S(1)}, u32[]{:S(2)}, u32[]{:S(2)}) collective-permute-start(f32[248,128]{1,0:T(8,128)S(1)} %get-tuple-element.29), channel_id=1, source_target_pairs={{0,24},{8,0},{16,8},{24,16},{1,25},{9,1},{17,9},{25,17},{2,26},{10... | collective-permute-start | bytes 380936 | tf_op jit(solution)/shard_map/ppermute | solution.py:610
  33.8 0.4 collective-permute-start.6
  34.2 0.0 copy-done.4
  34.2 3.4 %collective-permute-done.6.shares_1_ = f32[32,128]{1,0:T(8,128)S(1)} collective-permute-done((f32[32,128]{1,0:T(8,128)S(1)}, f32[32,128]{1,0:T(8,128)S(1)}, u32[]{:S(2)}, u32[]{:S(2)}) %collective-permute-start.6) | collective-permute-done | bytes 16416 | tf_op jit(solution)/shard_map/ppermute | solution.py:612
  37.6 0.0 collective-permute-done.7.from_left
  37.6 0.0 collective-permute-done.8.from_right
  37.6 0.0 copy-done.3
  37.6 22.8 %segments.1 = (f32[5,512,128]{2,1,0:T(8,128)}, f32[5,512,128]{2,1,0:T(8,128)}, f32[6,960,128]{2,1,0:T(8,128)S(1)}) custom-call(f32[3,5,5]{2,1,0:T(8,128)S(1)} %copy.11.jac, s32[8]{0:T(128)S(1)} %copy-done.3, s32[1]{0:T(128)S(6)} %copy.13.blade, f32[32,128]{1,0:T(8,128)S(1)} %get-tuple-element.26.shares_0_, ...), custom_call_target="tpu_custom_call", output_to_operand_aliasing={{2}: (5, {})} | custom-call | tf_op jit(solution)/shard_map/segments/pallas_call | solution.py:617
  (3 shorter events, 0.0 us)
Async XLA Ops:
  0.6 13.3 %copy-start.1 = (f32[32,16,128]{2,1,0:T(8,128)S(1)}, f32[32,16,128]{2,1,0:T(8,128)}, u32[]{:S(2)}) copy-start(f32[32,16,128]{2,1,0:T(8,128)} %dt.1) | copy-start | bytes 786436
  0.6 8.8 %copy-start.5 = (s32[32]{0:T(128)S(1)}, s32[32]{0:T(128)}, u32[]{:S(2)}) copy-start(s32[32]{0:T(128)} %param.11) | copy-start | bytes 388
  0.7 13.3 %copy-start.6 = (f32[32]{0:T(128)S(1)}, f32[32]{0:T(128)}, u32[]{:S(2)}) copy-start(f32[32]{0:T(128)} %param.12) | copy-start | bytes 388
  3.6 10.4 %collective-permute-start.3 = (f32[16,128]{1,0:T(8,128)}, f32[16,128]{1,0:T(8,128)S(1)}, u32[]{:S(2)}, u32[]{:S(2)}) collective-permute-start(f32[16,128]{1,0:T(8,128)} %get-tuple-element.22.part), channel_id=1, source_target_pairs={{0,1},{1,2},{2,3},{3,4},{4,5},{5,6},{6,7},{8,9},{9,10},{10,11},{11... | collective-permute-start | bytes 24584 | tf_op jit(solution)/shard_map/ppermute | solution.py:553
  7.6 6.4 %collective-permute-start.2 = (f32[16,128]{1,0:T(8,128)}, f32[16,128]{1,0:T(8,128)S(1)}, u32[]{:S(2)}, u32[]{:S(2)}) collective-permute-start(f32[16,128]{1,0:T(8,128)} %get-tuple-element.22.part), channel_id=1, source_target_pairs={{0,1},{1,0},{2,3},{3,2},{4,5},{5,4},{6,7},{7,6},{8,9},{9,8},{10,11... | collective-permute-start | bytes 24584 | tf_op jit(solution)/shard_map/ppermute | solution.py:552
  9.4 4.5 %collective-permute-start = (f32[6,4,8,128]{3,2,1,0:T(8,128)}, f32[6,4,8,128]{3,2,1,0:T(8,128)S(1)}, u32[]{:S(2)}, u32[]{:S(2)}) collective-permute-start(f32[6,4,8,128]{3,2,1,0:T(8,128)} %bitcast.19), channel_id=1, source_target_pairs={{0,1},{1,0},{2,3},{3,2},{4,5},{5,4},{6,7},{7,6},{8,9},{9,8},{10,11... | collective-permute-start | bytes 294920 | tf_op jit(solution)/shard_map/ppermute | solution.py:543
  13.9 14.7 %collective-permute-start.1 = (f32[6,4,24,128]{3,2,1,0:T(8,128)}, f32[6,4,24,128]{3,2,1,0:T(8,128)S(1)}, u32[]{:S(2)}, u32[]{:S(2)}) collective-permute-start(f32[6,4,24,128]{3,2,1,0:T(8,128)} %bitcast.18), channel_id=1, source_target_pairs={{0,1},{1,0},{2,3},{3,2},{4,5},{5,4},{6,7},{7,6},{8,9},{9,8},{10,11... | collective-permute-start | bytes 884744 | tf_op jit(solution)/shard_map/ppermute | solution.py:543
  13.9 1.3 %copy-start = (f32[5,32,16,128]{3,2,1,0:T(8,128)S(1)}, f32[5,32,16,128]{3,2,1,0:T(8,128)}, u32[]{:S(2)}) copy-start(f32[5,32,16,128]{3,2,1,0:T(8,128)} %state.1) | copy-start | bytes 3932164
  15.3 0.7 %copy-start.2 = (f32[16,128]{1,0:T(8,128)S(1)}, f32[16,128]{1,0:T(8,128)}, u32[]{:S(2)}) copy-start(f32[16,128]{1,0:T(8,128)} %get-tuple-element.22.part) | copy-start | bytes 24580
  16.5 7.8 %collective-permute-start.4 = (f32[496,128]{1,0:T(8,128)S(1)}, f32[496,128]{1,0:T(8,128)S(1)}, u32[]{:S(2)}, u32[]{:S(2)}) collective-permute-start(f32[496,128]{1,0:T(8,128)S(1)} %get-tuple-element.23), channel_id=1, source_target_pairs={{0,2},{2,4},{4,6},{1,3},{3,5},{5,7},{8,10},{10,12},{12,14},{9,11},... | collective-permute-start | bytes 761864 | tf_op jit(solution)/shard_map/ppermute | solution.py:591
  21.0 7.6 %collective-permute-start.5 = (f32[496,128]{1,0:T(8,128)S(1)}, f32[496,128]{1,0:T(8,128)S(1)}, u32[]{:S(2)}, u32[]{:S(2)}) collective-permute-start(f32[496,128]{1,0:T(8,128)S(1)} %get-tuple-element.24), channel_id=1, source_target_pairs={{2,0},{4,2},{6,4},{3,1},{5,3},{7,5},{10,8},{12,10},{14,12},{11,9},... | collective-permute-start | bytes 761864 | tf_op jit(solution)/shard_map/ppermute | solution.py:592
  28.6 5.5 %copy-start.4 = (f32[3,5,5]{2,0,1:T(4,128)S(1)}, f32[3,5,5]{2,0,1:T(4,128)}, u32[]{:S(2)}) copy-start(f32[3,5,5]{2,0,1:T(4,128)} %param.15) | copy-start | bytes 904
  28.6 8.9 %copy-start.3 = (s32[8]{0:T(128)S(1)}, s32[8]{0:T(128)}, u32[]{:S(2)}) copy-start(s32[8]{0:T(128)} %harm.3) | copy-start | bytes 100
  30.3 7.2 %collective-permute-start.7 = (f32[248,128]{1,0:T(8,128)S(1)}, f32[248,128]{1,0:T(8,128)S(1)}, u32[]{:S(2)}, u32[]{:S(2)}) collective-permute-start(f32[248,128]{1,0:T(8,128)S(1)} %get-tuple-element.28), channel_id=1, source_target_pairs={{0,8},{8,16},{16,24},{24,0},{1,9},{9,17},{17,25},{25,1},{2,10},{10... | collective-permute-start | bytes 380936 | tf_op jit(solution)/shard_map/ppermute | solution.py:609
  31.7 5.9 %collective-permute-start.8 = (f32[248,128]{1,0:T(8,128)S(1)}, f32[248,128]{1,0:T(8,128)S(1)}, u32[]{:S(2)}, u32[]{:S(2)}) collective-permute-start(f32[248,128]{1,0:T(8,128)S(1)} %get-tuple-element.29), channel_id=1, source_target_pairs={{0,24},{8,0},{16,8},{24,16},{1,25},{9,1},{17,9},{25,17},{2,26},{10... | collective-permute-start | bytes 380936 | tf_op jit(solution)/shard_map/ppermute | solution.py:610
  33.8 3.8 %collective-permute-start.6 = (f32[32,128]{1,0:T(8,128)S(1)}, f32[32,128]{1,0:T(8,128)S(1)}, u32[]{:S(2)}, u32[]{:S(2)}) collective-permute-start(f32[32,128]{1,0:T(8,128)S(1)} %get-tuple-element.26.shares_0_), channel_id=1, source_target_pairs={{0,16},{8,24},{16,0},{24,8},{1,17},{9,25},{17,1},{25,9},{2,18},{10... | collective-permute-start | bytes 49160 | tf_op jit(solution)/shard_map/ppermute | solution.py:612

commit v8 on v7

--- a/solution.py
+++ b/solution.py
@@ -36,40 +36,28 @@
     return lax.dot_general(a, b, (dims, ((), ())), precision=HIGH, preferred_element_type=jnp.float32)
 
 
-def axial_kernel(dims, state, dt, rotor, blade, harm, edge, bulk, part, *scratch):
-    nv, sl, al, cl, nh = (dims[k] for k in ("nv", "sl", "al", "cl", "nh"))
-    cells, dt_cells, rotor_v, blade_s, harm_s, sems = scratch
+def coef_kernel(dims, rotor, blade, harm, after, part):
+    del after
+    nv, cl = dims["nv"], dims["cl"]
+    ncells = cl * dims["n_circ"]
+    here = lax.axis_index("circ") * cl + lax.broadcasted_iota(jnp.int32, (1, cl), 1)
+    basis = make_basis(harm, blade, dims["nh"], here, ncells)
+    rl = rotor.shape[1]
+    part[...] = jnp.zeros_like(part)
+    part[:, : nv * rl] = dot(basis, rotor[...].reshape(nv * rl, cl), ((1,), (1,))) * (2.0 / ncells)
+
+
+def axial_kernel(dims, state, dt, edge, bulk, after):
+    nv, sl, al = (dims[k] for k in ("nv", "sl", "al"))
     axial = lax.axis_index("axial")
-    circ = lax.axis_index("circ")
     swap = dims["n_axial"] == 2
-    size = cells.shape[2]
-    at = pl.multiple_of(jnp.where(axial == 0, al - size, 0), 8) if swap else 0
-    copies = [
-        pltpu.make_async_copy(state.at[:, :, pl.ds(at, size), :], cells, sems.at[0]),
-        pltpu.make_async_copy(dt.at[:, pl.ds(at, size), :], dt_cells, sems.at[1]),
-        pltpu.make_async_copy(rotor, rotor_v, sems.at[2]),
-        pltpu.make_async_copy(blade, blade_s, sems.at[3]),
-        pltpu.make_async_copy(harm, harm_s, sems.at[4]),
-    ]
-    for copy in copies:
-        copy.start()
-    for copy in copies[2:]:
-        copy.wait()
-    ncells = cl * dims["n_circ"]
-    here = circ * cl + lax.broadcasted_iota(jnp.int32, (1, cl), 1)
-    basis = make_basis(harm_s, blade_s, nh, here, ncells)
-    rl = rotor_v.shape[1]
-    flat = rotor_v[...].reshape(nv * rl, cl)
-    part[...] = jnp.zeros_like(part)
-    part[:, : nv * rl] = dot(basis, flat, ((1,), (1,))) * (2.0 / ncells)
-    for copy in copies[:2]:
-        copy.wait()
+    size = al
+    after[...] = jnp.zeros_like(after)
 
     def put(side, base):
         for f in range(nv + 1):
             for i in range(W):
-                ref = cells.at[f] if f < nv else dt_cells
-                rows = ref[:, base + i, :]
+                rows = state[f, :, base + i, :] if f < nv else dt[:, base + i, :]
                 edge[side, f, i, 0:W] = rows[0:W]
                 edge[side, f, i, W:] = rows[sl - W :]
                 bulk[side, f, i] = rows[W : sl - W]
@@ -459,10 +447,10 @@
             view = p_src.at[:, pl.ds(around, 3 * br), :]
 
             values = block_cells(view, br)
-            for t in range(br // 8):
-                cell = values(t)
+            cells = [values(t) for t in range(br // 8)]
+            for t, cell in enumerate(cells):
                 turn(cell, [edge[v, pl.ds(around + 8 * t, 8), :] for v in range(nv)], pos4, pos3)
-                (result,) = apply([cell])
+            for t, result in enumerate(apply(cells)):
                 step = (2.0 * DISSIP * factor) * p_0[nv, pl.ds(base + 8 * t, 8), :]
                 for u in range(nv):
                     p_dst[u, pl.ds(base + 8 * t, 8), :] = p_0[u, pl.ds(base + 8 * t, 8), :] - step * result[u]
@@ -513,28 +501,27 @@
     dims.update(rl=rl, packs=packs, ride=ride)
     params = pltpu.CompilerParams(vmem_limit_bytes=48 * 2**20)
     sides = 1 if n_axial == 2 else 2
-    deep = 8 if n_axial == 2 else al
-
-    edge, bulk, part = pl.pallas_call(
+
+    edge, bulk, after = pl.pallas_call(
         functools.partial(axial_kernel, dims),
         out_shape=[
             jax.ShapeDtypeStruct((sides, nv + 1, W, 2 * W, cl), f32),
             jax.ShapeDtypeStruct((sides, nv + 1, W, sl - 2 * W, cl), f32),
-            jax.ShapeDtypeStruct((2 * nh, -(-nv * rl // 128) * 128), f32),
+            jax.ShapeDtypeStruct((8, 128), f32),
         ],
-        in_specs=[HBM] * 5,
+        in_specs=[VMEM] * 2,
         out_specs=[VMEM] * 3,
-        scratch_shapes=[
-            pltpu.VMEM((nv, sl, deep, cl), f32),
-            pltpu.VMEM((sl, deep, cl), f32),
-            pltpu.VMEM(rotor_outlet.shape, f32),
-            pltpu.SMEM(blade_count.shape, jnp.int32),
-            pltpu.SMEM(harmonic_list.shape, jnp.int32),
-            pltpu.SemaphoreType.DMA((5,)),
-        ],
-        compiler_params=pltpu.CompilerParams(vmem_limit_bytes=63 * 2**20),
+        compiler_params=params,
         name="axial_faces",
-    )(state, time_step, rotor_outlet, blade_count, harmonic_list)
+    )(state, time_step)
+    part = pl.pallas_call(
+        functools.partial(coef_kernel, dims),
+        out_shape=jax.ShapeDtypeStruct((2 * nh, -(-nv * rl // 128) * 128), f32),
+        in_specs=[VMEM, SMEM, SMEM, VMEM],
+        out_specs=VMEM,
+        compiler_params=params,
+        name="coef_share",
+    )(rotor_outlet, blade_count, harmonic_list, after)
     state = state.reshape(nv, sl * al, cl)
     time_step = time_step.reshape(sl * al, cl)
 
@@ -547,7 +534,6 @@
         return lo, hi
 
     lo_edge, hi_edge = axial_move(edge)
-    bulk, lo_edge, hi_edge = lax.optimization_barrier((bulk, lo_edge, hi_edge))
     if ride:
         other = lax.ppermute(part, "axial", [(0, 1), (1, 0)])
         before = lax.ppermute(part, ("span", "axial"), shift_pairs(n_span * n_axial, 1, False))

time: 60.7 us -> 59 us (0.972)
  Pallas kernels: 27.2 us -> 25.9 us
  waiting for transfers between devices: 13.5 us -> 12.2 us
  local copies, waits for them, and re-layouts: 2.04 us -> 2.77 us
    pallas_call x1, Pallas kernels: 2.21 us -> 0.22 us  [local(): pl.pallas_call(functools.partial(axial_kernel, dims), out_shape=[jax.Shap...]
    ppermute x2, starting transfers between devices: 0.08 us -> 1.47 us  [axial_move(): moved = lax.ppermute(faces[0], 'axial', [(0, 1), (1, 0)])]
    ppermute x1, starting transfers between devices: 4.56 us -> 3.37 us  [local(): below = lax.ppermute(up, 'span', shift_pairs(n_span, 1, False))]
    ppermute x2, waiting for transfers between devices: 4.46 us -> 3.44 us  [axial_move(): moved = lax.ppermute(faces[0], 'axial', [(0, 1), (1, 0)])]
    unnamed x15 -> x17, local copies, waits for them, and re-layouts: 2.03 us -> 2.77 us
    pallas_call x0 -> x1, Pallas kernels: none -> 0.73 us  [local(): pl.pallas_call(functools.partial(coef_kernel, dims), out_shape=jax.ShapeD...]
  transfers between devices with their start and end apart: 9 -> 9, of which waited for: 4 -> 5; matrix products, arithmetic and copies ran while one was open for 0% -> 0% of each run, Pallas kernels for 1% -> 1%
where the time goes in v8:
time: 59 us; the launch traced here: 58.7 us
  Pallas kernels  25.9 us (44%)
  starting transfers between devices  16.4 us (28%)
  waiting for transfers between devices  12.2 us (21%)
  local copies, waits for them, and re-layouts  2.77 us (5%)
  between operations  1.42 us (2%)
    pallas_call x1, Pallas kernels, local(): pl.pallas_call(functools.partial(step_kernel, dims), out_shape=[block, bl...  22.8 us
    ppermute x1, waiting for transfers between devices, local(): above = lax.ppermute(down, 'span', shift_pairs(n_span, -1, False))  4.4 us
    ppermute x1, starting transfers between devices, local(): lax.ppermute(part, ('span', 'axial'), shift_pairs(n_span * n_axial, 1, Fa...  3.95 us
    ppermute x2, waiting for transfers between devices, axial_move(): moved = lax.ppermute(faces[0], 'axial', [(0, 1), (1, 0)])  3.44 us
    ppermute x1, waiting for transfers between devices, local(): shares = [share, lax.ppermute(share, 'circ', shift_pairs(n_circ, 2, True))]  3.4 us
    ppermute x1, starting transfers between devices, local(): below = lax.ppermute(up, 'span', shift_pairs(n_span, 1, False))  3.37 us
    unnamed x17, local copies, waits for them, and re-layouts  2.77 us
    ppermute x1, starting transfers between devices, local(): from_right = lax.ppermute(left, 'circ', shift_pairs(n_circ, -1, True))  2.09 us
  transfers between devices with their start and end apart: 9, of which 5 were waited for; matrix products, arithmetic and copies ran while one was open for 0% of the time, Pallas kernels for 1%

profile of v8, /device:TPU:1, one launch (start us, length us, event | category | flops | bytes accessed | tf_op | source)
XLA Modules:
  0.0 58.7 jit_solution(16197923706860731447)
XLA Ops:
  0.6 0.0 copy-start.4
  0.6 0.0 copy-start.6
  0.7 0.0 copy-start.7
  1.3 0.0 copy-start
  1.3 1.3 %copy-done = f32[5,32,16,128]{3,2,1,0:T(8,128)S(1)} copy-done((f32[5,32,16,128]{3,2,1,0:T(8,128)S(1)}, f32[5,32,16,128]{3,2,1,0:T(8,128)}, u32[]{:S(2)}) %copy-start) | copy-done | bytes 1310744
  2.6 0.0 copy-start.2
  2.7 0.9 %copy-done.2 = f32[32,16,128]{2,1,0:T(8,128)S(1)} copy-done((f32[32,16,128]{2,1,0:T(8,128)S(1)}, f32[32,16,128]{2,1,0:T(8,128)}, u32[]{:S(2)}) %copy-start.2) | copy-done | bytes 262168
  3.6 0.0 copy-start.3
  3.6 0.0 copy-start.1
  3.6 0.2 axial_faces.1
  3.8 0.0 copy-done.4
  3.8 0.5 copy-done.3
  4.3 0.7 %coef_share.1.part = f32[16,128]{1,0:T(8,128)S(1)} custom-call(f32[5,8,128]{2,1,0:T(8,128)S(1)} %copy-done.3, s32[1]{0:T(128)S(6)} %copy.13.blade, s32[8]{0:T(128)S(1)} %copy-done.4, f32[8,128]{1,0:T(8,128)S(1)} %get-tuple-element.16.after), custom_call_target="tpu_custom_call" | custom-call | tf_op jit(solution)/shard_map/coef_share/pallas_call | solution.py:517
  5.1 4.0 %collective-permute-start.3 = (f32[16,128]{1,0:T(8,128)S(1)}, f32[16,128]{1,0:T(8,128)S(1)}, u32[]{:S(2)}, u32[]{:S(2)}) collective-permute-start(f32[16,128]{1,0:T(8,128)S(1)} %coef_share.1.part), channel_id=1, source_target_pairs={{0,1},{1,2},{2,3},{3,4},{4,5},{5,6},{6,7},{8,9},{9,10},{10,11},{11... | collective-permute-start | bytes 24584 | tf_op jit(solution)/shard_map/ppermute | solution.py:539
  9.0 1.8 %collective-permute-start.2 = (f32[16,128]{1,0:T(8,128)S(1)}, f32[16,128]{1,0:T(8,128)S(1)}, u32[]{:S(2)}, u32[]{:S(2)}) collective-permute-start(f32[16,128]{1,0:T(8,128)S(1)} %coef_share.1.part), channel_id=1, source_target_pairs={{0,1},{1,0},{2,3},{3,2},{4,5},{5,4},{6,7},{7,6},{8,9},{9,8},{10,11... | collective-permute-start | bytes 24584 | tf_op jit(solution)/shard_map/ppermute | solution.py:538
  10.9 0.1 collective-permute-start
  10.9 1.4 %collective-permute-start.1 = (f32[6,4,24,128]{3,2,1,0:T(8,128)S(1)}, f32[6,4,24,128]{3,2,1,0:T(8,128)S(1)}, u32[]{:S(2)}, u32[]{:S(2)}) collective-permute-start(f32[6,4,24,128]{3,2,1,0:T(8,128)S(1)} %bitcast.16), channel_id=1, source_target_pairs={{0,1},{1,0},{2,3},{3,2},{4,5},{5,4},{6,7},{7,6},{8,9},{9,8},{10,11... | collective-permute-start | bytes 884744 | tf_op jit(solution)/shard_map/ppermute | solution.py:530
  12.3 0.0 copy-done.6
  12.3 0.0 copy-done.7
  12.3 0.0 collective-permute-done.3.before
  12.4 0.0 collective-permute-done.2.other
  12.4 3.1 %collective-permute-done.lo.hi.lo_edge.hi_edge = f32[6,4,8,128]{3,2,1,0:T(8,128)S(1)} collective-permute-done((f32[6,4,8,128]{3,2,1,0:T(8,128)S(1)}, f32[6,4,8,128]{3,2,1,0:T(8,128)S(1)}, u32[]{:S(2)}, u32[]{:S(2)}) %collective-permute-start) | collective-permute-done | bytes 98336 | tf_op jit(solution)/shard_map/ppermute | solution.py:530
  15.5 0.0 copy-done.1
  15.5 0.5 span_faces.1
  16.0 3.4 %collective-permute-start.4 = (f32[496,128]{1,0:T(8,128)S(1)}, f32[496,128]{1,0:T(8,128)S(1)}, u32[]{:S(2)}, u32[]{:S(2)}) collective-permute-start(f32[496,128]{1,0:T(8,128)S(1)} %get-tuple-element.17), channel_id=1, source_target_pairs={{0,2},{2,4},{4,6},{1,3},{3,5},{5,7},{8,10},{10,12},{12,14},{9,11},... | collective-permute-start | bytes 761864 | tf_op jit(solution)/shard_map/ppermute | solution.py:577
  19.4 1.9 %collective-permute-start.5 = (f32[496,128]{1,0:T(8,128)S(1)}, f32[496,128]{1,0:T(8,128)S(1)}, u32[]{:S(2)}, u32[]{:S(2)}) collective-permute-start(f32[496,128]{1,0:T(8,128)S(1)} %get-tuple-element.18), channel_id=1, source_target_pairs={{2,0},{4,2},{6,4},{3,1},{5,3},{7,5},{10,8},{12,10},{14,12},{11,9},... | collective-permute-start | bytes 761864 | tf_op jit(solution)/shard_map/ppermute | solution.py:578
  21.3 0.3 collective-permute-done.1.lo.hi
  21.6 1.0 %collective-permute-done.4.below = f32[496,128]{1,0:T(8,128)S(1)} collective-permute-done((f32[496,128]{1,0:T(8,128)S(1)}, f32[496,128]{1,0:T(8,128)S(1)}, u32[]{:S(2)}, u32[]{:S(2)}) %collective-permute-start.4) | collective-permute-done | bytes 253984 | tf_op jit(solution)/shard_map/ppermute | solution.py:577
  22.6 4.4 %collective-permute-done.5.above = f32[496,128]{1,0:T(8,128)S(1)} collective-permute-done((f32[496,128]{1,0:T(8,128)S(1)}, f32[496,128]{1,0:T(8,128)S(1)}, u32[]{:S(2)}, u32[]{:S(2)}) %collective-permute-start.5) | collective-permute-done | bytes 253984 | tf_op jit(solution)/shard_map/ppermute | solution.py:578
  27.0 0.0 copy-start.5
  27.0 1.7 %circ_faces.1 = (f32[6,960,128]{2,1,0:T(8,128)S(1)}, f32[248,128]{1,0:T(8,128)S(1)}, f32[248,128]{1,0:T(8,128)S(1)}, f32[32,128]{1,0:T(8,128)S(1)}) custom-call(f32[5,512,128]{2,1,0:T(8,128)S(1)} %bitcast.12, f32[512,128]{1,0:T(8,128)S(1)} %bitcast.15, f32[6,4,8,128]{3,2,1,0:T(8,128)S(1)} %collective-permute-done.lo.hi.lo_edge.hi_edge, ...), custom_call_target="tpu_custom_call" | custom-call | tf_op jit(solution)/shard_map/circ_faces/pallas_call | solution.py:581
  28.7 1.3 %collective-permute-start.7 = (f32[248,128]{1,0:T(8,128)S(1)}, f32[248,128]{1,0:T(8,128)S(1)}, u32[]{:S(2)}, u32[]{:S(2)}) collective-permute-start(f32[248,128]{1,0:T(8,128)S(1)} %get-tuple-element.22), channel_id=1, source_target_pairs={{0,8},{8,16},{16,24},{24,0},{1,9},{9,17},{17,25},{25,1},{2,10},{10... | collective-permute-start | bytes 380936 | tf_op jit(solution)/shard_map/ppermute | solution.py:595
  30.0 2.1 %collective-permute-start.8 = (f32[248,128]{1,0:T(8,128)S(1)}, f32[248,128]{1,0:T(8,128)S(1)}, u32[]{:S(2)}, u32[]{:S(2)}) collective-permute-start(f32[248,128]{1,0:T(8,128)S(1)} %get-tuple-element.23), channel_id=1, source_target_pairs={{0,24},{8,0},{16,8},{24,16},{1,25},{9,1},{17,9},{25,17},{2,26},{10... | collective-permute-start | bytes 380936 | tf_op jit(solution)/shard_map/ppermute | solution.py:596
  32.1 0.4 collective-permute-start.6
  32.5 0.0 copy-done.5
  32.5 3.4 %collective-permute-done.6.shares_1_ = f32[32,128]{1,0:T(8,128)S(1)} collective-permute-done((f32[32,128]{1,0:T(8,128)S(1)}, f32[32,128]{1,0:T(8,128)S(1)}, u32[]{:S(2)}, u32[]{:S(2)}) %collective-permute-start.6) | collective-permute-done | bytes 16416 | tf_op jit(solution)/shard_map/ppermute | solution.py:598
  35.9 0.0 collective-permute-done.7.from_left
  35.9 0.0 collective-permute-done.8.from_right
  35.9 22.8 %segments.1 = (f32[5,512,128]{2,1,0:T(8,128)}, f32[5,512,128]{2,1,0:T(8,128)}, f32[6,960,128]{2,1,0:T(8,128)S(1)}) custom-call(f32[3,5,5]{2,1,0:T(8,128)S(1)} %copy.11.jac, s32[8]{0:T(128)S(1)} %copy-done.4, s32[1]{0:T(128)S(6)} %copy.13.blade, f32[32,128]{1,0:T(8,128)S(1)} %get-tuple-element.20.shares_0_, ...), custom_call_target="tpu_custom_call", output_to_operand_aliasing={{2}: (5, {})} | custom-call | tf_op jit(solution)/shard_map/segments/pallas_call | solution.py:603
  (3 shorter events, 0.0 us)
Async XLA Ops:
  0.6 3.2 %copy-start.4 = (s32[8]{0:T(128)S(1)}, s32[8]{0:T(128)}, u32[]{:S(2)}) copy-start(s32[8]{0:T(128)} %harm.3) | copy-start | bytes 100
  0.6 11.7 %copy-start.6 = (s32[32]{0:T(128)S(1)}, s32[32]{0:T(128)}, u32[]{:S(2)}) copy-start(s32[32]{0:T(128)} %param.11) | copy-start | bytes 388
  0.7 11.7 %copy-start.7 = (f32[32]{0:T(128)S(1)}, f32[32]{0:T(128)}, u32[]{:S(2)}) copy-start(f32[32]{0:T(128)} %param.12) | copy-start | bytes 388
  1.3 1.3 %copy-start = (f32[5,32,16,128]{3,2,1,0:T(8,128)S(1)}, f32[5,32,16,128]{3,2,1,0:T(8,128)}, u32[]{:S(2)}) copy-start(f32[5,32,16,128]{3,2,1,0:T(8,128)} %state.1) | copy-start | bytes 3932164
  2.6 0.9 %copy-start.2 = (f32[32,16,128]{2,1,0:T(8,128)S(1)}, f32[32,16,128]{2,1,0:T(8,128)}, u32[]{:S(2)}) copy-start(f32[32,16,128]{2,1,0:T(8,128)} %dt.1) | copy-start | bytes 786436
  3.6 0.7 %copy-start.3 = (f32[5,8,128]{2,1,0:T(8,128)S(1)}, f32[5,8,128]{2,1,0:T(8,128)}, u32[]{:S(2)}) copy-start(f32[5,8,128]{2,1,0:T(8,128)} %rotor.1) | copy-start | bytes 61444
  3.6 11.9 %copy-start.1 = (f32[5,32,16,128]{3,2,1,0:T(8,128)S(1)}, f32[5,32,16,128]{3,2,1,0:T(8,128)}, u32[]{:S(2)}) copy-start(f32[5,32,16,128]{3,2,1,0:T(8,128)} %state.1) | copy-start | bytes 3932164
  5.1 7.3 %collective-permute-start.3 = (f32[16,128]{1,0:T(8,128)S(1)}, f32[16,128]{1,0:T(8,128)S(1)}, u32[]{:S(2)}, u32[]{:S(2)}) collective-permute-start(f32[16,128]{1,0:T(8,128)S(1)} %coef_share.1.part), channel_id=1, source_target_pairs={{0,1},{1,2},{2,3},{3,4},{4,5},{5,6},{6,7},{8,9},{9,10},{10,11},{11... | collective-permute-start | bytes 24584 | tf_op jit(solution)/shard_map/ppermute | solution.py:539
  9.0 3.3 %collective-permute-start.2 = (f32[16,128]{1,0:T(8,128)S(1)}, f32[16,128]{1,0:T(8,128)S(1)}, u32[]{:S(2)}, u32[]{:S(2)}) collective-permute-start(f32[16,128]{1,0:T(8,128)S(1)} %coef_share.1.part), channel_id=1, source_target_pairs={{0,1},{1,0},{2,3},{3,2},{4,5},{5,4},{6,7},{7,6},{8,9},{9,8},{10,11... | collective-permute-start | bytes 24584 | tf_op jit(solution)/shard_map/ppermute | solution.py:538
  10.9 4.6 %collective-permute-start = (f32[6,4,8,128]{3,2,1,0:T(8,128)S(1)}, f32[6,4,8,128]{3,2,1,0:T(8,128)S(1)}, u32[]{:S(2)}, u32[]{:S(2)}) collective-permute-start(f32[6,4,8,128]{3,2,1,0:T(8,128)S(1)} %bitcast.17), channel_id=1, source_target_pairs={{0,1},{1,0},{2,3},{3,2},{4,5},{5,4},{6,7},{7,6},{8,9},{9,8},{10,11... | collective-permute-start | bytes 294920 | tf_op jit(solution)/shard_map/ppermute | solution.py:530
  10.9 10.7 %collective-permute-start.1 = (f32[6,4,24,128]{3,2,1,0:T(8,128)S(1)}, f32[6,4,24,128]{3,2,1,0:T(8,128)S(1)}, u32[]{:S(2)}, u32[]{:S(2)}) collective-permute-start(f32[6,4,24,128]{3,2,1,0:T(8,128)S(1)} %bitcast.16), channel_id=1, source_target_pairs={{0,1},{1,0},{2,3},{3,2},{4,5},{5,4},{6,7},{7,6},{8,9},{9,8},{10,11... | collective-permute-start | bytes 884744 | tf_op jit(solution)/shard_map/ppermute | solution.py:530
  16.0 6.6 %collective-permute-start.4 = (f32[496,128]{1,0:T(8,128)S(1)}, f32[496,128]{1,0:T(8,128)S(1)}, u32[]{:S(2)}, u32[]{:S(2)}) collective-permute-start(f32[496,128]{1,0:T(8,128)S(1)} %get-tuple-element.17), channel_id=1, source_target_pairs={{0,2},{2,4},{4,6},{1,3},{3,5},{5,7},{8,10},{10,12},{12,14},{9,11},... | collective-permute-start | bytes 761864 | tf_op jit(solution)/shard_map/ppermute | solution.py:577
  19.4 7.6 %collective-permute-start.5 = (f32[496,128]{1,0:T(8,128)S(1)}, f32[496,128]{1,0:T(8,128)S(1)}, u32[]{:S(2)}, u32[]{:S(2)}) collective-permute-start(f32[496,128]{1,0:T(8,128)S(1)} %get-tuple-element.18), channel_id=1, source_target_pairs={{2,0},{4,2},{6,4},{3,1},{5,3},{7,5},{10,8},{12,10},{14,12},{11,9},... | collective-permute-start | bytes 761864 | tf_op jit(solution)/shard_map/ppermute | solution.py:578
  27.0 5.5 %copy-start.5 = (f32[3,5,5]{2,0,1:T(4,128)S(1)}, f32[3,5,5]{2,0,1:T(4,128)}, u32[]{:S(2)}) copy-start(f32[3,5,5]{2,0,1:T(4,128)} %param.15) | copy-start | bytes 904
  28.7 7.2 %collective-permute-start.7 = (f32[248,128]{1,0:T(8,128)S(1)}, f32[248,128]{1,0:T(8,128)S(1)}, u32[]{:S(2)}, u32[]{:S(2)}) collective-permute-start(f32[248,128]{1,0:T(8,128)S(1)} %get-tuple-element.22), channel_id=1, source_target_pairs={{0,8},{8,16},{16,24},{24,0},{1,9},{9,17},{17,25},{25,1},{2,10},{10... | collective-permute-start | bytes 380936 | tf_op jit(solution)/shard_map/ppermute | solution.py:595
  30.0 5.9 %collective-permute-start.8 = (f32[248,128]{1,0:T(8,128)S(1)}, f32[248,128]{1,0:T(8,128)S(1)}, u32[]{:S(2)}, u32[]{:S(2)}) collective-permute-start(f32[248,128]{1,0:T(8,128)S(1)} %get-tuple-element.23), channel_id=1, source_target_pairs={{0,24},{8,0},{16,8},{24,16},{1,25},{9,1},{17,9},{25,17},{2,26},{10... | collective-permute-start | bytes 380936 | tf_op jit(solution)/shard_map/ppermute | solution.py:596
  32.1 3.8 %collective-permute-start.6 = (f32[32,128]{1,0:T(8,128)S(1)}, f32[32,128]{1,0:T(8,128)S(1)}, u32[]{:S(2)}, u32[]{:S(2)}) collective-permute-start(f32[32,128]{1,0:T(8,128)S(1)} %get-tuple-element.20.shares_0_), channel_id=1, source_target_pairs={{0,16},{8,24},{16,0},{24,8},{1,17},{9,25},{17,1},{25,9},{2,18},{10... | collective-permute-start | bytes 49160 | tf_op jit(solution)/shard_map/ppermute | solution.py:598

commit v9 on v8

--- a/solution.py
+++ b/solution.py
@@ -271,30 +271,28 @@
     if dims["ride"]:
         rows = slice(half * ng * br, None)
         packed = from_left[rows, :] + from_right[rows, :] + shares[0][...] + shares[1][...]
-        inter = []
-        for v in range(nv):
-            pack, first = divmod(v, 128 // wide)
-            part = pltpu.roll(packed[pack * 2 * nh : (pack + 1) * 2 * nh, :], (-first * wide) % 128, 1)
-            inter.append(jnp.where(lane < wide, part, 0.0))
+        inter = [packed[i * 2 * nh : (i + 1) * 2 * nh, :] for i in range(dims["packs"])]
+        each = 128 // wide
     else:
         inter = ghost_table(dims, shares, span)
+        each = 1
     start = circ * cl
     own = make_basis(harm, blade, nh, start + lax.broadcasted_iota(jnp.int32, (1, cl), 1), ncells)
     pos = lane % 8
     halo_cells = lax.rem(start + jnp.where(pos < 4, pos - 4, pos + cl - 4) + ncells, ncells)
     halo = make_basis(harm, blade, nh, halo_cells, ncells)
-    s_id = lax.broadcasted_iota(jnp.int32, (128, 128), 0)
-    r_id = lax.broadcasted_iota(jnp.int32, (128, 128), 1) // 8
+    s_id = lax.broadcasted_iota(jnp.int32, (wide, 128), 0)
+    r_id = lax.broadcasted_iota(jnp.int32, (wide, 128), 1) // 8
 
     @pl.when(axial == 0)
     def _():
+        ghosts = [dot(part, own, ((0,), (0,))) for part in inter]
+        halos = [dot(part, halo, ((0,), (0,))) for part in inter]
         for v in range(nv):
-            part = inter[v]
-            ghost = dot(part, own, ((0,), (0,)))
-            ext[v, pl.ds(7, sl + 2 * W, stride=br), :] = ghost[: sl + 2 * W, :]
-            ghost = dot(part, halo, ((0,), (0,)))
+            rows = slice(v % each * wide, (v % each + 1) * wide)
+            ext[v, pl.ds(7, wide, stride=br), :] = ghosts[v // each][rows]
             for g in range(ng):
-                picked = jnp.where(s_id == ng * r_id + g, ghost, 0.0)
+                picked = jnp.where(s_id == ng * r_id + g, halos[v // each][rows], 0.0)
                 at = (g + 1) * br + 7
                 p_0[v, at : at + 1, :] = jnp.sum(picked, axis=0, keepdims=True)
 

time: 59 us -> 58.7 us (level)
  no operation moved by 1% of the time
where the time goes in v9:
time: 58.7 us; the launch traced here: 58.4 us
  Pallas kernels  25.6 us (44%)
  starting transfers between devices  16.4 us (28%)
  waiting for transfers between devices  12.2 us (21%)
  local copies, waits for them, and re-layouts  2.77 us (5%)
  between operations  1.42 us (2%)
    pallas_call x1, Pallas kernels, local(): pl.pallas_call(functools.partial(step_kernel, dims), out_shape=[block, bl...  22.5 us
    ppermute x1, waiting for transfers between devices, local(): above = lax.ppermute(down, 'span', shift_pairs(n_span, -1, False))  4.4 us
    ppermute x1, starting transfers between devices, local(): lax.ppermute(part, ('span', 'axial'), shift_pairs(n_span * n_axial, 1, Fa...  3.95 us
    ppermute x2, waiting for transfers between devices, axial_move(): moved = lax.ppermute(faces[0], 'axial', [(0, 1), (1, 0)])  3.44 us
    ppermute x1, waiting for transfers between devices, local(): shares = [share, lax.ppermute(share, 'circ', shift_pairs(n_circ, 2, True))]  3.4 us
    ppermute x1, starting transfers between devices, local(): below = lax.ppermute(up, 'span', shift_pairs(n_span, 1, False))  3.37 us
    unnamed x17, local copies, waits for them, and re-layouts  2.77 us
    ppermute x1, starting transfers between devices, local(): from_right = lax.ppermute(left, 'circ', shift_pairs(n_circ, -1, True))  2.09 us
  transfers between devices with their start and end apart: 9, of which 5 were waited for; matrix products, arithmetic and copies ran while one was open for 0% of the time, Pallas kernels for 1%

profile of v9, /device:TPU:1, one launch (start us, length us, event | category | flops | bytes accessed | tf_op | source)
XLA Modules:
  0.0 58.4 jit_solution(8285257604941104001)
XLA Ops:
  0.6 0.0 copy-start.4
  0.6 0.0 copy-start.6
  0.7 0.0 copy-start.7
  1.3 0.0 copy-start
  1.3 1.3 %copy-done = f32[5,32,16,128]{3,2,1,0:T(8,128)S(1)} copy-done((f32[5,32,16,128]{3,2,1,0:T(8,128)S(1)}, f32[5,32,16,128]{3,2,1,0:T(8,128)}, u32[]{:S(2)}) %copy-start) | copy-done | bytes 1310744
  2.6 0.0 copy-start.2
  2.7 0.9 %copy-done.2 = f32[32,16,128]{2,1,0:T(8,128)S(1)} copy-done((f32[32,16,128]{2,1,0:T(8,128)S(1)}, f32[32,16,128]{2,1,0:T(8,128)}, u32[]{:S(2)}) %copy-start.2) | copy-done | bytes 262168
  3.6 0.0 copy-start.3
  3.6 0.0 copy-start.1
  3.6 0.2 axial_faces.1
  3.8 0.0 copy-done.4
  3.8 0.5 copy-done.3
  4.3 0.7 %coef_share.1.part = f32[16,128]{1,0:T(8,128)S(1)} custom-call(f32[5,8,128]{2,1,0:T(8,128)S(1)} %copy-done.3, s32[1]{0:T(128)S(6)} %copy.13.blade, s32[8]{0:T(128)S(1)} %copy-done.4, f32[8,128]{1,0:T(8,128)S(1)} %get-tuple-element.16.after), custom_call_target="tpu_custom_call" | custom-call | tf_op jit(solution)/shard_map/coef_share/pallas_call | solution.py:515
  5.1 4.0 %collective-permute-start.3 = (f32[16,128]{1,0:T(8,128)S(1)}, f32[16,128]{1,0:T(8,128)S(1)}, u32[]{:S(2)}, u32[]{:S(2)}) collective-permute-start(f32[16,128]{1,0:T(8,128)S(1)} %coef_share.1.part), channel_id=1, source_target_pairs={{0,1},{1,2},{2,3},{3,4},{4,5},{5,6},{6,7},{8,9},{9,10},{10,11},{11... | collective-permute-start | bytes 24584 | tf_op jit(solution)/shard_map/ppermute | solution.py:537
  9.0 1.8 %collective-permute-start.2 = (f32[16,128]{1,0:T(8,128)S(1)}, f32[16,128]{1,0:T(8,128)S(1)}, u32[]{:S(2)}, u32[]{:S(2)}) collective-permute-start(f32[16,128]{1,0:T(8,128)S(1)} %coef_share.1.part), channel_id=1, source_target_pairs={{0,1},{1,0},{2,3},{3,2},{4,5},{5,4},{6,7},{7,6},{8,9},{9,8},{10,11... | collective-permute-start | bytes 24584 | tf_op jit(solution)/shard_map/ppermute | solution.py:536
  10.9 0.1 collective-permute-start
  10.9 1.4 %collective-permute-start.1 = (f32[6,4,24,128]{3,2,1,0:T(8,128)S(1)}, f32[6,4,24,128]{3,2,1,0:T(8,128)S(1)}, u32[]{:S(2)}, u32[]{:S(2)}) collective-permute-start(f32[6,4,24,128]{3,2,1,0:T(8,128)S(1)} %bitcast.16), channel_id=1, source_target_pairs={{0,1},{1,0},{2,3},{3,2},{4,5},{5,4},{6,7},{7,6},{8,9},{9,8},{10,11... | collective-permute-start | bytes 884744 | tf_op jit(solution)/shard_map/ppermute | solution.py:528
  12.3 0.0 copy-done.6
  12.3 0.0 copy-done.7
  12.3 0.0 collective-permute-done.3.before
  12.4 0.0 collective-permute-done.2.other
  12.4 3.1 %collective-permute-done.lo.hi.lo_edge.hi_edge = f32[6,4,8,128]{3,2,1,0:T(8,128)S(1)} collective-permute-done((f32[6,4,8,128]{3,2,1,0:T(8,128)S(1)}, f32[6,4,8,128]{3,2,1,0:T(8,128)S(1)}, u32[]{:S(2)}, u32[]{:S(2)}) %collective-permute-start) | collective-permute-done | bytes 98336 | tf_op jit(solution)/shard_map/ppermute | solution.py:528
  15.5 0.0 copy-done.1
  15.5 0.5 span_faces.1
  16.0 3.4 %collective-permute-start.4 = (f32[496,128]{1,0:T(8,128)S(1)}, f32[496,128]{1,0:T(8,128)S(1)}, u32[]{:S(2)}, u32[]{:S(2)}) collective-permute-start(f32[496,128]{1,0:T(8,128)S(1)} %get-tuple-element.17), channel_id=1, source_target_pairs={{0,2},{2,4},{4,6},{1,3},{3,5},{5,7},{8,10},{10,12},{12,14},{9,11},... | collective-permute-start | bytes 761864 | tf_op jit(solution)/shard_map/ppermute | solution.py:575
  19.4 1.9 %collective-permute-start.5 = (f32[496,128]{1,0:T(8,128)S(1)}, f32[496,128]{1,0:T(8,128)S(1)}, u32[]{:S(2)}, u32[]{:S(2)}) collective-permute-start(f32[496,128]{1,0:T(8,128)S(1)} %get-tuple-element.18), channel_id=1, source_target_pairs={{2,0},{4,2},{6,4},{3,1},{5,3},{7,5},{10,8},{12,10},{14,12},{11,9},... | collective-permute-start | bytes 761864 | tf_op jit(solution)/shard_map/ppermute | solution.py:576
  21.3 0.3 collective-permute-done.1.lo.hi
  21.6 1.0 %collective-permute-done.4.below = f32[496,128]{1,0:T(8,128)S(1)} collective-permute-done((f32[496,128]{1,0:T(8,128)S(1)}, f32[496,128]{1,0:T(8,128)S(1)}, u32[]{:S(2)}, u32[]{:S(2)}) %collective-permute-start.4) | collective-permute-done | bytes 253984 | tf_op jit(solution)/shard_map/ppermute | solution.py:575
  22.6 4.4 %collective-permute-done.5.above = f32[496,128]{1,0:T(8,128)S(1)} collective-permute-done((f32[496,128]{1,0:T(8,128)S(1)}, f32[496,128]{1,0:T(8,128)S(1)}, u32[]{:S(2)}, u32[]{:S(2)}) %collective-permute-start.5) | collective-permute-done | bytes 253984 | tf_op jit(solution)/shard_map/ppermute | solution.py:576
  27.0 0.0 copy-start.5
  27.0 1.7 %circ_faces.1 = (f32[6,960,128]{2,1,0:T(8,128)S(1)}, f32[248,128]{1,0:T(8,128)S(1)}, f32[248,128]{1,0:T(8,128)S(1)}, f32[32,128]{1,0:T(8,128)S(1)}) custom-call(f32[5,512,128]{2,1,0:T(8,128)S(1)} %bitcast.12, f32[512,128]{1,0:T(8,128)S(1)} %bitcast.15, f32[6,4,8,128]{3,2,1,0:T(8,128)S(1)} %collective-permute-done.lo.hi.lo_edge.hi_edge, ...), custom_call_target="tpu_custom_call" | custom-call | tf_op jit(solution)/shard_map/circ_faces/pallas_call | solution.py:579
  28.7 1.3 %collective-permute-start.7 = (f32[248,128]{1,0:T(8,128)S(1)}, f32[248,128]{1,0:T(8,128)S(1)}, u32[]{:S(2)}, u32[]{:S(2)}) collective-permute-start(f32[248,128]{1,0:T(8,128)S(1)} %get-tuple-element.22), channel_id=1, source_target_pairs={{0,8},{8,16},{16,24},{24,0},{1,9},{9,17},{17,25},{25,1},{2,10},{10... | collective-permute-start | bytes 380936 | tf_op jit(solution)/shard_map/ppermute | solution.py:593
  30.0 2.1 %collective-permute-start.8 = (f32[248,128]{1,0:T(8,128)S(1)}, f32[248,128]{1,0:T(8,128)S(1)}, u32[]{:S(2)}, u32[]{:S(2)}) collective-permute-start(f32[248,128]{1,0:T(8,128)S(1)} %get-tuple-element.23), channel_id=1, source_target_pairs={{0,24},{8,0},{16,8},{24,16},{1,25},{9,1},{17,9},{25,17},{2,26},{10... | collective-permute-start | bytes 380936 | tf_op jit(solution)/shard_map/ppermute | solution.py:594
  32.1 0.4 collective-permute-start.6
  32.5 0.0 copy-done.5
  32.5 3.4 %collective-permute-done.6.shares_1_ = f32[32,128]{1,0:T(8,128)S(1)} collective-permute-done((f32[32,128]{1,0:T(8,128)S(1)}, f32[32,128]{1,0:T(8,128)S(1)}, u32[]{:S(2)}, u32[]{:S(2)}) %collective-permute-start.6) | collective-permute-done | bytes 16416 | tf_op jit(solution)/shard_map/ppermute | solution.py:596
  35.9 0.0 collective-permute-done.7.from_left
  35.9 0.0 collective-permute-done.8.from_right
  35.9 22.5 %segments.1 = (f32[5,512,128]{2,1,0:T(8,128)}, f32[5,512,128]{2,1,0:T(8,128)}, f32[6,960,128]{2,1,0:T(8,128)S(1)}) custom-call(f32[3,5,5]{2,1,0:T(8,128)S(1)} %copy.11.jac, s32[8]{0:T(128)S(1)} %copy-done.4, s32[1]{0:T(128)S(6)} %copy.13.blade, f32[32,128]{1,0:T(8,128)S(1)} %get-tuple-element.20.shares_0_, ...), custom_call_target="tpu_custom_call", output_to_operand_aliasing={{2}: (5, {})} | custom-call | tf_op jit(solution)/shard_map/segments/pallas_call | solution.py:601
  (3 shorter events, 0.0 us)
Async XLA Ops:
  0.6 3.2 %copy-start.4 = (s32[8]{0:T(128)S(1)}, s32[8]{0:T(128)}, u32[]{:S(2)}) copy-start(s32[8]{0:T(128)} %harm.3) | copy-start | bytes 100
  0.6 11.7 %copy-start.6 = (s32[32]{0:T(128)S(1)}, s32[32]{0:T(128)}, u32[]{:S(2)}) copy-start(s32[32]{0:T(128)} %param.11) | copy-start | bytes 388
  0.7 11.7 %copy-start.7 = (f32[32]{0:T(128)S(1)}, f32[32]{0:T(128)}, u32[]{:S(2)}) copy-start(f32[32]{0:T(128)} %param.12) | copy-start | bytes 388
  1.3 1.3 %copy-start = (f32[5,32,16,128]{3,2,1,0:T(8,128)S(1)}, f32[5,32,16,128]{3,2,1,0:T(8,128)}, u32[]{:S(2)}) copy-start(f32[5,32,16,128]{3,2,1,0:T(8,128)} %state.1) | copy-start | bytes 3932164
  2.6 0.9 %copy-start.2 = (f32[32,16,128]{2,1,0:T(8,128)S(1)}, f32[32,16,128]{2,1,0:T(8,128)}, u32[]{:S(2)}) copy-start(f32[32,16,128]{2,1,0:T(8,128)} %dt.1) | copy-start | bytes 786436
  3.6 0.7 %copy-start.3 = (f32[5,8,128]{2,1,0:T(8,128)S(1)}, f32[5,8,128]{2,1,0:T(8,128)}, u32[]{:S(2)}) copy-start(f32[5,8,128]{2,1,0:T(8,128)} %rotor.1) | copy-start | bytes 61444
  3.6 11.9 %copy-start.1 = (f32[5,32,16,128]{3,2,1,0:T(8,128)S(1)}, f32[5,32,16,128]{3,2,1,0:T(8,128)}, u32[]{:S(2)}) copy-start(f32[5,32,16,128]{3,2,1,0:T(8,128)} %state.1) | copy-start | bytes 3932164
  5.1 7.3 %collective-permute-start.3 = (f32[16,128]{1,0:T(8,128)S(1)}, f32[16,128]{1,0:T(8,128)S(1)}, u32[]{:S(2)}, u32[]{:S(2)}) collective-permute-start(f32[16,128]{1,0:T(8,128)S(1)} %coef_share.1.part), channel_id=1, source_target_pairs={{0,1},{1,2},{2,3},{3,4},{4,5},{5,6},{6,7},{8,9},{9,10},{10,11},{11... | collective-permute-start | bytes 24584 | tf_op jit(solution)/shard_map/ppermute | solution.py:537
  9.0 3.3 %collective-permute-start.2 = (f32[16,128]{1,0:T(8,128)S(1)}, f32[16,128]{1,0:T(8,128)S(1)}, u32[]{:S(2)}, u32[]{:S(2)}) collective-permute-start(f32[16,128]{1,0:T(8,128)S(1)} %coef_share.1.part), channel_id=1, source_target_pairs={{0,1},{1,0},{2,3},{3,2},{4,5},{5,4},{6,7},{7,6},{8,9},{9,8},{10,11... | collective-permute-start | bytes 24584 | tf_op jit(solution)/shard_map/ppermute | solution.py:536
  10.9 4.6 %collective-permute-start = (f32[6,4,8,128]{3,2,1,0:T(8,128)S(1)}, f32[6,4,8,128]{3,2,1,0:T(8,128)S(1)}, u32[]{:S(2)}, u32[]{:S(2)}) collective-permute-start(f32[6,4,8,128]{3,2,1,0:T(8,128)S(1)} %bitcast.17), channel_id=1, source_target_pairs={{0,1},{1,0},{2,3},{3,2},{4,5},{5,4},{6,7},{7,6},{8,9},{9,8},{10,11... | collective-permute-start | bytes 294920 | tf_op jit(solution)/shard_map/ppermute | solution.py:528
  10.9 10.7 %collective-permute-start.1 = (f32[6,4,24,128]{3,2,1,0:T(8,128)S(1)}, f32[6,4,24,128]{3,2,1,0:T(8,128)S(1)}, u32[]{:S(2)}, u32[]{:S(2)}) collective-permute-start(f32[6,4,24,128]{3,2,1,0:T(8,128)S(1)} %bitcast.16), channel_id=1, source_target_pairs={{0,1},{1,0},{2,3},{3,2},{4,5},{5,4},{6,7},{7,6},{8,9},{9,8},{10,11... | collective-permute-start | bytes 884744 | tf_op jit(solution)/shard_map/ppermute | solution.py:528
  16.0 6.6 %collective-permute-start.4 = (f32[496,128]{1,0:T(8,128)S(1)}, f32[496,128]{1,0:T(8,128)S(1)}, u32[]{:S(2)}, u32[]{:S(2)}) collective-permute-start(f32[496,128]{1,0:T(8,128)S(1)} %get-tuple-element.17), channel_id=1, source_target_pairs={{0,2},{2,4},{4,6},{1,3},{3,5},{5,7},{8,10},{10,12},{12,14},{9,11},... | collective-permute-start | bytes 761864 | tf_op jit(solution)/shard_map/ppermute | solution.py:575
  19.4 7.6 %collective-permute-start.5 = (f32[496,128]{1,0:T(8,128)S(1)}, f32[496,128]{1,0:T(8,128)S(1)}, u32[]{:S(2)}, u32[]{:S(2)}) collective-permute-start(f32[496,128]{1,0:T(8,128)S(1)} %get-tuple-element.18), channel_id=1, source_target_pairs={{2,0},{4,2},{6,4},{3,1},{5,3},{7,5},{10,8},{12,10},{14,12},{11,9},... | collective-permute-start | bytes 761864 | tf_op jit(solution)/shard_map/ppermute | solution.py:576
  27.0 5.5 %copy-start.5 = (f32[3,5,5]{2,0,1:T(4,128)S(1)}, f32[3,5,5]{2,0,1:T(4,128)}, u32[]{:S(2)}) copy-start(f32[3,5,5]{2,0,1:T(4,128)} %param.15) | copy-start | bytes 904
  28.7 7.2 %collective-permute-start.7 = (f32[248,128]{1,0:T(8,128)S(1)}, f32[248,128]{1,0:T(8,128)S(1)}, u32[]{:S(2)}, u32[]{:S(2)}) collective-permute-start(f32[248,128]{1,0:T(8,128)S(1)} %get-tuple-element.22), channel_id=1, source_target_pairs={{0,8},{8,16},{16,24},{24,0},{1,9},{9,17},{17,25},{25,1},{2,10},{10... | collective-permute-start | bytes 380936 | tf_op jit(solution)/shard_map/ppermute | solution.py:593
  30.0 5.9 %collective-permute-start.8 = (f32[248,128]{1,0:T(8,128)S(1)}, f32[248,128]{1,0:T(8,128)S(1)}, u32[]{:S(2)}, u32[]{:S(2)}) collective-permute-start(f32[248,128]{1,0:T(8,128)S(1)} %get-tuple-element.23), channel_id=1, source_target_pairs={{0,24},{8,0},{16,8},{24,16},{1,25},{9,1},{17,9},{25,17},{2,26},{10... | collective-permute-start | bytes 380936 | tf_op jit(solution)/shard_map/ppermute | solution.py:594
  32.1 3.8 %collective-permute-start.6 = (f32[32,128]{1,0:T(8,128)S(1)}, f32[32,128]{1,0:T(8,128)S(1)}, u32[]{:S(2)}, u32[]{:S(2)}) collective-permute-start(f32[32,128]{1,0:T(8,128)S(1)} %get-tuple-element.20.shares_0_), channel_id=1, source_target_pairs={{0,16},{8,24},{16,0},{24,8},{1,17},{9,25},{17,1},{25,9},{2,18},{10... | collective-permute-start | bytes 49160 | tf_op jit(solution)/shard_map/ppermute | solution.py:596

commit v10 on v9

--- a/solution.py
+++ b/solution.py
@@ -391,7 +391,6 @@
 
             cells = prepare(groups[0])
             for n, group in enumerate(groups):
-                following = prepare(groups[n + 1]) if n + 1 < len(groups) else None
                 results = apply(cells)
                 for (i, t), cell, result in zip(group, cells, results):
                     row = pl.multiple_of((b + i) * br, 8) + 8 * t
@@ -405,7 +404,7 @@
                             if t > 0 and number == 0:
                                 rows = pl.ds(pl.multiple_of((b + i - 1) * al, 8) + t - 1, 8, stride=turns)
                                 res_v[u, rows, :] = (2.0 * DISSIP) * result[u]
-                cells = following
+                cells = prepare(groups[n + 1]) if n + 1 < len(groups) else None
 
         def run(start, count, first):
             def loop(j, carry):

time: 58.7 us -> 58.5 us (level)
  no operation moved by 1% of the time
where the time goes in v10:
time: 58.5 us; the launch traced here: 58.3 us
  Pallas kernels  25.5 us (44%)
  starting transfers between devices  16.4 us (28%)
  waiting for transfers between devices  12.2 us (21%)
  local copies, waits for them, and re-layouts  2.77 us (5%)
  between operations  1.42 us (2%)
    pallas_call x1, Pallas kernels, local(): pl.pallas_call(functools.partial(step_kernel, dims), out_shape=[block, bl...  22.3 us
    ppermute x1, waiting for transfers between devices, local(): above = lax.ppermute(down, 'span', shift_pairs(n_span, -1, False))  4.4 us
    ppermute x1, starting transfers between devices, local(): lax.ppermute(part, ('span', 'axial'), shift_pairs(n_span * n_axial, 1, Fa...  3.95 us
    ppermute x2, waiting for transfers between devices, axial_move(): moved = lax.ppermute(faces[0], 'axial', [(0, 1), (1, 0)])  3.44 us
    ppermute x1, waiting for transfers between devices, local(): shares = [share, lax.ppermute(share, 'circ', shift_pairs(n_circ, 2, True))]  3.4 us
    ppermute x1, starting transfers between devices, local(): below = lax.ppermute(up, 'span', shift_pairs(n_span, 1, False))  3.37 us
    unnamed x17, local copies, waits for them, and re-layouts  2.77 us
    ppermute x1, starting transfers between devices, local(): from_right = lax.ppermute(left, 'circ', shift_pairs(n_circ, -1, True))  2.09 us
  transfers between devices with their start and end apart: 9, of which 5 were waited for; matrix products, arithmetic and copies ran while one was open for 0% of the time, Pallas kernels for 1%

profile of v10, /device:TPU:1, one launch (start us, length us, event | category | flops | bytes accessed | tf_op | source)
XLA Modules:
  0.0 58.3 jit_solution(3971633055562911185)
XLA Ops:
  0.6 0.0 copy-start.4
  0.6 0.0 copy-start.6
  0.7 0.0 copy-start.7
  1.3 0.0 copy-start
  1.3 1.3 %copy-done = f32[5,32,16,128]{3,2,1,0:T(8,128)S(1)} copy-done((f32[5,32,16,128]{3,2,1,0:T(8,128)S(1)}, f32[5,32,16,128]{3,2,1,0:T(8,128)}, u32[]{:S(2)}) %copy-start) | copy-done | bytes 1310744
  2.6 0.0 copy-start.2
  2.7 0.9 %copy-done.2 = f32[32,16,128]{2,1,0:T(8,128)S(1)} copy-done((f32[32,16,128]{2,1,0:T(8,128)S(1)}, f32[32,16,128]{2,1,0:T(8,128)}, u32[]{:S(2)}) %copy-start.2) | copy-done | bytes 262168
  3.6 0.0 copy-start.3
  3.6 0.0 copy-start.1
  3.6 0.2 axial_faces.1
  3.8 0.0 copy-done.4
  3.8 0.5 copy-done.3
  4.3 0.7 %coef_share.1.part = f32[16,128]{1,0:T(8,128)S(1)} custom-call(f32[5,8,128]{2,1,0:T(8,128)S(1)} %copy-done.3, s32[1]{0:T(128)S(6)} %copy.13.blade, s32[8]{0:T(128)S(1)} %copy-done.4, f32[8,128]{1,0:T(8,128)S(1)} %get-tuple-element.16.after), custom_call_target="tpu_custom_call" | custom-call | tf_op jit(solution)/shard_map/coef_share/pallas_call | solution.py:514
  5.1 4.0 %collective-permute-start.3 = (f32[16,128]{1,0:T(8,128)S(1)}, f32[16,128]{1,0:T(8,128)S(1)}, u32[]{:S(2)}, u32[]{:S(2)}) collective-permute-start(f32[16,128]{1,0:T(8,128)S(1)} %coef_share.1.part), channel_id=1, source_target_pairs={{0,1},{1,2},{2,3},{3,4},{4,5},{5,6},{6,7},{8,9},{9,10},{10,11},{11... | collective-permute-start | bytes 24584 | tf_op jit(solution)/shard_map/ppermute | solution.py:536
  9.0 1.8 %collective-permute-start.2 = (f32[16,128]{1,0:T(8,128)S(1)}, f32[16,128]{1,0:T(8,128)S(1)}, u32[]{:S(2)}, u32[]{:S(2)}) collective-permute-start(f32[16,128]{1,0:T(8,128)S(1)} %coef_share.1.part), channel_id=1, source_target_pairs={{0,1},{1,0},{2,3},{3,2},{4,5},{5,4},{6,7},{7,6},{8,9},{9,8},{10,11... | collective-permute-start | bytes 24584 | tf_op jit(solution)/shard_map/ppermute | solution.py:535
  10.9 0.1 collective-permute-start
  10.9 1.4 %collective-permute-start.1 = (f32[6,4,24,128]{3,2,1,0:T(8,128)S(1)}, f32[6,4,24,128]{3,2,1,0:T(8,128)S(1)}, u32[]{:S(2)}, u32[]{:S(2)}) collective-permute-start(f32[6,4,24,128]{3,2,1,0:T(8,128)S(1)} %bitcast.16), channel_id=1, source_target_pairs={{0,1},{1,0},{2,3},{3,2},{4,5},{5,4},{6,7},{7,6},{8,9},{9,8},{10,11... | collective-permute-start | bytes 884744 | tf_op jit(solution)/shard_map/ppermute | solution.py:527
  12.3 0.0 copy-done.6
  12.3 0.0 copy-done.7
  12.3 0.0 collective-permute-done.3.before
  12.4 0.0 collective-permute-done.2.other
  12.4 3.1 %collective-permute-done.lo.hi.lo_edge.hi_edge = f32[6,4,8,128]{3,2,1,0:T(8,128)S(1)} collective-permute-done((f32[6,4,8,128]{3,2,1,0:T(8,128)S(1)}, f32[6,4,8,128]{3,2,1,0:T(8,128)S(1)}, u32[]{:S(2)}, u32[]{:S(2)}) %collective-permute-start) | collective-permute-done | bytes 98336 | tf_op jit(solution)/shard_map/ppermute | solution.py:527
  15.5 0.0 copy-done.1
  15.5 0.5 span_faces.1
  16.0 3.4 %collective-permute-start.4 = (f32[496,128]{1,0:T(8,128)S(1)}, f32[496,128]{1,0:T(8,128)S(1)}, u32[]{:S(2)}, u32[]{:S(2)}) collective-permute-start(f32[496,128]{1,0:T(8,128)S(1)} %get-tuple-element.17), channel_id=1, source_target_pairs={{0,2},{2,4},{4,6},{1,3},{3,5},{5,7},{8,10},{10,12},{12,14},{9,11},... | collective-permute-start | bytes 761864 | tf_op jit(solution)/shard_map/ppermute | solution.py:574
  19.4 1.9 %collective-permute-start.5 = (f32[496,128]{1,0:T(8,128)S(1)}, f32[496,128]{1,0:T(8,128)S(1)}, u32[]{:S(2)}, u32[]{:S(2)}) collective-permute-start(f32[496,128]{1,0:T(8,128)S(1)} %get-tuple-element.18), channel_id=1, source_target_pairs={{2,0},{4,2},{6,4},{3,1},{5,3},{7,5},{10,8},{12,10},{14,12},{11,9},... | collective-permute-start | bytes 761864 | tf_op jit(solution)/shard_map/ppermute | solution.py:575
  21.3 0.3 collective-permute-done.1.lo.hi
  21.6 1.0 %collective-permute-done.4.below = f32[496,128]{1,0:T(8,128)S(1)} collective-permute-done((f32[496,128]{1,0:T(8,128)S(1)}, f32[496,128]{1,0:T(8,128)S(1)}, u32[]{:S(2)}, u32[]{:S(2)}) %collective-permute-start.4) | collective-permute-done | bytes 253984 | tf_op jit(solution)/shard_map/ppermute | solution.py:574
  22.6 4.4 %collective-permute-done.5.above = f32[496,128]{1,0:T(8,128)S(1)} collective-permute-done((f32[496,128]{1,0:T(8,128)S(1)}, f32[496,128]{1,0:T(8,128)S(1)}, u32[]{:S(2)}, u32[]{:S(2)}) %collective-permute-start.5) | collective-permute-done | bytes 253984 | tf_op jit(solution)/shard_map/ppermute | solution.py:575
  27.0 0.0 copy-start.5
  27.0 1.7 %circ_faces.1 = (f32[6,960,128]{2,1,0:T(8,128)S(1)}, f32[248,128]{1,0:T(8,128)S(1)}, f32[248,128]{1,0:T(8,128)S(1)}, f32[32,128]{1,0:T(8,128)S(1)}) custom-call(f32[5,512,128]{2,1,0:T(8,128)S(1)} %bitcast.12, f32[512,128]{1,0:T(8,128)S(1)} %bitcast.15, f32[6,4,8,128]{3,2,1,0:T(8,128)S(1)} %collective-permute-done.lo.hi.lo_edge.hi_edge, ...), custom_call_target="tpu_custom_call" | custom-call | tf_op jit(solution)/shard_map/circ_faces/pallas_call | solution.py:578
  28.7 1.3 %collective-permute-start.7 = (f32[248,128]{1,0:T(8,128)S(1)}, f32[248,128]{1,0:T(8,128)S(1)}, u32[]{:S(2)}, u32[]{:S(2)}) collective-permute-start(f32[248,128]{1,0:T(8,128)S(1)} %get-tuple-element.22), channel_id=1, source_target_pairs={{0,8},{8,16},{16,24},{24,0},{1,9},{9,17},{17,25},{25,1},{2,10},{10... | collective-permute-start | bytes 380936 | tf_op jit(solution)/shard_map/ppermute | solution.py:592
  30.0 2.1 %collective-permute-start.8 = (f32[248,128]{1,0:T(8,128)S(1)}, f32[248,128]{1,0:T(8,128)S(1)}, u32[]{:S(2)}, u32[]{:S(2)}) collective-permute-start(f32[248,128]{1,0:T(8,128)S(1)} %get-tuple-element.23), channel_id=1, source_target_pairs={{0,24},{8,0},{16,8},{24,16},{1,25},{9,1},{17,9},{25,17},{2,26},{10... | collective-permute-start | bytes 380936 | tf_op jit(solution)/shard_map/ppermute | solution.py:593
  32.1 0.4 collective-permute-start.6
  32.5 0.0 copy-done.5
  32.5 3.4 %collective-permute-done.6.shares_1_ = f32[32,128]{1,0:T(8,128)S(1)} collective-permute-done((f32[32,128]{1,0:T(8,128)S(1)}, f32[32,128]{1,0:T(8,128)S(1)}, u32[]{:S(2)}, u32[]{:S(2)}) %collective-permute-start.6) | collective-permute-done | bytes 16416 | tf_op jit(solution)/shard_map/ppermute | solution.py:595
  35.9 0.0 collective-permute-done.7.from_left
  35.9 0.0 collective-permute-done.8.from_right
  35.9 22.3 %segments.1 = (f32[5,512,128]{2,1,0:T(8,128)}, f32[5,512,128]{2,1,0:T(8,128)}, f32[6,960,128]{2,1,0:T(8,128)S(1)}) custom-call(f32[3,5,5]{2,1,0:T(8,128)S(1)} %copy.11.jac, s32[8]{0:T(128)S(1)} %copy-done.4, s32[1]{0:T(128)S(6)} %copy.13.blade, f32[32,128]{1,0:T(8,128)S(1)} %get-tuple-element.20.shares_0_, ...), custom_call_target="tpu_custom_call", output_to_operand_aliasing={{2}: (5, {})} | custom-call | tf_op jit(solution)/shard_map/segments/pallas_call | solution.py:600
  (3 shorter events, 0.0 us)
Async XLA Ops:
  0.6 3.2 %copy-start.4 = (s32[8]{0:T(128)S(1)}, s32[8]{0:T(128)}, u32[]{:S(2)}) copy-start(s32[8]{0:T(128)} %harm.3) | copy-start | bytes 100
  0.6 11.7 %copy-start.6 = (s32[32]{0:T(128)S(1)}, s32[32]{0:T(128)}, u32[]{:S(2)}) copy-start(s32[32]{0:T(128)} %param.11) | copy-start | bytes 388
  0.7 11.7 %copy-start.7 = (f32[32]{0:T(128)S(1)}, f32[32]{0:T(128)}, u32[]{:S(2)}) copy-start(f32[32]{0:T(128)} %param.12) | copy-start | bytes 388
  1.3 1.3 %copy-start = (f32[5,32,16,128]{3,2,1,0:T(8,128)S(1)}, f32[5,32,16,128]{3,2,1,0:T(8,128)}, u32[]{:S(2)}) copy-start(f32[5,32,16,128]{3,2,1,0:T(8,128)} %state.1) | copy-start | bytes 3932164
  2.6 0.9 %copy-start.2 = (f32[32,16,128]{2,1,0:T(8,128)S(1)}, f32[32,16,128]{2,1,0:T(8,128)}, u32[]{:S(2)}) copy-start(f32[32,16,128]{2,1,0:T(8,128)} %dt.1) | copy-start | bytes 786436
  3.6 0.7 %copy-start.3 = (f32[5,8,128]{2,1,0:T(8,128)S(1)}, f32[5,8,128]{2,1,0:T(8,128)}, u32[]{:S(2)}) copy-start(f32[5,8,128]{2,1,0:T(8,128)} %rotor.1) | copy-start | bytes 61444
  3.6 11.9 %copy-start.1 = (f32[5,32,16,128]{3,2,1,0:T(8,128)S(1)}, f32[5,32,16,128]{3,2,1,0:T(8,128)}, u32[]{:S(2)}) copy-start(f32[5,32,16,128]{3,2,1,0:T(8,128)} %state.1) | copy-start | bytes 3932164
  5.1 7.3 %collective-permute-start.3 = (f32[16,128]{1,0:T(8,128)S(1)}, f32[16,128]{1,0:T(8,128)S(1)}, u32[]{:S(2)}, u32[]{:S(2)}) collective-permute-start(f32[16,128]{1,0:T(8,128)S(1)} %coef_share.1.part), channel_id=1, source_target_pairs={{0,1},{1,2},{2,3},{3,4},{4,5},{5,6},{6,7},{8,9},{9,10},{10,11},{11... | collective-permute-start | bytes 24584 | tf_op jit(solution)/shard_map/ppermute | solution.py:536
  9.0 3.3 %collective-permute-start.2 = (f32[16,128]{1,0:T(8,128)S(1)}, f32[16,128]{1,0:T(8,128)S(1)}, u32[]{:S(2)}, u32[]{:S(2)}) collective-permute-start(f32[16,128]{1,0:T(8,128)S(1)} %coef_share.1.part), channel_id=1, source_target_pairs={{0,1},{1,0},{2,3},{3,2},{4,5},{5,4},{6,7},{7,6},{8,9},{9,8},{10,11... | collective-permute-start | bytes 24584 | tf_op jit(solution)/shard_map/ppermute | solution.py:535
  10.9 4.6 %collective-permute-start = (f32[6,4,8,128]{3,2,1,0:T(8,128)S(1)}, f32[6,4,8,128]{3,2,1,0:T(8,128)S(1)}, u32[]{:S(2)}, u32[]{:S(2)}) collective-permute-start(f32[6,4,8,128]{3,2,1,0:T(8,128)S(1)} %bitcast.17), channel_id=1, source_target_pairs={{0,1},{1,0},{2,3},{3,2},{4,5},{5,4},{6,7},{7,6},{8,9},{9,8},{10,11... | collective-permute-start | bytes 294920 | tf_op jit(solution)/shard_map/ppermute | solution.py:527
  10.9 10.7 %collective-permute-start.1 = (f32[6,4,24,128]{3,2,1,0:T(8,128)S(1)}, f32[6,4,24,128]{3,2,1,0:T(8,128)S(1)}, u32[]{:S(2)}, u32[]{:S(2)}) collective-permute-start(f32[6,4,24,128]{3,2,1,0:T(8,128)S(1)} %bitcast.16), channel_id=1, source_target_pairs={{0,1},{1,0},{2,3},{3,2},{4,5},{5,4},{6,7},{7,6},{8,9},{9,8},{10,11... | collective-permute-start | bytes 884744 | tf_op jit(solution)/shard_map/ppermute | solution.py:527
  16.0 6.6 %collective-permute-start.4 = (f32[496,128]{1,0:T(8,128)S(1)}, f32[496,128]{1,0:T(8,128)S(1)}, u32[]{:S(2)}, u32[]{:S(2)}) collective-permute-start(f32[496,128]{1,0:T(8,128)S(1)} %get-tuple-element.17), channel_id=1, source_target_pairs={{0,2},{2,4},{4,6},{1,3},{3,5},{5,7},{8,10},{10,12},{12,14},{9,11},... | collective-permute-start | bytes 761864 | tf_op jit(solution)/shard_map/ppermute | solution.py:574
  19.4 7.6 %collective-permute-start.5 = (f32[496,128]{1,0:T(8,128)S(1)}, f32[496,128]{1,0:T(8,128)S(1)}, u32[]{:S(2)}, u32[]{:S(2)}) collective-permute-start(f32[496,128]{1,0:T(8,128)S(1)} %get-tuple-element.18), channel_id=1, source_target_pairs={{2,0},{4,2},{6,4},{3,1},{5,3},{7,5},{10,8},{12,10},{14,12},{11,9},... | collective-permute-start | bytes 761864 | tf_op jit(solution)/shard_map/ppermute | solution.py:575
  27.0 5.5 %copy-start.5 = (f32[3,5,5]{2,0,1:T(4,128)S(1)}, f32[3,5,5]{2,0,1:T(4,128)}, u32[]{:S(2)}) copy-start(f32[3,5,5]{2,0,1:T(4,128)} %param.15) | copy-start | bytes 904
  28.7 7.2 %collective-permute-start.7 = (f32[248,128]{1,0:T(8,128)S(1)}, f32[248,128]{1,0:T(8,128)S(1)}, u32[]{:S(2)}, u32[]{:S(2)}) collective-permute-start(f32[248,128]{1,0:T(8,128)S(1)} %get-tuple-element.22), channel_id=1, source_target_pairs={{0,8},{8,16},{16,24},{24,0},{1,9},{9,17},{17,25},{25,1},{2,10},{10... | collective-permute-start | bytes 380936 | tf_op jit(solution)/shard_map/ppermute | solution.py:592
  30.0 5.9 %collective-permute-start.8 = (f32[248,128]{1,0:T(8,128)S(1)}, f32[248,128]{1,0:T(8,128)S(1)}, u32[]{:S(2)}, u32[]{:S(2)}) collective-permute-start(f32[248,128]{1,0:T(8,128)S(1)} %get-tuple-element.23), channel_id=1, source_target_pairs={{0,24},{8,0},{16,8},{24,16},{1,25},{9,1},{17,9},{25,17},{2,26},{10... | collective-permute-start | bytes 380936 | tf_op jit(solution)/shard_map/ppermute | solution.py:593
  32.1 3.8 %collective-permute-start.6 = (f32[32,128]{1,0:T(8,128)S(1)}, f32[32,128]{1,0:T(8,128)S(1)}, u32[]{:S(2)}, u32[]{:S(2)}) collective-permute-start(f32[32,128]{1,0:T(8,128)S(1)} %get-tuple-element.20.shares_0_), channel_id=1, source_target_pairs={{0,16},{8,24},{16,0},{24,8},{1,17},{9,25},{17,1},{25,9},{2,18},{10... | collective-permute-start | bytes 49160 | tf_op jit(solution)/shard_map/ppermute | solution.py:595
